TPU v7x, 128 devices: a whole 4x4x4 slice. The times are simulated.
128 devices in a mesh: fs: 32 (over z, x, core), pol: 4 (over y).
Axes of the slice: x: 4, y: 4, z: 4, core: 2. Of those that a mesh axis runs over, the one named last changes fastest.
Arguments:
- facets: bfloat16 [4, 64, 4096, 128], P('pol', 'fs'), may hold values from -6 to 6
- owners: int32 [64], replicated, may hold values from 0 to 31, as said below
- counts: int32 [64], replicated, may hold values from 1 to 8, as said below
- coords: float32 [2, 128, 8, 128], P(None, 'fs'), may hold values from 0 to 512
- station_ids: int32 [128, 8, 2, 128], P('fs'), may hold values from 0 to 511
- jones_table: float32 [8, 512], replicated, may hold values from -3 to 3
Outputs:
- predicted: float32 [4, 2, 128, 8, 128], P('pol', None, 'fs')
Inputs may be any that keep to these rules, and one draw needn't show every extreme that they name: `owners`: each fs index owns at most 4 subgrids, and some index owns exactly 4. `counts`: some subgrid has exactly 8 blocks.
All inputs are finite; a program needn't handle non-finite values.
Results may differ from a plain program's by a relative error of at most 0.0055.
Values may be sent and summed in bfloat16 or wider, within the bound.
No kernel may reach another device: no remote copies, remote signals or barrier semaphores. Data moves between devices by JAX's collectives and lax.ppermute only.
A program may use at most 64 MiB of HBM per device.

v0:
```python
import math

import jax
import jax.numpy as jnp
from jax import lax
from jax.sharding import PartitionSpec as P

R = 8
W = 64
S = 64
MAXB = 8
VB = 128
FH = 4096
SG = 512


def dft_tables(length):
    indices = jnp.arange(length, dtype=jnp.int32)
    phases = indices[:, None] * indices[None, :] % length
    angles = phases.astype(jnp.float32) * (2.0 * math.pi / length)
    return (jnp.cos(angles).astype(jnp.bfloat16), jnp.sin(angles).astype(jnp.bfloat16))


def turn_table(rows, cols, length):
    row_index = jnp.arange(rows, dtype=jnp.int32)
    col_index = jnp.arange(cols, dtype=jnp.int32)
    phases = row_index[:, None] * col_index[None, :] % length
    angles = phases.astype(jnp.float32) * (2.0 * math.pi / length)
    return (jnp.cos(angles), jnp.sin(angles))


def cell_phases(positions, cells):
    offsets = jnp.arange(cells, dtype=jnp.float32) - cells // 2
    angles = jnp.mod(positions[:, None] * offsets[None, :], float(cells)) * (2.0 * math.pi / cells)
    return (jnp.cos(angles), jnp.sin(angles))


def complex_product(left_real, left_imag, right_real, right_imag):
    return (
        left_real * right_real - left_imag * right_imag,
        left_real * right_imag + left_imag * right_real,
    )


def table_entry(table, position):
    entries = lax.dynamic_slice_in_dim(table, 2 * position, 2, 0)
    return (entries[0], entries[1])


def on_device(facets, owners, counts, coords, station_ids, jones_table):
    device_count = lax.axis_size("fs")
    device_index = lax.axis_index("fs")
    capacity = coords.shape[1]
    strips = facets[0]
    facet_local = strips.shape[0]
    shaped_strips = strips.reshape(facet_local, W, S, 2 * W)
    first_cos, first_sin = dft_tables(W)
    second_cos, second_sin = dft_tables(S)
    turn_cos, turn_sin = turn_table(W, S, FH)
    scale = 1.0 / math.sqrt(FH)
    cos_part = jnp.einsum(
        "kn,fnmc->fkmc", first_cos, shaped_strips, preferred_element_type=jnp.float32
    )
    sin_part = jnp.einsum(
        "kn,fnmc->fkmc", first_sin, shaped_strips, preferred_element_type=jnp.float32
    )
    section_real = cos_part[..., :W] + sin_part[..., W:]
    section_imag = cos_part[..., W:] - sin_part[..., :W]
    tc = turn_cos[None, :, :, None]
    ts = turn_sin[None, :, :, None]
    turned = jnp.concatenate(
        [section_real * tc + section_imag * ts, section_imag * tc - section_real * ts], axis=3
    ).astype(jnp.bfloat16)
    cos_two = jnp.einsum("qm,fkmc->qkfc", second_cos, turned, preferred_element_type=jnp.float32)
    sin_two = jnp.einsum("qm,fkmc->qkfc", second_sin, turned, preferred_element_type=jnp.float32)
    real_two = (cos_two[..., :W] + sin_two[..., W:]) * scale
    imag_two = (cos_two[..., W:] - sin_two[..., :W]) * scale
    windows = jnp.concatenate([real_two, imag_two], axis=3).astype(jnp.bfloat16)
    owned = (owners[None, :] == jnp.arange(device_count, dtype=jnp.int32)[:, None]).astype(
        jnp.int32
    )
    ranks = jnp.cumsum(owned, axis=1) - 1
    matches = owned[:, :, None] * (
        ranks[:, :, None] == jnp.arange(capacity, dtype=jnp.int32)[None, None, :]
    ).astype(jnp.int32)
    slot_subgrid = jnp.sum(matches * jnp.arange(S, dtype=jnp.int32)[None, :, None], axis=1)
    slot_valid = jnp.sum(matches, axis=1)
    local_subgrid = lax.dynamic_index_in_dim(slot_subgrid, device_index, 0, keepdims=False)
    local_valid = lax.dynamic_index_in_dim(slot_valid, device_index, 0, keepdims=False)

    def degrid(tile, positions):
        upper = tile.shape[0] // R
        shaped = tile.reshape(R, upper, W, facet_local, 2 * W)
        row_cos, row_sin = cell_phases(positions[0].reshape(-1), SG)
        row_cos = row_cos.astype(jnp.bfloat16).reshape(-1, R, W)
        row_sin = row_sin.astype(jnp.bfloat16).reshape(-1, R, W)
        cos_grid = jnp.einsum(
            "rak,aukjn->rujn", row_cos, shaped, preferred_element_type=jnp.float32
        )
        sin_grid = jnp.einsum(
            "rak,aukjn->rujn", row_sin, shaped, preferred_element_type=jnp.float32
        )
        real_part = cos_grid[..., :W] + sin_grid[..., W:]
        imag_part = cos_grid[..., W:] - sin_grid[..., :W]
        col_cos, col_sin = cell_phases(positions[1].reshape(-1), SG)
        col_cos = col_cos.reshape(real_part.shape)
        col_sin = col_sin.reshape(real_part.shape)
        vis_real = jnp.sum(real_part * col_cos + imag_part * col_sin, axis=(1, 2, 3)) / SG
        vis_imag = jnp.sum(imag_part * col_cos - real_part * col_sin, axis=(1, 2, 3)) / SG
        return jnp.stack([vis_real, vis_imag]).reshape(2, MAXB, VB)

    picked = jnp.take(windows, slot_subgrid.reshape(-1), axis=0)
    present = slot_valid.reshape(-1) > 0
    picked = jnp.where(present[:, None, None, None], picked, jnp.zeros((), jnp.bfloat16))
    picked = picked.reshape(device_count, capacity, W, facet_local, 2 * W)
    received = lax.all_to_all(picked, "fs", split_axis=0, concat_axis=0, tiled=True)

    def slot_predict(index):
        tile = lax.dynamic_index_in_dim(received, index, 1, keepdims=False)
        positions = lax.dynamic_index_in_dim(coords, index, 1, keepdims=False)
        return degrid(tile, positions)

    visible = lax.map(slot_predict, jnp.arange(capacity, dtype=jnp.int32))
    block_limit = jnp.take(counts, local_subgrid) * local_valid
    keep = jnp.arange(MAXB, dtype=jnp.int32)[None, :] < block_limit[:, None]
    left = jnp.take(jones_table, station_ids[:, :, 0, :], axis=1)
    right = jnp.take(jones_table, station_ids[:, :, 1, :], axis=1)
    own_vis = jnp.moveaxis(visible, 0, 1)
    pol_index = lax.axis_index("pol")
    components = lax.all_gather(own_vis[None], "pol", axis=0, tiled=True)
    row_side = pol_index // 2
    col_side = pol_index % 2
    total_real = jnp.zeros(own_vis.shape[1:], jnp.float32)
    total_imag = jnp.zeros(own_vis.shape[1:], jnp.float32)
    for inner_row in range(2):
        for inner_col in range(2):
            left_real, left_imag = table_entry(left, 2 * row_side + inner_row)
            right_real, right_imag = table_entry(right, 2 * col_side + inner_col)
            comp_real = components[2 * inner_row + inner_col, 0]
            comp_imag = components[2 * inner_row + inner_col, 1]
            step_real, step_imag = complex_product(left_real, left_imag, comp_real, comp_imag)
            step_real, step_imag = complex_product(step_real, step_imag, right_real, -right_imag)
            total_real = total_real + step_real
            total_imag = total_imag + step_imag
    corrected = jnp.stack([total_real, total_imag])[None]
    return jnp.where(keep[None, None, :, :, None], corrected, 0.0)


def solution(mesh):
    return jax.shard_map(
        on_device,
        mesh=mesh,
        in_specs=(
            P("pol", "fs", None, None),
            P(),
            P(),
            P(None, "fs", None, None),
            P("fs", None, None, None),
            P(),
        ),
        out_specs=P("pol", None, "fs", None, None),
        check_vma=False,
    )
```

profile of v0, /device:TPU:0, one launch (start us, length us, event | category | flops | bytes accessed | tf_op | source)
XLA Modules:
  0.0 244.9 jit_solution(9204618091506685177)
XLA Ops:
  1.6 3.7 %convolution_bitcast_fusion.4 = f32[2,64,64,128]{3,1,2,0:T(8,128)} fusion(bf16[2,64,64,128]{3,2,1,0:T(8,128)(2,1)S(1)} %bitcast.173), kind=kOutput, calls=%fused_computation.65 | convolution fusion | flops 134279168 | bytes 6291456 | tf_op jit(solution)/shard_map/kn,fnmc->fkmc/dot_general | solution.py:64
  5.3 3.8 %convolution_bitcast_fusion.5 = f32[2,64,64,128]{3,1,2,0:T(8,128)} fusion(bf16[2,64,64,128]{3,2,1,0:T(8,128)(2,1)S(1)} %bitcast.172), kind=kOutput, calls=%fused_computation.66 | convolution fusion | flops 134279168 | bytes 6291456 | tf_op jit(solution)/shard_map/kn,fnmc->fkmc/dot_general | solution.py:61
  9.5 7.8 %add_convert_fusion = (bf16[2,64,64,64]{3,1,2,0:T(8,128)(2,1)S(1)}, bf16[2,64,64,64]{3,1,2,0:T(8,128)(2,1)S(1)}) fusion(f32[64,64]{0,1:T(8,128)S(1)} %copy.59, f32[64,64]{0,1:T(8,128)S(1)} %copy.58, f32[2,64,64,128]{3,1,2,0:T(8,128)} %convolution_bitcast_fusion.4, f32[2,64,64,128]{3,1,2,0:T(8,128)} %convolution_bitcast_fusion.5), kind=kLoop, calls=%fused_computation.62 | loop fusion | flops 5242880 | bytes 10518528 | tf_op jit(solution)/shard_map/convert.2
  25.6 2.7 %copy.63 = bf16[64,64,2,128]{3,1,2,0:T(8,128)(2,1)} copy(bf16[64,64,2,128]{3,0,1,2:T(8,128)(2,1)S(1)} %pad_maximum_fusion.1) | data formatting | bytes 4194304 | tf_op jit(solution)/shard_map/concatenate | solution.py:78
  29.2 4.6 %gather_fusion.1 = bf16[128,64,2,128]{3,1,2,0:T(8,128)(2,1)} fusion(bf16[64,64,2,128]{3,1,2,0:T(8,128)(2,1)} %copy.63, s32[1024]{0:T(1024)S(1)} %pad_clamp_fusion), kind=kCustom, calls=%fused_computation.3 | custom fusion | bytes 8389120 | tf_op jit(solution)/shard_map/jit(_take)/gather | solution.py:112
  33.8 3.9 %select_select_fusion = bf16[32,4,64,2,128]{4,2,3,1,0:T(8,128)(2,1)} fusion(bf16[32,4,64,2,128]{4,2,3,1,0:T(8,128)(2,1)} %bitcast.176, pred[32,4]{1,0:T(8,128)(4,1)S(1)} %copy.55, pred[32,4]{1,0:T(8,128)(4,1)S(1)} %copy.54), kind=kLoop, calls=%fused_computation.60 | loop fusion | flops 4194304 | bytes 8388864 | tf_op jit(solution)/shard_map/jit(_where)/select_n | solution.py:114
  37.7 8.5 %all-to-all-start = ((bf16[32,4,64,2,128]{4,2,3,1,0:T(8,128)(2,1)}), bf16[32,4,64,2,128]{4,2,3,1,0:T(8,128)(2,1)}, u32[]{:S(2)}, u32[]{:S(2)}) async-start(bf16[32,4,64,2,128]{4,2,3,1,0:T(8,128)(2,1)} %select_select_fusion), calls=%async_computation | async-start | bytes 8388608 | tf_op jit(solution)/shard_map/all_to_all | solution.py:116
  46.4 14.1 %gather_fusion.3 = f32[4096,8]{1,0:T(8,128)} fusion(f32[8,512]{0,1:T(8,128)S(1)} %copy.52, s32[4096]{0:T(1024)S(1)} %bitcast_clamp_fusion), kind=kCustom, calls=%fused_computation.1.clone | custom fusion | bytes 278528 | tf_op jit(solution)/shard_map/jit(_take)/gather | solution.py:127
  62.7 14.1 %gather_fusion.2 = f32[4096,8]{1,0:T(8,128)} fusion(f32[8,512]{0,1:T(8,128)S(1)} %copy.52, s32[4096]{0:T(1024)S(1)} %bitcast_clamp_fusion.1), kind=kCustom, calls=%fused_computation.clone | custom fusion | bytes 278528 | tf_op jit(solution)/shard_map/jit(_take)/gather | solution.py:126
  80.1 19.6 %all-to-all-done = bf16[32,4,64,2,128]{4,2,3,1,0:T(8,128)(2,1)} async-done(((bf16[32,4,64,2,128]{4,2,3,1,0:T(8,128)(2,1)}), bf16[32,4,64,2,128]{4,2,3,1,0:T(8,128)(2,1)}, u32[]{:S(2)}, u32[]{:S(2)}) %all-to-all-start) | async-done | bytes 4194336 | tf_op jit(solution)/shard_map/all_to_all | solution.py:116
  99.7 131.6 %while.12 = (s32[]{:T(128)}, f32[4,2,8,128]{3,2,1,0:T(8,128)S(1)}, s32[4]{0:T(128)S(1)}, f32[2,4,8,128]{3,2,1,0:T(8,128)}, bf16[32,4,64,2,128]{4,2,3,1,0:T(8,128...) while((s32[]{:T(128)}, f32[4,2,8,128]{3,2,1,0:T(8,128)S(1)}, s32[4]{0:T(128)S(1)}, ...), condition=%wide.region_6.8_spmd, body=%wide.region_3.7_spmd.sunk | while | flops 2166364160 | bytes 21051560 | solution.py:123
  104.3 9.0 %convolution_bitcast_fusion.9 = f32[1024,4,2,128]{0,3,2,1:T(8,128)S(1)} fusion(f32[8,64]{1,0:T(8,128)S(1)} %add_add_fusion.5, f32[1024]{0:T(1024)S(1)} %get-tuple-element.147, bf16[8,4,64,2,128]{4,2,3,1,0:T(8,128)(2,1)S(1)} %bitcast.174), kind=kOutput, calls=%fused_computation.7.clone.1 | convolution fusion | flops 1078460416 | bytes 5249024 | tf_op jit(solution)/shard_map/while/body/eval_jaxpr/rak,aukjn->rujn/dot_general | solution.py:97
  113.3 9.1 %convolution_bitcast_fusion.8 = f32[1024,4,2,128]{0,3,2,1:T(8,128)S(1)} fusion(f32[8,64]{1,0:T(8,128)S(1)} %add_add_fusion.5, f32[1024]{0:T(1024)S(1)} %get-tuple-element.147, bf16[8,4,64,2,128]{4,2,3,1,0:T(8,128)(2,1)S(1)} %bitcast.175), kind=kOutput, calls=%fused_computation.6.clone.1 | convolution fusion | flops 1078460416 | bytes 5249024 | tf_op jit(solution)/shard_map/while/body/eval_jaxpr/rak,aukjn->rujn/dot_general | solution.py:100
  122.4 10.2 %add_reduce_fusion.2 = (f32[1024]{0:T(1024)S(1)}, f32[1024]{0:T(1024)S(1)}) fusion(f32[4,2,64]{2,1,0:T(2,128)S(1)} %add_add_fusion.4, f32[1024]{0:T(1024)S(1)} %get-tuple-element.146, f32[1024,4,2,128]{0,3,2,1:T(8,128)S(1)} %convolution_bitcast_fusion.8, f32[1024,4,2,128]{0,3,2,1:T(8,128)S(1)} %convolution_bitcast_fusion.9), kind=kLoop, calls=%fused_computation.13.clone.1 | loop fusion | flops 9435136 | bytes 8402944 | tf_op jit(solution)/shard_map/while/body/eval_jaxpr/reduce_sum | solution.py:108
  137.2 9.0 %convolution_bitcast_fusion.9 = f32[1024,4,2,128]{0,3,2,1:T(8,128)S(1)} fusion(f32[8,64]{1,0:T(8,128)S(1)} %add_add_fusion.5, f32[1024]{0:T(1024)S(1)} %get-tuple-element.147, bf16[8,4,64,2,128]{4,2,3,1,0:T(8,128)(2,1)S(1)} %bitcast.174), kind=kOutput, calls=%fused_computation.7.clone.1 | convolution fusion | flops 1078460416 | bytes 5249024 | tf_op jit(solution)/shard_map/while/body/eval_jaxpr/rak,aukjn->rujn/dot_general | solution.py:97
  146.2 9.1 %convolution_bitcast_fusion.8 = f32[1024,4,2,128]{0,3,2,1:T(8,128)S(1)} fusion(f32[8,64]{1,0:T(8,128)S(1)} %add_add_fusion.5, f32[1024]{0:T(1024)S(1)} %get-tuple-element.147, bf16[8,4,64,2,128]{4,2,3,1,0:T(8,128)(2,1)S(1)} %bitcast.175), kind=kOutput, calls=%fused_computation.6.clone.1 | convolution fusion | flops 1078460416 | bytes 5249024 | tf_op jit(solution)/shard_map/while/body/eval_jaxpr/rak,aukjn->rujn/dot_general | solution.py:100
  155.3 10.2 %add_reduce_fusion.2 = (f32[1024]{0:T(1024)S(1)}, f32[1024]{0:T(1024)S(1)}) fusion(f32[4,2,64]{2,1,0:T(2,128)S(1)} %add_add_fusion.4, f32[1024]{0:T(1024)S(1)} %get-tuple-element.146, f32[1024,4,2,128]{0,3,2,1:T(8,128)S(1)} %convolution_bitcast_fusion.8, f32[1024,4,2,128]{0,3,2,1:T(8,128)S(1)} %convolution_bitcast_fusion.9), kind=kLoop, calls=%fused_computation.13.clone.1 | loop fusion | flops 9435136 | bytes 8402944 | tf_op jit(solution)/shard_map/while/body/eval_jaxpr/reduce_sum | solution.py:108
  170.0 9.0 %convolution_bitcast_fusion.9 = f32[1024,4,2,128]{0,3,2,1:T(8,128)S(1)} fusion(f32[8,64]{1,0:T(8,128)S(1)} %add_add_fusion.5, f32[1024]{0:T(1024)S(1)} %get-tuple-element.147, bf16[8,4,64,2,128]{4,2,3,1,0:T(8,128)(2,1)S(1)} %bitcast.174), kind=kOutput, calls=%fused_computation.7.clone.1 | convolution fusion | flops 1078460416 | bytes 5249024 | tf_op jit(solution)/shard_map/while/body/eval_jaxpr/rak,aukjn->rujn/dot_general | solution.py:97
  179.0 9.1 %convolution_bitcast_fusion.8 = f32[1024,4,2,128]{0,3,2,1:T(8,128)S(1)} fusion(f32[8,64]{1,0:T(8,128)S(1)} %add_add_fusion.5, f32[1024]{0:T(1024)S(1)} %get-tuple-element.147, bf16[8,4,64,2,128]{4,2,3,1,0:T(8,128)(2,1)S(1)} %bitcast.175), kind=kOutput, calls=%fused_computation.6.clone.1 | convolution fusion | flops 1078460416 | bytes 5249024 | tf_op jit(solution)/shard_map/while/body/eval_jaxpr/rak,aukjn->rujn/dot_general | solution.py:100
  188.1 10.2 %add_reduce_fusion.2 = (f32[1024]{0:T(1024)S(1)}, f32[1024]{0:T(1024)S(1)}) fusion(f32[4,2,64]{2,1,0:T(2,128)S(1)} %add_add_fusion.4, f32[1024]{0:T(1024)S(1)} %get-tuple-element.146, f32[1024,4,2,128]{0,3,2,1:T(8,128)S(1)} %convolution_bitcast_fusion.8, f32[1024,4,2,128]{0,3,2,1:T(8,128)S(1)} %convolution_bitcast_fusion.9), kind=kLoop, calls=%fused_computation.13.clone.1 | loop fusion | flops 9435136 | bytes 8402944 | tf_op jit(solution)/shard_map/while/body/eval_jaxpr/reduce_sum | solution.py:108
  202.9 9.0 %convolution_bitcast_fusion.9 = f32[1024,4,2,128]{0,3,2,1:T(8,128)S(1)} fusion(f32[8,64]{1,0:T(8,128)S(1)} %add_add_fusion.5, f32[1024]{0:T(1024)S(1)} %get-tuple-element.147, bf16[8,4,64,2,128]{4,2,3,1,0:T(8,128)(2,1)S(1)} %bitcast.174), kind=kOutput, calls=%fused_computation.7.clone.1 | convolution fusion | flops 1078460416 | bytes 5249024 | tf_op jit(solution)/shard_map/while/body/eval_jaxpr/rak,aukjn->rujn/dot_general | solution.py:97
  211.9 9.1 %convolution_bitcast_fusion.8 = f32[1024,4,2,128]{0,3,2,1:T(8,128)S(1)} fusion(f32[8,64]{1,0:T(8,128)S(1)} %add_add_fusion.5, f32[1024]{0:T(1024)S(1)} %get-tuple-element.147, bf16[8,4,64,2,128]{4,2,3,1,0:T(8,128)(2,1)S(1)} %bitcast.175), kind=kOutput, calls=%fused_computation.6.clone.1 | convolution fusion | flops 1078460416 | bytes 5249024 | tf_op jit(solution)/shard_map/while/body/eval_jaxpr/rak,aukjn->rujn/dot_general | solution.py:100
  220.9 10.2 %add_reduce_fusion.2 = (f32[1024]{0:T(1024)S(1)}, f32[1024]{0:T(1024)S(1)}) fusion(f32[4,2,64]{2,1,0:T(2,128)S(1)} %add_add_fusion.4, f32[1024]{0:T(1024)S(1)} %get-tuple-element.146, f32[1024,4,2,128]{0,3,2,1:T(8,128)S(1)} %convolution_bitcast_fusion.8, f32[1024,4,2,128]{0,3,2,1:T(8,128)S(1)} %convolution_bitcast_fusion.9), kind=kLoop, calls=%fused_computation.13.clone.1 | loop fusion | flops 9435136 | bytes 8402944 | tf_op jit(solution)/shard_map/while/body/eval_jaxpr/reduce_sum | solution.py:108
  231.2 12.5 %all-gather = f32[8,4,8,128]{3,2,0,1:T(8,128)S(1)} all-gather(f32[2,4,8,128]{3,2,0,1:T(8,128)S(1)} %bitcast.184), channel_id=2, replica_groups=mesh['fs'=32,'pol'=4] {'pol'}, dimensions={0}, use_global_device_ids=true | all-gather | bytes 163840 | tf_op jit(solution)/shard_map/all_gather | solution.py:130
  (80 shorter events, 28.0 us)
Async XLA Ops:
  0.0 1.6 copy-start
  25.5 2.7 %copy-start.4 = (s32[64]{0:T(128)S(1)}, s32[64]{0:T(128)}, u32[]{:S(2)}) copy-start(s32[64]{0:T(128)} %param.11) | copy-start | bytes 772
  37.6 8.6 %copy-start.3 = (f32[8,512]{1,0:T(8,128)S(1)}, f32[8,512]{1,0:T(8,128)}, u32[]{:S(2)}) copy-start(f32[8,512]{1,0:T(8,128)} %param.15) | copy-start | bytes 49156
  37.7 8.7 %copy-start.2 = (s32[4,8,2,128]{3,2,1,0:T(2,128)S(1)}, s32[4,8,2,128]{3,2,1,0:T(2,128)}, u32[]{:S(2)}) copy-start(s32[4,8,2,128]{3,2,1,0:T(2,128)} %param.14) | copy-start | bytes 98308
  37.7 62.0 %all-to-all-start = ((bf16[32,4,64,2,128]{4,2,3,1,0:T(8,128)(2,1)}), bf16[32,4,64,2,128]{4,2,3,1,0:T(8,128)(2,1)}, u32[]{:S(2)}, u32[]{:S(2)}) async-start(bf16[32,4,64,2,128]{4,2,3,1,0:T(8,128)(2,1)} %select_select_fusion), calls=%async_computation | async-start | bytes 8388608 | tf_op jit(solution)/shard_map/all_to_all | solution.py:116
  62.7 16.5 %copy-start.1 = (s32[64]{0:T(128)S(1)}, s32[64]{0:T(128)}, u32[]{:S(2)}) copy-start(s32[64]{0:T(128)} %param.12) | copy-start | bytes 772
where the time goes:
time: 249 us; the launch traced here: 245 us
  matrix products  83.2 us (33%)
  other arithmetic  59.1 us (24%)
  local copies, waits for them, and re-layouts  53.4 us (21%)
  waiting for transfers between devices  19.6 us (8%)
  blocking collectives  12.5 us (5%)
  starting transfers between devices  8.51 us (3%)
  loops' own time  7.85 us (3%)
    reduce_sum x4, other arithmetic, degrid(): jnp.sum(real_part * col_cos + imag_part * col_sin, axis=(1, 2, 3)) / SG  40.9 us
    dot_general x4, matrix products, degrid(): jnp.einsum('rak,aukjn->rujn', row_sin, shaped, preferred_element_type=jnp...  36.3 us
    dot_general x4, matrix products, degrid(): jnp.einsum('rak,aukjn->rujn', row_cos, shaped, preferred_element_type=jnp...  35.9 us
    all_to_all x1, waiting for transfers between devices, on_device(): lax.all_to_all(picked, 'fs', split_axis=0, concat_axis=0, tiled=True)  19.6 us
    gather x2, local copies, waits for them, and re-layouts, on_device(): right = jnp.take(jones_table, station_ids[:, :, 1, :], axis=1)  16.3 us
    gather x2, local copies, waits for them, and re-layouts, on_device(): left = jnp.take(jones_table, station_ids[:, :, 0, :], axis=1)  16.3 us
    all_gather x1, blocking collectives, on_device(): components = lax.all_gather(own_vis[None], 'pol', axis=0, tiled=True)  12.5 us
    another operation x2, other arithmetic  10.1 us
  transfers between devices with their start and end apart: 1, of which 1 were waited for; matrix products, arithmetic and copies ran while one was open for 14% of the time, Pallas kernels for 0%

commit v1 on v0

v1 whole, which is shorter than its diff:
```python
import math

import jax
import jax.numpy as jnp
import numpy as np
from jax import lax
from jax.experimental import pallas as pl
from jax.experimental.pallas import tpu as pltpu
from jax.sharding import PartitionSpec as P

R = 8
W = 64
S = 64
MAXB = 8
VB = 128
FH = 4096
SG = 512
CAP = 4
UNITS = 256
VMEM_LIMIT = 48 * 1024 * 1024
F32 = jnp.float32
BF16 = jnp.bfloat16


def first_table():
    index = np.arange(W)
    angles = (index[:, None] * index[None, :] % W) * (2.0 * math.pi / W)
    return np.concatenate([np.cos(angles), np.sin(angles)], axis=0).astype(BF16)


def second_table():
    k1 = np.arange(W)[:, None, None]
    k2 = np.arange(S)[None, :, None]
    n1 = np.arange(W)[None, None, :]
    angles = (n1 * (k1 + W * k2) % FH) * (2.0 * math.pi / FH)
    cos, sin = np.cos(angles), np.sin(angles)
    upper = np.concatenate([cos, -sin], axis=2)
    lower = np.concatenate([sin, cos], axis=2)
    return np.concatenate([upper, lower], axis=1).astype(BF16)


def mirror_table():
    table = np.zeros((2 * W, 2 * W), np.float32)
    index = np.arange(W)
    table[W - 1 - index, index] = 1.0
    table[2 * W - 1 - index, W + index] = 1.0
    return table.astype(BF16)


SIN_TERMS = (3.14159264, -5.16771008, 2.55007752, -0.598291286, 0.0776576603)
COS_TERMS = (0.999999953, -4.93479283, 4.05841135, -1.33187657, 0.219689611)


def polynomial(terms, x):
    total = jnp.full_like(x, terms[-1])
    for term in terms[-2::-1]:
        total = total * x + term
    return total


def turns_to_phase(turns):
    part = turns - jnp.round(turns)
    square = part * part
    half_sin = part * polynomial(SIN_TERMS, square)
    half_cos = polynomial(COS_TERMS, square)
    twice = half_sin + half_sin
    return (1.0 - twice * half_sin, twice * half_cos)


def rotate(cos, sin, step_cos, step_sin):
    return (cos * step_cos - sin * step_sin, sin * step_cos + cos * step_sin)


def transform_kernel(facets_ref, first_ref, second_ref, mirror_ref, out_ref, rows, sections, mixed):
    mirror = mirror_ref[...]
    piece = 512

    @pl.loop(0, FH // piece)
    def _(step):
        at = pl.ds(pl.multiple_of(step * piece, piece), piece)
        rows[0, at, :] = jnp.dot(facets_ref[0, at, :], mirror, preferred_element_type=F32)
        rows[1, at, :] = facets_ref[1, at, :].astype(F32)

    first = first_ref[...]

    @pl.loop(0, W // 8)
    def _(step):
        for inner in range(8):
            n1 = step * 8 + inner
            strip = jnp.concatenate([rows[f, pl.ds(n1, W, stride=W), :] for f in range(2)], axis=1)
            part = jnp.dot(first, strip.astype(BF16), preferred_element_type=F32)
            for f in range(2):
                lanes = slice(2 * W * f, 2 * W * (f + 1))
                sections[f, pl.ds(n1, W, stride=2 * W), :] = part[:W, lanes]
                sections[f, pl.ds(W + n1, W, stride=2 * W), :] = part[W:, lanes]

    low_lanes = lax.broadcasted_iota(jnp.int32, (S, 2 * W), 1) < W

    def window(k1):
        at = pl.ds(pl.multiple_of(k1 * 2 * W, 2 * W), 2 * W)
        section = jnp.concatenate([sections[f, at, :] for f in range(2)], axis=1).astype(BF16)
        return jnp.dot(second_ref[k1], section, preferred_element_type=F32)

    @pl.loop(0, W // 4)
    def _(step):
        for inner in range(2):
            index = step * 2 + inner
            above = window(W // 2 + index)
            below = window(W // 2 - 1 - index)
            for half, grid in enumerate((above + below, above - below)):
                cos_0, cos_1 = grid[:S, : 2 * W], grid[:S, 2 * W :]
                sin_0, sin_1 = grid[S:, : 2 * W], grid[S:, 2 * W :]
                cos_sum, cos_gap = cos_1 + cos_0, cos_1 - cos_0
                sin_sum, sin_gap = sin_1 + sin_0, sin_1 - sin_0
                real = jnp.where(low_lanes, cos_sum, cos_gap) + pltpu.roll(
                    jnp.where(low_lanes, -sin_gap, sin_sum), W, 1
                )
                imag = pltpu.roll(jnp.where(low_lanes, -cos_gap, cos_sum), W, 1) - jnp.where(
                    low_lanes, sin_sum, sin_gap
                )
                mixed[pl.ds(64 * half + index, S, stride=2 * W), :] = real
                mixed[pl.ds(64 * half + 32 + index, S, stride=2 * W), :] = imag

    @pl.loop(0, S // 4)
    def _(step):
        for inner in range(4):
            s = step * 4 + inner
            at = pl.ds(pl.multiple_of(s * 2 * W, 2 * W), 2 * W)
            out_ref[s] = mixed[at, :].astype(BF16)


def transform(strips):
    return pl.pallas_call(
        transform_kernel,
        out_shape=jax.ShapeDtypeStruct((S, 2 * W, 2 * W), BF16),
        in_specs=[pl.BlockSpec(memory_space=pltpu.VMEM)] * 4,
        out_specs=pl.BlockSpec(memory_space=pltpu.VMEM),
        scratch_shapes=[
            pltpu.VMEM((2, FH, 2 * W), F32),
            pltpu.VMEM((2, 2 * FH, 2 * W), F32),
            pltpu.VMEM((2 * FH, 2 * W), F32),
        ],
        compiler_params=pltpu.CompilerParams(vmem_limit_bytes=VMEM_LIMIT),
        cost_estimate=pl.CostEstimate(flops=1_000_000_000, bytes_accessed=8_000_000, transcendentals=0),
    )(strips, jnp.asarray(first_table()), jnp.asarray(second_table()), jnp.asarray(mirror_table()))


def degrid_kernel(units, total, limits, centres, own_ref, other_ref, coords_ref, out_ref, steps, sums):
    @pl.loop(0, 16)
    def _(o):
        for c in range(CAP):
            for axis in range(2):
                cos, sin = turns_to_phase(coords_ref[o, axis, c] * (8.0 / SG))
                steps[2 * axis, o * CAP + c] = cos
                steps[2 * axis + 1, o * CAP + c] = sin

    cells = (lax.broadcasted_iota(jnp.int32, (8, VB), 0).astype(F32) + 0.5) * (1.0 / SG)

    def ladder(position, step_cos, step_sin, count):
        cos, sin = turns_to_phase(position * cells)
        both = [(cos, sin)]
        step_cos = jnp.broadcast_to(step_cos, (8, VB))
        step_sin = jnp.broadcast_to(step_sin, (8, VB))
        for _ in range(count - 1):
            cos, sin = rotate(cos, sin, step_cos, step_sin)
            both.append((cos, sin))
        return both

    def unit(index):
        word = units[index]
        pair = word % 4
        s = (word // 4) % S
        g = word // (4 * S)
        o, c = g // CAP, g % CAP
        phases, weights = [], []
        for h in range(2):
            b = 2 * pair + h
            row = pl.ds(b, 1)
            along_y = ladder(coords_ref[o, 1, c, row, :], steps[2, g, row, :], steps[3, g, row, :], 8)
            phases.append(jnp.concatenate([t[0] for t in along_y] + [t[1] for t in along_y], axis=0).astype(BF16))
            weights.append(ladder(coords_ref[o, 0, c, row, :], steps[0, g, row, :], steps[1, g, row, :], 4))
        phases = jnp.concatenate(phases, axis=1)
        both = jnp.concatenate([own_ref[s], other_ref[s]], axis=0)
        grid = jnp.dot(both, phases, preferred_element_type=F32)
        for h in range(2):
            b = 2 * pair + h
            lanes = slice(VB * h, VB * (h + 1))
            for q in range(2):
                real = imag = None
                for i, (cos, sin) in enumerate(weights[h]):
                    at = 128 * q + 8 * i
                    sum_real, sum_imag = grid[at : at + 8, lanes], grid[at + 32 : at + 40, lanes]
                    gap_real, gap_imag = grid[at + 64 : at + 72, lanes], grid[at + 96 : at + 104, lanes]
                    step_real = cos * sum_real + sin * gap_imag
                    step_imag = cos * sum_imag - sin * gap_real
                    real = step_real if real is None else real + step_real
                    imag = step_imag if imag is None else imag + step_imag
                at = pl.ds(pl.multiple_of(8 * b, 8), 8)
                sums[4 * g + 2 * q, at, :] = real
                sums[4 * g + 2 * q + 1, at, :] = imag

    @pl.loop(0, total[0])
    def _(index):
        unit(index)

    centre_x, centre_own, centre_other = centres[0], centres[1], centres[2]

    @pl.loop(0, 16 * CAP)
    def _(g):
        o, c = g // CAP, g % CAP

        @pl.when(limits[g] > 0)
        def _():
            x, y = coords_ref[o, 0, c], coords_ref[o, 1, c]
            real = imag = jnp.zeros((MAXB, VB), F32)
            for q, centre_y in enumerate((centre_own, centre_other)):
                total_real = sums[4 * g + 2 * q, pl.ds(0, MAXB, stride=8), :]
                total_imag = sums[4 * g + 2 * q + 1, pl.ds(0, MAXB, stride=8), :]
                for r in range(1, 8):
                    total_real = total_real + sums[4 * g + 2 * q, pl.ds(r, MAXB, stride=8), :]
                    total_imag = total_imag + sums[4 * g + 2 * q + 1, pl.ds(r, MAXB, stride=8), :]
                cos, sin = turns_to_phase((x * centre_x + y * centre_y) * (1.0 / SG))
                real = real + (cos * total_real + sin * total_imag)
                imag = imag + (cos * total_imag - sin * total_real)
            scale = 1.0 / (math.sqrt(FH) * SG)
            value = (jnp.concatenate([real, imag], axis=0) * scale).astype(BF16)
            for copy in range(4):
                out_ref[o, copy, c] = value


def degrid(units, total, limits, centres, own, other, coords):
    smem = pl.BlockSpec(memory_space=pltpu.SMEM)
    vmem = pl.BlockSpec(memory_space=pltpu.VMEM)
    return pl.pallas_call(
        degrid_kernel,
        out_shape=jax.ShapeDtypeStruct((16, 4, CAP, 2 * MAXB, VB), BF16),
        in_specs=[smem] * 4 + [vmem] * 3,
        out_specs=vmem,
        scratch_shapes=[
            pltpu.VMEM((4, 16 * CAP, MAXB, VB), F32),
            pltpu.VMEM((16 * CAP * 4, 8 * MAXB, VB), F32),
        ],
        compiler_params=pltpu.CompilerParams(vmem_limit_bytes=VMEM_LIMIT),
        cost_estimate=pl.CostEstimate(flops=4_000_000_000, bytes_accessed=8_000_000, transcendentals=0),
    )(units, total, limits, centres, own, other, coords)


def correct_kernel(limits, place, parts_ref, stations_ref, table_ref, out_ref):
    me, pol = place[0], place[1]
    row_side, col_side = pol // 2, pol % 2
    block = lax.broadcasted_iota(jnp.int32, (MAXB, VB), 0)

    def side(which):
        return [
            jnp.where(which == 1, table_ref[4:8, at : at + VB], table_ref[0:4, at : at + VB])
            for at in range(0, 4 * VB, VB)
        ]

    def entry(table, row, station):
        lane, chunk = station % VB, station // VB
        value = jnp.zeros((MAXB, VB), F32)
        for part in range(4):
            line = jnp.broadcast_to(table[part][row : row + 1], (MAXB, VB))
            value = jnp.where(chunk == part, jnp.take_along_axis(line, lane, axis=1), value)
        return value

    left_table, right_table = side(row_side), side(col_side)

    for c in range(CAP):
        left, right = stations_ref[c, 0], stations_ref[c, 1]
        lefts = [[entry(left_table, 2 * k + ri, left) for ri in range(2)] for k in range(2)]
        rights = [[entry(right_table, 2 * k + ri, right) for ri in range(2)] for k in range(2)]
        total_real = total_imag = jnp.zeros((MAXB, VB), F32)
        for inner_row in range(2):
            part_real = part_imag = jnp.zeros((MAXB, VB), F32)
            for inner_col in range(2):
                comp = parts_ref[0, 2 * inner_row + inner_col, c].astype(F32)
                for o in range(1, 16):
                    comp = comp + parts_ref[o, 2 * inner_row + inner_col, c].astype(F32)
                real, imag = comp[:MAXB], comp[MAXB:]
                right_real, right_imag = rights[inner_col]
                part_real = part_real + (real * right_real + imag * right_imag)
                part_imag = part_imag + (imag * right_real - real * right_imag)
            left_real, left_imag = lefts[inner_row]
            total_real = total_real + (left_real * part_real - left_imag * part_imag)
            total_imag = total_imag + (left_real * part_imag + left_imag * part_real)
        keep = block < limits[me * CAP + c]
        out_ref[0, 0, c] = jnp.where(keep, total_real, 0.0)
        out_ref[0, 1, c] = jnp.where(keep, total_imag, 0.0)


def correct(limits, place, parts, stations, table):
    smem = pl.BlockSpec(memory_space=pltpu.SMEM)
    vmem = pl.BlockSpec(memory_space=pltpu.VMEM)
    return pl.pallas_call(
        correct_kernel,
        out_shape=jax.ShapeDtypeStruct((1, 2, CAP, MAXB, VB), F32),
        in_specs=[smem] * 2 + [vmem] * 3,
        out_specs=vmem,
        compiler_params=pltpu.CompilerParams(vmem_limit_bytes=VMEM_LIMIT),
    )(limits, place, parts, stations, table)


def on_device(facets, owners, counts, coords, station_ids, jones_table):
    chip = lax.axis_index("z") * 4 + lax.axis_index("x")
    core = lax.axis_index("core")
    pol = lax.axis_index("pol")

    spread = jnp.broadcast_to(coords[None], (16,) + coords.shape)
    coords_all = lax.all_to_all(spread, ("z", "x"), split_axis=0, concat_axis=0, tiled=True)

    index = jnp.arange(S, dtype=jnp.int32)
    before = index[None, :] < index[:, None]
    mine = owners % 2 == core
    pairs = jnp.where(mine, (counts + 1) // 2, 0)
    rank = jnp.sum(jnp.where(before & (owners[None, :] == owners[:, None]), 1, 0), axis=1)
    first_unit = jnp.sum(jnp.where(before, pairs[None, :], 0), axis=1)
    slot = (owners // 2) * CAP + rank
    unit_index = jnp.arange(UNITS, dtype=jnp.int32)[:, None]
    offset = unit_index - first_unit[None, :]
    words = (slot * S + index)[None, :] * 4 + offset
    units = jnp.sum(jnp.where((offset >= 0) & (offset < pairs[None, :]), words, 0), axis=1)
    total = jnp.sum(pairs).reshape(1)
    slots = jnp.arange(16 * CAP, dtype=jnp.int32)[:, None]
    limits = jnp.sum(jnp.where((slots == slot[None, :]) & mine[None, :], counts[None, :], 0), axis=1)

    first_facet = 2 * (chip * 2 + core)
    other_facet = 2 * (chip * 2 + 1 - core)
    half = SG // 2
    centres = jnp.stack(
        [
            W * (first_facet // R) + (W // 2 - 0.5 - half),
            W * (first_facet % R) + (W - 0.5 - half),
            W * (other_facet % R) + (W - 0.5 - half),
        ]
    ).astype(F32)

    own = transform(facets[0])
    other = lax.ppermute(own, "core", [(0, 1), (1, 0)])
    parts = degrid(units, total, limits, centres, own, other, coords_all)
    parts = parts.reshape(64, CAP, 2 * MAXB, VB)
    parts = lax.all_to_all(parts, ("z", "x", "pol"), split_axis=0, concat_axis=0, tiled=True)
    parts = parts.reshape(16, 4, CAP, 2 * MAXB, VB)
    stations = jnp.moveaxis(station_ids, 2, 1)
    place = jnp.stack([chip, pol]).astype(jnp.int32)
    return correct(limits, place, parts, stations, jones_table)


def solution(mesh):
    split = jax.sharding.Mesh(mesh.devices.reshape(4, 4, 2, 4), ("z", "x", "core", "pol"))
    fs = ("z", "x", "core")
    return jax.shard_map(
        on_device,
        mesh=split,
        in_specs=(P("pol", fs, None, None), P(), P(), P(None, fs, None, None), P(fs, None, None, None), P()),
        out_specs=P("pol", None, fs, None, None),
        check_vma=False,
    )
```

time: 249 us -> 94.9 us (0.38); the launches traced: 245 us -> 93.9 us
  matrix products: 83.2 us -> 0 us
  other arithmetic: 59.1 us -> 1.3 us
  local copies, waits for them, and re-layouts: 53.4 us -> 3.99 us
  Pallas kernels: 0 us -> 44.5 us
  blocking collectives: 12.5 us -> 0 us
  waiting for transfers between devices: 19.6 us -> 29.3 us
  loops' own time: 7.85 us -> 0 us
  starting transfers between devices: 8.51 us -> 14.8 us
    dot_general x12 -> x0, matrix products: 83.2 us -> none  [the longest x4 36.3 us: degrid(): jnp.einsum('rak,aukjn->rujn', row_sin, shaped, preferred_element_type=jnp...]
    pallas_call x0 -> x3, Pallas kernels: none -> 44.5 us  [the longest x1 23.3 us: degrid(): pl.pallas_call(degrid_kernel, out_shape=jax.ShapeDtypeStruct((16, 4, CAP,...]
    reduce_sum x5, other arithmetic: 41.1 us -> 1.15 us  [the longest x1 0.64 us: on_device(): total = jnp.sum(pairs).reshape(1)]
    gather x6 -> x0, local copies, waits for them, and re-layouts: 37.8 us -> none  [the longest x2 16.3 us: on_device(): right = jnp.take(jones_table, station_ids[:, :, 1, :], axis=1)]
    all_gather x1 -> x0, blocking collectives: 12.5 us -> none  [on_device(): components = lax.all_gather(own_vis[None], 'pol', axis=0, tiled=True)]
    another operation x5 -> x2, other arithmetic: 10.4 us -> 0.15 us  [the longest x1 0.08 us: on_device(): place = jnp.stack([chip, pol]).astype(jnp.int32)]
    all_to_all x1 -> x2, waiting for transfers between devices: 19.6 us -> 29.3 us  [the longest x1 18.3 us: on_device(): lax.all_to_all(parts, ('z', 'x', 'pol'), split_axis=0, concat_axis=0, til...]
    another operation x1 -> x0, loops' own time: 7.85 us -> none  [on_device(): visible = lax.map(slot_predict, jnp.arange(capacity, dtype=jnp.int32))]
  transfers between devices with their start and end apart: 1 -> 3, of which waited for: 1 -> 2; matrix products, arithmetic and copies ran while one was open for 14% -> 2% of each run, Pallas kernels for 0% -> 0%
where the time goes in v1:
time: 94.9 us; the launch traced here: 93.9 us
  Pallas kernels  44.5 us (47%)
  waiting for transfers between devices  29.3 us (31%)
  starting transfers between devices  14.8 us (16%)
  local copies, waits for them, and re-layouts  3.99 us (4%)
  other arithmetic  1.3 us (1%)
    pallas_call x1, Pallas kernels, degrid(): pl.pallas_call(degrid_kernel, out_shape=jax.ShapeDtypeStruct((16, 4, CAP,...  23.3 us
    pallas_call x1, Pallas kernels, transform(): pl.pallas_call(transform_kernel, out_shape=jax.ShapeDtypeStruct((S, 2 * W...  19.8 us
    all_to_all x1, waiting for transfers between devices, on_device(): lax.all_to_all(parts, ('z', 'x', 'pol'), split_axis=0, concat_axis=0, til...  18.3 us
    all_to_all x1, waiting for transfers between devices, on_device(): lax.all_to_all(spread, ('z', 'x'), split_axis=0, concat_axis=0, tiled=True)  10.9 us
    all_to_all x1, starting transfers between devices, on_device(): lax.all_to_all(spread, ('z', 'x'), split_axis=0, concat_axis=0, tiled=True)  7.94 us
    all_to_all x1, starting transfers between devices, on_device(): lax.all_to_all(parts, ('z', 'x', 'pol'), split_axis=0, concat_axis=0, til...  6.74 us
    unnamed x17, local copies, waits for them, and re-layouts  3.13 us
  transfers between devices with their start and end apart: 3, of which 2 were waited for; matrix products, arithmetic and copies ran while one was open for 2% of the time, Pallas kernels for 0%

profile of v1, /device:TPU:0, one launch (start us, length us, event | category | flops | bytes accessed | tf_op | source)
XLA Modules:
  0.0 93.9 jit_solution(2376051088219227399)
XLA Ops:
  0.0 1.6 %copy-done = bf16[1,2,4096,128]{3,2,1,0:T(8,128)(2,1)S(1)} copy-done((bf16[1,2,4096,128]{3,2,1,0:T(8,128)(2,1)S(1)}, bf16[1,2,4096,128]{3,2,1,0:T(8,128)(2,1)}, u32[]{:S(2)}) %copy-start) | copy-done | bytes 2097176
  1.6 0.8 copy-done.1
  2.4 0.8 copy-done.2
  3.1 19.8 %shard_map.91.own_ref = bf16[64,128,128]{2,1,0:T(8,128)(2,1)S(1)} custom-call(bf16[2,4096,128]{2,1,0:T(8,128)(2,1)S(1)} %bitcast.13, bf16[128,64]{1,0:T(8,128)(2,1)S(1)} %copy-done.1, bf16[64,128,128]{2,1,0:T(8,128)(2,1)} %constant.98.clone.second_ref, bf16[128,128]{1,0:T(8,128)(2,1)S(1)} %copy-done.2), custom_call_target="tpu_custom_call" | custom-call | flops 1000000000 | bytes 8000000 | tf_op jit(solution)/shard_map/pallas_call | solution.py:133
  22.9 0.1 collective-permute-start
  23.0 0.0 copy-done.4
  23.0 0.9 broadcast_in_dim.51
  23.9 7.9 %all-to-all-start = ((f32[16,2,4,8,128]{4,3,2,1,0:T(8,128)}), f32[16,2,4,8,128]{4,3,2,1,0:T(8,128)S(1)}, u32[]{:S(2)}, u32[]{:S(2)}) async-start(f32[16,2,4,8,128]{4,3,2,1,0:T(8,128)} %broadcast_in_dim.51), calls=%async_computation | async-start | bytes 1048576 | tf_op jit(solution)/shard_map/all_to_all | solution.py:310
  31.8 0.0 copy-done.7
  31.8 0.2 select_reduce_fusion.3
  32.0 0.0 copy-done.6
  32.0 0.6 fusion.7
  32.6 0.1 pad_maximum_fusion.centres
  32.7 0.1 select_reduce_fusion.1
  32.8 0.1 select_reduce_fusion.2.limits
  32.9 0.1 select_reduce_fusion.units
  33.1 10.9 %all-to-all-done.coords_ref = f32[16,2,4,8,128]{4,3,2,1,0:T(8,128)S(1)} async-done(((f32[16,2,4,8,128]{4,3,2,1,0:T(8,128)}), f32[16,2,4,8,128]{4,3,2,1,0:T(8,128)S(1)}, u32[]{:S(2)}, u32[]{:S(2)}) %all-to-all-start) | async-done | bytes 524320 | tf_op jit(solution)/shard_map/all_to_all | solution.py:310
  44.0 0.0 collective-permute-done.other_ref
  44.0 23.3 %shard_map.92 = bf16[16,4,4,16,128]{4,3,2,1,0:T(8,128)(2,1)} custom-call(s32[256]{0:T(256)S(1)} %select_reduce_fusion.units, s32[1]{0:T(128)} %bitcast.2.total, s32[64]{0:T(128)S(1)} %select_reduce_fusion.2.limits, f32[3]{0:T(128)S(1)} %pad_maximum_fusion.centres, bf16[64,128,128]{2,1,0:T(8,128)(2,1)S(1)} %shard_map.91.own_ref, ...), custom_call_target="tpu_custom_call" | custom-call | flops 4000000000 | bytes 8000000 | tf_op jit(solution)/shard_map/pallas_call | solution.py:234
  67.3 6.7 %all-to-all-start.1 = ((bf16[64,4,16,128]{3,2,1,0:T(8,128)(2,1)}), bf16[64,4,16,128]{3,2,1,0:T(8,128)(2,1)S(1)}, u32[]{:S(2)}, u32[]{:S(2)}) async-start(bf16[64,4,16,128]{3,2,1,0:T(8,128)(2,1)} %bitcast.7), calls=%async_computation.1 | async-start | bytes 2097152 | tf_op jit(solution)/shard_map/all_to_all | solution.py:342
  74.1 0.1 pad_add_fusion.place
  74.2 18.3 %all-to-all-done.1 = bf16[64,4,16,128]{3,2,1,0:T(8,128)(2,1)S(1)} async-done(((bf16[64,4,16,128]{3,2,1,0:T(8,128)(2,1)}), bf16[64,4,16,128]{3,2,1,0:T(8,128)(2,1)S(1)}, u32[]{:S(2)}, u32[]{:S(2)}) %all-to-all-start.1) | async-done | bytes 1048608 | tf_op jit(solution)/shard_map/all_to_all | solution.py:342
  92.5 0.0 copy-done.3
  92.5 1.4 %shard_map.93 = f32[1,2,4,8,128]{4,3,2,1,0:T(8,128)} custom-call(s32[64]{0:T(128)S(1)} %select_reduce_fusion.2.limits, s32[2]{0:T(128)S(1)} %pad_add_fusion.place, bf16[16,4,4,16,128]{4,3,2,1,0:T(8,128)(2,1)S(1)} %bitcast.12, s32[4,2,8,128]{3,2,1,0:T(8,128)S(1)} %bitcast.14, f32[8,512]{1,0:T(8,128)S(1)} %copy-done.3), custom_call_target="tpu_custom_call" | custom-call | tf_op jit(solution)/shard_map/pallas_call | solution.py:295
  (10 shorter events, 0.0 us)
Async XLA Ops:
  0.0 1.6 %copy-start = (bf16[1,2,4096,128]{3,2,1,0:T(8,128)(2,1)S(1)}, bf16[1,2,4096,128]{3,2,1,0:T(8,128)(2,1)}, u32[]{:S(2)}) copy-start(bf16[1,2,4096,128]{3,2,1,0:T(8,128)(2,1)} %param.9) | copy-start | bytes 6291460
  1.6 0.8 copy-start.1
  2.4 0.8 copy-start.2
  3.1 19.9 %copy-start.4 = (f32[2,4,8,128]{3,2,1,0:T(8,128)S(1)}, f32[2,4,8,128]{3,2,1,0:T(8,128)}, u32[]{:S(2)}) copy-start(f32[2,4,8,128]{3,2,1,0:T(8,128)} %param.12) | copy-start | bytes 98308
  3.1 28.7 %copy-start.7 = (s32[64]{0:T(128)S(1)}, s32[64]{0:T(128)}, u32[]{:S(2)}) copy-start(s32[64]{0:T(128)} %param.10) | copy-start | bytes 772
  3.1 28.9 %copy-start.6 = (s32[64]{0:T(128)S(1)}, s32[64]{0:T(128)}, u32[]{:S(2)}) copy-start(s32[64]{0:T(128)} %param.11) | copy-start | bytes 772
  22.9 21.1 %collective-permute-start = (bf16[64,128,128]{2,1,0:T(8,128)(2,1)S(1)}, bf16[64,128,128]{2,1,0:T(8,128)(2,1)}, u32[]{:S(2)}, u32[]{:S(2)}) collective-permute-start(bf16[64,128,128]{2,1,0:T(8,128)(2,1)S(1)} %shard_map.91.own_ref), channel_id=1, source_target_pairs={{0,4},{4,0},{1,5},{5,1},{2,6},{6,2},{3,7},{7,3},{8,12},{12,8},{9,1... | collective-permute-start | bytes 6291464 | tf_op jit(solution)/shard_map/ppermute | solution.py:339
  23.9 20.1 %all-to-all-start = ((f32[16,2,4,8,128]{4,3,2,1,0:T(8,128)}), f32[16,2,4,8,128]{4,3,2,1,0:T(8,128)S(1)}, u32[]{:S(2)}, u32[]{:S(2)}) async-start(f32[16,2,4,8,128]{4,3,2,1,0:T(8,128)} %broadcast_in_dim.51), calls=%async_computation | async-start | bytes 1048576 | tf_op jit(solution)/shard_map/all_to_all | solution.py:310
  67.3 6.8 %copy-start.5 = (s32[4,8,2,128]{3,2,1,0:T(2,128)S(1)}, s32[4,8,2,128]{3,2,1,0:T(2,128)}, u32[]{:S(2)}) copy-start(s32[4,8,2,128]{3,2,1,0:T(2,128)} %param.13) | copy-start | bytes 98308
  67.3 25.2 %copy-start.3 = (f32[8,512]{1,0:T(8,128)S(1)}, f32[8,512]{1,0:T(8,128)}, u32[]{:S(2)}) copy-start(f32[8,512]{1,0:T(8,128)} %table_ref.1) | copy-start | bytes 49156
  67.3 25.2 %all-to-all-start.1 = ((bf16[64,4,16,128]{3,2,1,0:T(8,128)(2,1)}), bf16[64,4,16,128]{3,2,1,0:T(8,128)(2,1)S(1)}, u32[]{:S(2)}, u32[]{:S(2)}) async-start(bf16[64,4,16,128]{3,2,1,0:T(8,128)(2,1)} %bitcast.7), calls=%async_computation.1 | async-start | bytes 2097152 | tf_op jit(solution)/shard_map/all_to_all | solution.py:342

commit v2 on v1

--- a/solution.py
+++ b/solution.py
@@ -1,3 +1,4 @@
+import functools
 import math
 
 import jax
@@ -17,6 +18,8 @@
 SG = 512
 CAP = 4
 UNITS = 256
+GROUP = 16
+TOGETHER = 8
 VMEM_LIMIT = 48 * 1024 * 1024
 F32 = jnp.float32
 BF16 = jnp.bfloat16
@@ -25,7 +28,8 @@
 def first_table():
     index = np.arange(W)
     angles = (index[:, None] * index[None, :] % W) * (2.0 * math.pi / W)
-    return np.concatenate([np.cos(angles), np.sin(angles)], axis=0).astype(BF16)
+    waves = np.concatenate([np.cos(angles[: W // 2 + 1]), np.sin(angles[1 : W // 2])], axis=0)
+    return np.kron(waves, np.eye(GROUP)).astype(BF16)
 
 
 def second_table():
@@ -34,8 +38,9 @@
     n1 = np.arange(W)[None, None, :]
     angles = (n1 * (k1 + W * k2) % FH) * (2.0 * math.pi / FH)
     cos, sin = np.cos(angles), np.sin(angles)
-    upper = np.concatenate([cos, -sin], axis=2)
-    lower = np.concatenate([sin, cos], axis=2)
+    sign = np.where(k1 % (W // 2) == 0, 0.0, np.where(k1 < W // 2, 1.0, -1.0))
+    upper = np.concatenate([cos, -sin * sign], axis=2)
+    lower = np.concatenate([sin, cos * sign], axis=2)
     return np.concatenate([upper, lower], axis=1).astype(BF16)
 
 
@@ -71,43 +76,43 @@
     return (cos * step_cos - sin * step_sin, sin * step_cos + cos * step_sin)
 
 
-def transform_kernel(facets_ref, first_ref, second_ref, mirror_ref, out_ref, rows, sections, mixed):
+def transform_kernel(facets_ref, first_ref, second_ref, mirror_ref, out_ref, mirrored, sections, mixed):
     mirror = mirror_ref[...]
-    piece = 512
-
-    @pl.loop(0, FH // piece)
+    half = W // 2
+
+    @pl.loop(0, W // GROUP)
+    def _(h):
+        at = pl.ds(pl.multiple_of(h * GROUP, GROUP), GROUP)
+        mirrored[...] = jnp.dot(
+            facets_ref[0, :, at, :].reshape(W * GROUP, 2 * W), mirror, preferred_element_type=F32
+        ).astype(BF16)
+        strips = jnp.concatenate([mirrored[...], facets_ref[1, :, at, :].reshape(W * GROUP, 2 * W)], axis=1)
+        for piece in range(4):
+            rows = slice(piece * 256, piece * 256 + 256)
+            part = jnp.dot(first_ref[rows, :], strips, preferred_element_type=F32).astype(BF16)
+            for f in range(2):
+                block = part[:, 2 * W * f : 2 * W * (f + 1)].reshape(16, GROUP, 2 * W)
+                sections[f, piece * 16 : piece * 16 + 16, at, :] = block
+
+    low_lanes = lax.broadcasted_iota(jnp.int32, (S, 2 * W), 1) < W
+
+    def window(k1, fold):
+        section = jnp.concatenate(
+            [
+                jnp.concatenate([sections[f, fold], sections[f, jnp.minimum(half + fold, W - 1)]], axis=0)
+                for f in range(2)
+            ],
+            axis=1,
+        )
+        return jnp.dot(second_ref[k1], section, preferred_element_type=F32)
+
+    @pl.loop(0, half // 4)
     def _(step):
-        at = pl.ds(pl.multiple_of(step * piece, piece), piece)
-        rows[0, at, :] = jnp.dot(facets_ref[0, at, :], mirror, preferred_element_type=F32)
-        rows[1, at, :] = facets_ref[1, at, :].astype(F32)
-
-    first = first_ref[...]
-
-    @pl.loop(0, W // 8)
-    def _(step):
-        for inner in range(8):
-            n1 = step * 8 + inner
-            strip = jnp.concatenate([rows[f, pl.ds(n1, W, stride=W), :] for f in range(2)], axis=1)
-            part = jnp.dot(first, strip.astype(BF16), preferred_element_type=F32)
-            for f in range(2):
-                lanes = slice(2 * W * f, 2 * W * (f + 1))
-                sections[f, pl.ds(n1, W, stride=2 * W), :] = part[:W, lanes]
-                sections[f, pl.ds(W + n1, W, stride=2 * W), :] = part[W:, lanes]
-
-    low_lanes = lax.broadcasted_iota(jnp.int32, (S, 2 * W), 1) < W
-
-    def window(k1):
-        at = pl.ds(pl.multiple_of(k1 * 2 * W, 2 * W), 2 * W)
-        section = jnp.concatenate([sections[f, at, :] for f in range(2)], axis=1).astype(BF16)
-        return jnp.dot(second_ref[k1], section, preferred_element_type=F32)
-
-    @pl.loop(0, W // 4)
-    def _(step):
-        for inner in range(2):
-            index = step * 2 + inner
-            above = window(W // 2 + index)
-            below = window(W // 2 - 1 - index)
-            for half, grid in enumerate((above + below, above - below)):
+        for inner in range(4):
+            index = step * 4 + inner
+            above = window(half + index, half - index)
+            below = window(half - 1 - index, half - 1 - index)
+            for pick, grid in enumerate((above + below, above - below)):
                 cos_0, cos_1 = grid[:S, : 2 * W], grid[:S, 2 * W :]
                 sin_0, sin_1 = grid[S:, : 2 * W], grid[S:, 2 * W :]
                 cos_sum, cos_gap = cos_1 + cos_0, cos_1 - cos_0
@@ -118,15 +123,17 @@
                 imag = pltpu.roll(jnp.where(low_lanes, -cos_gap, cos_sum), W, 1) - jnp.where(
                     low_lanes, sin_sum, sin_gap
                 )
-                mixed[pl.ds(64 * half + index, S, stride=2 * W), :] = real
-                mixed[pl.ds(64 * half + 32 + index, S, stride=2 * W), :] = imag
-
-    @pl.loop(0, S // 4)
+                mixed[2 * pick, index] = real
+                mixed[2 * pick + 1, index] = imag
+
+    @pl.loop(0, S // 8)
     def _(step):
-        for inner in range(4):
-            s = step * 4 + inner
-            at = pl.ds(pl.multiple_of(s * 2 * W, 2 * W), 2 * W)
-            out_ref[s] = mixed[at, :].astype(BF16)
+        at = pl.ds(pl.multiple_of(step * 8, 8), 8)
+        for kind in range(4):
+            for i in range(0, half, 16):
+                halves = [jnp.swapaxes(mixed[kind, i + j : i + j + 8, at, :], 0, 1) for j in (0, 8)]
+                rows = slice(half * kind + i, half * kind + i + 16)
+                out_ref[at, rows, :] = jnp.concatenate(halves, axis=1).astype(BF16)
 
 
 def transform(strips):
@@ -136,16 +143,17 @@
         in_specs=[pl.BlockSpec(memory_space=pltpu.VMEM)] * 4,
         out_specs=pl.BlockSpec(memory_space=pltpu.VMEM),
         scratch_shapes=[
-            pltpu.VMEM((2, FH, 2 * W), F32),
-            pltpu.VMEM((2, 2 * FH, 2 * W), F32),
-            pltpu.VMEM((2 * FH, 2 * W), F32),
+            pltpu.VMEM((W * GROUP, 2 * W), BF16),
+            pltpu.VMEM((2, W, W, 2 * W), BF16),
+            pltpu.VMEM((4, W // 2, S, 2 * W), F32),
         ],
         compiler_params=pltpu.CompilerParams(vmem_limit_bytes=VMEM_LIMIT),
-        cost_estimate=pl.CostEstimate(flops=1_000_000_000, bytes_accessed=8_000_000, transcendentals=0),
-    )(strips, jnp.asarray(first_table()), jnp.asarray(second_table()), jnp.asarray(mirror_table()))
-
-
-def degrid_kernel(units, total, limits, centres, own_ref, other_ref, coords_ref, out_ref, steps, sums):
+        cost_estimate=pl.CostEstimate(flops=12_000_000_000, bytes_accessed=8_000_000, transcendentals=0),
+        name="transform",
+    )(strips.reshape(2, W, W, 2 * W), jnp.asarray(first_table()), jnp.asarray(second_table()), jnp.asarray(mirror_table()))
+
+
+def degrid_kernel(together, units, total, limits, centres, own_ref, other_ref, coords_ref, out_ref, steps, sums):
     @pl.loop(0, 16)
     def _(o):
         for c in range(CAP):
@@ -166,28 +174,28 @@
             both.append((cos, sin))
         return both
 
-    def unit(index):
+    def place(index):
         word = units[index]
-        pair = word % 4
-        s = (word // 4) % S
         g = word // (4 * S)
-        o, c = g // CAP, g % CAP
-        phases, weights = [], []
+        kept = jnp.where(index < total[0], g, 16 * CAP)
+        return (g // CAP, g % CAP, g, kept, (word // 4) % S, 2 * (word % 4))
+
+    def phases_of(o, c, g, kept, s, b):
+        blocks = []
         for h in range(2):
-            b = 2 * pair + h
-            row = pl.ds(b, 1)
-            along_y = ladder(coords_ref[o, 1, c, row, :], steps[2, g, row, :], steps[3, g, row, :], 8)
-            phases.append(jnp.concatenate([t[0] for t in along_y] + [t[1] for t in along_y], axis=0).astype(BF16))
-            weights.append(ladder(coords_ref[o, 0, c, row, :], steps[0, g, row, :], steps[1, g, row, :], 4))
-        phases = jnp.concatenate(phases, axis=1)
-        both = jnp.concatenate([own_ref[s], other_ref[s]], axis=0)
-        grid = jnp.dot(both, phases, preferred_element_type=F32)
+            row = pl.ds(b + h, 1)
+            along = ladder(coords_ref[o, 1, c, row, :], steps[2, g, row, :], steps[3, g, row, :], 8)
+            blocks.append(jnp.concatenate([t[0] for t in along] + [t[1] for t in along], axis=0).astype(BF16))
+        return jnp.concatenate(blocks, axis=1)
+
+    def finish(grid, o, c, g, kept, s, b):
         for h in range(2):
-            b = 2 * pair + h
+            row = pl.ds(b + h, 1)
             lanes = slice(VB * h, VB * (h + 1))
+            weights = ladder(coords_ref[o, 0, c, row, :], steps[0, g, row, :], steps[1, g, row, :], 4)
             for q in range(2):
                 real = imag = None
-                for i, (cos, sin) in enumerate(weights[h]):
+                for i, (cos, sin) in enumerate(weights):
                     at = 128 * q + 8 * i
                     sum_real, sum_imag = grid[at : at + 8, lanes], grid[at + 32 : at + 40, lanes]
                     gap_real, gap_imag = grid[at + 64 : at + 72, lanes], grid[at + 96 : at + 104, lanes]
@@ -195,13 +203,20 @@
                     step_imag = cos * sum_imag - sin * gap_real
                     real = step_real if real is None else real + step_real
                     imag = step_imag if imag is None else imag + step_imag
-                at = pl.ds(pl.multiple_of(8 * b, 8), 8)
-                sums[4 * g + 2 * q, at, :] = real
-                sums[4 * g + 2 * q + 1, at, :] = imag
-
-    @pl.loop(0, total[0])
-    def _(index):
-        unit(index)
+                at = pl.ds(pl.multiple_of(8 * (b + h), 8), 8)
+                sums[4 * kept + 2 * q, at, :] = real
+                sums[4 * kept + 2 * q + 1, at, :] = imag
+
+    @pl.loop(0, (total[0] + together - 1) // together)
+    def _(step):
+        at = [place(step * together + j) for j in range(together)]
+        phases = [phases_of(*a) for a in at]
+        grids = []
+        for a, p in zip(at, phases):
+            both = jnp.concatenate([own_ref[a[4]], other_ref[a[4]]], axis=0)
+            grids.append(jnp.dot(both, p, preferred_element_type=F32))
+        for a, grid in zip(at, grids):
+            finish(grid, *a)
 
     centre_x, centre_own, centre_other = centres[0], centres[1], centres[2]
 
@@ -228,20 +243,21 @@
                 out_ref[o, copy, c] = value
 
 
-def degrid(units, total, limits, centres, own, other, coords):
+def degrid(units, total, limits, centres, own, other, coords, together=TOGETHER):
     smem = pl.BlockSpec(memory_space=pltpu.SMEM)
     vmem = pl.BlockSpec(memory_space=pltpu.VMEM)
     return pl.pallas_call(
-        degrid_kernel,
+        functools.partial(degrid_kernel, together),
         out_shape=jax.ShapeDtypeStruct((16, 4, CAP, 2 * MAXB, VB), BF16),
         in_specs=[smem] * 4 + [vmem] * 3,
         out_specs=vmem,
         scratch_shapes=[
             pltpu.VMEM((4, 16 * CAP, MAXB, VB), F32),
-            pltpu.VMEM((16 * CAP * 4, 8 * MAXB, VB), F32),
+            pltpu.VMEM(((16 * CAP + 1) * 4, 8 * MAXB, VB), F32),
         ],
         compiler_params=pltpu.CompilerParams(vmem_limit_bytes=VMEM_LIMIT),
-        cost_estimate=pl.CostEstimate(flops=4_000_000_000, bytes_accessed=8_000_000, transcendentals=0),
+        cost_estimate=pl.CostEstimate(flops=12_000_000_000, bytes_accessed=8_000_000, transcendentals=0),
+        name="degrid",
     )(units, total, limits, centres, own, other, coords)
 
 
@@ -298,6 +314,7 @@
         in_specs=[smem] * 2 + [vmem] * 3,
         out_specs=vmem,
         compiler_params=pltpu.CompilerParams(vmem_limit_bytes=VMEM_LIMIT),
+        name="correct",
     )(limits, place, parts, stations, table)
 
 
@@ -336,7 +353,8 @@
     ).astype(F32)
 
     own = transform(facets[0])
-    other = lax.ppermute(own, "core", [(0, 1), (1, 0)])
+    sent, coords_all = lax.optimization_barrier((own, coords_all))
+    other = lax.ppermute(sent, "core", [(0, 1), (1, 0)])
     parts = degrid(units, total, limits, centres, own, other, coords_all)
     parts = parts.reshape(64, CAP, 2 * MAXB, VB)
     parts = lax.all_to_all(parts, ("z", "x", "pol"), split_axis=0, concat_axis=0, tiled=True)

time: 94.9 us -> 68.9 us (0.73)
  Pallas kernels: 44.5 us -> 21.7 us
  waiting for transfers between devices: 29.3 us -> 22.5 us
  starting transfers between devices: 14.8 us -> 19 us
    pallas_call x1, Pallas kernels: 23.3 us -> 10.7 us  [degrid(): pl.pallas_call(functools.partial(degrid_kernel, together), out_shape=jax....]
    all_to_all x1, waiting for transfers between devices: 10.9 us -> 0.01 us  [on_device(): lax.all_to_all(spread, ('z', 'x'), split_axis=0, concat_axis=0, tiled=True)]
    pallas_call x1, Pallas kernels: 19.8 us -> 9.54 us  [transform(): pl.pallas_call(transform_kernel, out_shape=jax.ShapeDtypeStruct((S, 2 * W...]
    all_to_all x1, starting transfers between devices: 6.74 us -> 10.9 us  [on_device(): lax.all_to_all(parts, ('z', 'x', 'pol'), split_axis=0, concat_axis=0, til...]
    ppermute x1, waiting for transfers between devices: 0.01 us -> 2.98 us  [on_device(): other = lax.ppermute(sent, 'core', [(0, 1), (1, 0)])]
    all_to_all x1, waiting for transfers between devices: 18.3 us -> 19.5 us  [on_device(): lax.all_to_all(parts, ('z', 'x', 'pol'), split_axis=0, concat_axis=0, til...]
    unnamed x17 -> x13, local copies, waits for them, and re-layouts: 3.13 us -> 2.36 us
  transfers between devices with their start and end apart: 3 -> 3, of which waited for: 2 -> 2; matrix products, arithmetic and copies ran while one was open for 2% -> 2% of each run, Pallas kernels for 0% -> 14%
where the time goes in v2:
time: 68.9 us; the launch traced here: 68.5 us
  waiting for transfers between devices  22.5 us (33%)
  Pallas kernels  21.7 us (31%)
  starting transfers between devices  19 us (28%)
  local copies, waits for them, and re-layouts  3.97 us (6%)
  other arithmetic  1.31 us (2%)
    all_to_all x1, waiting for transfers between devices, on_device(): lax.all_to_all(parts, ('z', 'x', 'pol'), split_axis=0, concat_axis=0, til...  19.5 us
    all_to_all x1, starting transfers between devices, on_device(): lax.all_to_all(parts, ('z', 'x', 'pol'), split_axis=0, concat_axis=0, til...  10.9 us
    pallas_call x1, Pallas kernels, degrid(): pl.pallas_call(functools.partial(degrid_kernel, together), out_shape=jax....  10.7 us
    pallas_call x1, Pallas kernels, transform(): pl.pallas_call(transform_kernel, out_shape=jax.ShapeDtypeStruct((S, 2 * W...  9.54 us
    all_to_all x1, starting transfers between devices, on_device(): lax.all_to_all(spread, ('z', 'x'), split_axis=0, concat_axis=0, tiled=True)  7.96 us
    ppermute x1, waiting for transfers between devices, on_device(): other = lax.ppermute(sent, 'core', [(0, 1), (1, 0)])  2.98 us
    unnamed x13, local copies, waits for them, and re-layouts  2.36 us
    broadcast_in_dim x1, local copies, waits for them, and re-layouts, on_device(): spread = jnp.broadcast_to(coords[None], (16,) + coords.shape)  1.6 us
  transfers between devices with their start and end apart: 3, of which 2 were waited for; matrix products, arithmetic and copies ran while one was open for 2% of the time, Pallas kernels for 14%

profile of v2, /device:TPU:0, one launch (start us, length us, event | category | flops | bytes accessed | tf_op | source)
XLA Modules:
  0.0 68.5 jit_solution(10386505270733836913)
XLA Ops:
  0.0 1.6 %broadcast_in_dim.51 = f32[16,2,4,8,128]{4,3,2,1,0:T(8,128)} broadcast(f32[2,4,8,128]{3,2,1,0:T(8,128)} %param.12), dimensions={1,2,3,4} | broadcast | bytes 557056 | tf_op jit(solution)/shard_map/broadcast_in_dim | solution.py:326
  1.6 8.0 %all-to-all-start = ((f32[16,2,4,8,128]{4,3,2,1,0:T(8,128)}), f32[16,2,4,8,128]{4,3,2,1,0:T(8,128)S(1)}, u32[]{:S(2)}, u32[]{:S(2)}) async-start(f32[16,2,4,8,128]{4,3,2,1,0:T(8,128)} %broadcast_in_dim.51), calls=%async_computation | async-start | bytes 1048576 | tf_op jit(solution)/shard_map/all_to_all | solution.py:327
  9.6 0.0 copy-start.1
  9.6 1.6 %copy-done.1 = bf16[1,2,4096,128]{3,2,1,0:T(8,128)(2,1)S(1)} copy-done((bf16[1,2,4096,128]{3,2,1,0:T(8,128)(2,1)S(1)}, bf16[1,2,4096,128]{3,2,1,0:T(8,128)(2,1)}, u32[]{:S(2)}) %copy-start.1) | copy-done | bytes 2097176
  11.2 0.8 %copy-done.2 = bf16[128,128]{1,0:T(8,128)(2,1)S(1)} copy-done((bf16[128,128]{1,0:T(8,128)(2,1)S(1)}, bf16[128,128]{1,0:T(8,128)(2,1)}, u32[]{:S(2)}) %copy-start.2) | copy-done | bytes 32792
  11.9 9.5 %transform.1.own_ref = bf16[64,128,128]{2,1,0:T(8,128)(2,1)S(1)} custom-call(bf16[2,64,64,128]{3,2,1,0:T(8,128)(2,1)S(1)} %bitcast.14, bf16[1024,1024]{1,0:T(8,128)(2,1)} %constant.97.clone.first_ref, bf16[64,128,128]{2,1,0:T(8,128)(2,1)} %constant.98.clone.second_ref, bf16[128,128]{1,0:T(8,128)(2,1)S(1)} %copy-done.2), custom_call_target="tpu_custom_call" | custom-call | flops 12000000000 | bytes 8000000 | tf_op jit(solution)/shard_map/transform/pallas_call | solution.py:140
  21.5 0.0 all-to-all-done.coords_ref
  21.5 0.1 collective-permute-start
  21.6 0.1 pad_maximum_fusion.centres
  21.7 0.0 copy-done.5
  21.7 0.2 select_reduce_fusion.3
  21.9 0.0 copy-done.4
  21.9 0.6 fusion.7
  22.5 0.1 select_reduce_fusion.1
  22.6 0.1 select_reduce_fusion.2.limits
  22.8 0.1 select_reduce_fusion.units
  22.9 3.0 %collective-permute-done.other_ref = bf16[64,128,128]{2,1,0:T(8,128)(2,1)} collective-permute-done((bf16[64,128,128]{2,1,0:T(8,128)(2,1)S(1)}, bf16[64,128,128]{2,1,0:T(8,128)(2,1)}, u32[]{:S(2)}, u32[]{:S(2)}) %collective-permute-start) | collective-permute-done | bytes 2097184 | tf_op jit(solution)/shard_map/ppermute | solution.py:357
  25.9 10.7 %degrid.1 = bf16[16,4,4,16,128]{4,3,2,1,0:T(8,128)(2,1)} custom-call(s32[256]{0:T(256)S(1)} %select_reduce_fusion.units, s32[1]{0:T(128)} %bitcast.2.total, s32[64]{0:T(128)S(1)} %select_reduce_fusion.2.limits, f32[3]{0:T(128)S(1)} %pad_maximum_fusion.centres, bf16[64,128,128]{2,1,0:T(8,128)(2,1)S(1)} %transform.1.own_ref, ...), custom_call_target="tpu_custom_call" | custom-call | flops 12000000000 | bytes 8000000 | tf_op jit(solution)/shard_map/degrid/pallas_call | solution.py:249
  36.6 10.9 %all-to-all-start.1 = ((bf16[64,4,16,128]{3,2,1,0:T(8,128)(2,1)}), bf16[64,4,16,128]{3,2,1,0:T(8,128)(2,1)S(1)}, u32[]{:S(2)}, u32[]{:S(2)}) async-start(bf16[64,4,16,128]{3,2,1,0:T(8,128)(2,1)} %bitcast.7), calls=%async_computation.1 | async-start | bytes 2097152 | tf_op jit(solution)/shard_map/all_to_all | solution.py:360
  47.5 0.0 copy-done.3
  47.5 0.1 pad_add_fusion.place
  47.6 19.5 %all-to-all-done.1 = bf16[64,4,16,128]{3,2,1,0:T(8,128)(2,1)S(1)} async-done(((bf16[64,4,16,128]{3,2,1,0:T(8,128)(2,1)}), bf16[64,4,16,128]{3,2,1,0:T(8,128)(2,1)S(1)}, u32[]{:S(2)}, u32[]{:S(2)}) %all-to-all-start.1) | async-done | bytes 1048608 | tf_op jit(solution)/shard_map/all_to_all | solution.py:360
  67.1 0.0 copy-done
  67.1 1.4 %correct.1 = f32[1,2,4,8,128]{4,3,2,1,0:T(8,128)} custom-call(s32[64]{0:T(128)S(1)} %select_reduce_fusion.2.limits, s32[2]{0:T(128)S(1)} %pad_add_fusion.place, bf16[16,4,4,16,128]{4,3,2,1,0:T(8,128)(2,1)S(1)} %bitcast.12, s32[4,2,8,128]{3,2,1,0:T(8,128)S(1)} %bitcast.13, f32[8,512]{1,0:T(8,128)S(1)} %copy-done), custom_call_target="tpu_custom_call" | custom-call | tf_op jit(solution)/shard_map/correct/pallas_call | solution.py:311
  (6 shorter events, 0.0 us)
Async XLA Ops:
  1.6 19.9 %all-to-all-start = ((f32[16,2,4,8,128]{4,3,2,1,0:T(8,128)}), f32[16,2,4,8,128]{4,3,2,1,0:T(8,128)S(1)}, u32[]{:S(2)}, u32[]{:S(2)}) async-start(f32[16,2,4,8,128]{4,3,2,1,0:T(8,128)} %broadcast_in_dim.51), calls=%async_computation | async-start | bytes 1048576 | tf_op jit(solution)/shard_map/all_to_all | solution.py:327
  9.6 1.6 %copy-start.1 = (bf16[1,2,4096,128]{3,2,1,0:T(8,128)(2,1)S(1)}, bf16[1,2,4096,128]{3,2,1,0:T(8,128)(2,1)}, u32[]{:S(2)}) copy-start(bf16[1,2,4096,128]{3,2,1,0:T(8,128)(2,1)} %param.9) | copy-start | bytes 6291460
  11.2 0.8 %copy-start.2 = (bf16[128,128]{1,0:T(8,128)(2,1)S(1)}, bf16[128,128]{1,0:T(8,128)(2,1)}, u32[]{:S(2)}) copy-start(bf16[128,128]{1,0:T(8,128)(2,1)} %constant.99.clone.mirror_ref) | copy-start | bytes 98308
  11.9 9.8 %copy-start.5 = (s32[64]{0:T(128)S(1)}, s32[64]{0:T(128)}, u32[]{:S(2)}) copy-start(s32[64]{0:T(128)} %param.10) | copy-start | bytes 772
  11.9 10.0 %copy-start.4 = (s32[64]{0:T(128)S(1)}, s32[64]{0:T(128)}, u32[]{:S(2)}) copy-start(s32[64]{0:T(128)} %param.11) | copy-start | bytes 772
  21.5 4.4 %collective-permute-start = (bf16[64,128,128]{2,1,0:T(8,128)(2,1)S(1)}, bf16[64,128,128]{2,1,0:T(8,128)(2,1)}, u32[]{:S(2)}, u32[]{:S(2)}) collective-permute-start(bf16[64,128,128]{2,1,0:T(8,128)(2,1)S(1)} %transform.1.own_ref), channel_id=1, source_target_pairs={{0,4},{4,0},{1,5},{5,1},{2,6},{6,2},{3,7},{7,3},{8,12},{12,8},{9,1... | collective-permute-start | bytes 6291464 | tf_op jit(solution)/shard_map/ppermute | solution.py:357
  36.6 10.9 %copy-start.3 = (s32[4,8,2,128]{3,2,1,0:T(2,128)S(1)}, s32[4,8,2,128]{3,2,1,0:T(2,128)}, u32[]{:S(2)}) copy-start(s32[4,8,2,128]{3,2,1,0:T(2,128)} %param.13) | copy-start | bytes 98308
  36.6 30.5 %copy-start = (f32[8,512]{1,0:T(8,128)S(1)}, f32[8,512]{1,0:T(8,128)}, u32[]{:S(2)}) copy-start(f32[8,512]{1,0:T(8,128)} %table_ref.1) | copy-start | bytes 49156
  36.6 30.5 %all-to-all-start.1 = ((bf16[64,4,16,128]{3,2,1,0:T(8,128)(2,1)}), bf16[64,4,16,128]{3,2,1,0:T(8,128)(2,1)S(1)}, u32[]{:S(2)}, u32[]{:S(2)}) async-start(bf16[64,4,16,128]{3,2,1,0:T(8,128)(2,1)} %bitcast.7), calls=%async_computation.1 | async-start | bytes 2097152 | tf_op jit(solution)/shard_map/all_to_all | solution.py:360

commit v3 on v2

--- a/solution.py
+++ b/solution.py
@@ -44,14 +44,6 @@
     return np.concatenate([upper, lower], axis=1).astype(BF16)
 
 
-def mirror_table():
-    table = np.zeros((2 * W, 2 * W), np.float32)
-    index = np.arange(W)
-    table[W - 1 - index, index] = 1.0
-    table[2 * W - 1 - index, W + index] = 1.0
-    return table.astype(BF16)
-
-
 SIN_TERMS = (3.14159264, -5.16771008, 2.55007752, -0.598291286, 0.0776576603)
 COS_TERMS = (0.999999953, -4.93479283, 4.05841135, -1.33187657, 0.219689611)
 
@@ -76,23 +68,40 @@
     return (cos * step_cos - sin * step_sin, sin * step_cos + cos * step_sin)
 
 
-def transform_kernel(facets_ref, first_ref, second_ref, mirror_ref, out_ref, mirrored, sections, mixed):
-    mirror = mirror_ref[...]
+def transform_kernel(
+    facets_hbm, first_hbm, second_hbm, out_ref, facets_ref, first_ref, second_ref, sections, mixed, sems
+):
     half = W // 2
-
-    @pl.loop(0, W // GROUP)
-    def _(h):
-        at = pl.ds(pl.multiple_of(h * GROUP, GROUP), GROUP)
-        mirrored[...] = jnp.dot(
-            facets_ref[0, :, at, :].reshape(W * GROUP, 2 * W), mirror, preferred_element_type=F32
+    first_copy = pltpu.make_async_copy(first_hbm, first_ref, sems.at[0])
+    second_copy = pltpu.make_async_copy(second_hbm, second_ref, sems.at[1])
+    strip_copies = [
+        pltpu.make_async_copy(facets_hbm.at[:, :, pl.ds(GROUP * h, GROUP), :], facets_ref.at[h], sems.at[2 + h])
+        for h in range(W // GROUP)
+    ]
+    strip_copies[0].start()
+    first_copy.start()
+    for copy in strip_copies[1:]:
+        copy.start()
+    second_copy.start()
+    row = lax.broadcasted_iota(jnp.int32, (2 * W, 2 * W), 0)
+    lane = lax.broadcasted_iota(jnp.int32, (2 * W, 2 * W), 1)
+    mirror = jnp.where(row == jnp.where(lane < W, W - 1, 3 * W - 1) - lane, 1.0, 0.0).astype(BF16)
+    for h in range(W // GROUP):
+        at = slice(GROUP * h, GROUP * h + GROUP)
+        strip_copies[h].wait()
+        mirrored = jnp.dot(
+            facets_ref[h, 0].reshape(W * GROUP, 2 * W), mirror, preferred_element_type=F32
         ).astype(BF16)
-        strips = jnp.concatenate([mirrored[...], facets_ref[1, :, at, :].reshape(W * GROUP, 2 * W)], axis=1)
+        strips = jnp.concatenate([mirrored, facets_ref[h, 1].reshape(W * GROUP, 2 * W)], axis=1)
+        if h == 0:
+            first_copy.wait()
         for piece in range(4):
             rows = slice(piece * 256, piece * 256 + 256)
             part = jnp.dot(first_ref[rows, :], strips, preferred_element_type=F32).astype(BF16)
             for f in range(2):
                 block = part[:, 2 * W * f : 2 * W * (f + 1)].reshape(16, GROUP, 2 * W)
                 sections[f, piece * 16 : piece * 16 + 16, at, :] = block
+    second_copy.wait()
 
     low_lanes = lax.broadcasted_iota(jnp.int32, (S, 2 * W), 1) < W
 
@@ -136,32 +145,43 @@
                 out_ref[at, rows, :] = jnp.concatenate(halves, axis=1).astype(BF16)
 
 
+def in_hbm(array):
+    return pltpu.with_memory_space_constraint(array, pltpu.HBM)
+
+
 def transform(strips):
     return pl.pallas_call(
         transform_kernel,
         out_shape=jax.ShapeDtypeStruct((S, 2 * W, 2 * W), BF16),
-        in_specs=[pl.BlockSpec(memory_space=pltpu.VMEM)] * 4,
+        in_specs=[pl.BlockSpec(memory_space=pltpu.HBM)] * 3,
         out_specs=pl.BlockSpec(memory_space=pltpu.VMEM),
         scratch_shapes=[
-            pltpu.VMEM((W * GROUP, 2 * W), BF16),
+            pltpu.VMEM((W // GROUP, 2, W, GROUP, 2 * W), BF16),
+            pltpu.VMEM((W * GROUP, W * GROUP), BF16),
+            pltpu.VMEM((W, 2 * W, 2 * W), BF16),
             pltpu.VMEM((2, W, W, 2 * W), BF16),
             pltpu.VMEM((4, W // 2, S, 2 * W), F32),
+            pltpu.SemaphoreType.DMA((2 + W // GROUP,)),
         ],
         compiler_params=pltpu.CompilerParams(vmem_limit_bytes=VMEM_LIMIT),
         cost_estimate=pl.CostEstimate(flops=12_000_000_000, bytes_accessed=8_000_000, transcendentals=0),
         name="transform",
-    )(strips.reshape(2, W, W, 2 * W), jnp.asarray(first_table()), jnp.asarray(second_table()), jnp.asarray(mirror_table()))
-
-
-def degrid_kernel(together, units, total, limits, centres, own_ref, other_ref, coords_ref, out_ref, steps, sums):
+    )(*(in_hbm(x) for x in (strips.reshape(2, W, W, 2 * W), jnp.asarray(first_table()), jnp.asarray(second_table()))))
+
+
+def degrid_kernel(together, units, total, limits, centres, own_ref, other_hbm, coords_ref, out_ref, steps, sums, other_ref, sem):
+    other_copy = pltpu.make_async_copy(other_hbm, other_ref, sem)
+    other_copy.start()
+
     @pl.loop(0, 16)
     def _(o):
         for c in range(CAP):
             for axis in range(2):
-                cos, sin = turns_to_phase(coords_ref[o, axis, c] * (8.0 / SG))
+                cos, sin = turns_to_phase(coords_ref[o, axis * CAP + c] * (8.0 / SG))
                 steps[2 * axis, o * CAP + c] = cos
                 steps[2 * axis + 1, o * CAP + c] = sin
 
+    other_copy.wait()
     cells = (lax.broadcasted_iota(jnp.int32, (8, VB), 0).astype(F32) + 0.5) * (1.0 / SG)
 
     def ladder(position, step_cos, step_sin, count):
@@ -184,7 +204,7 @@
         blocks = []
         for h in range(2):
             row = pl.ds(b + h, 1)
-            along = ladder(coords_ref[o, 1, c, row, :], steps[2, g, row, :], steps[3, g, row, :], 8)
+            along = ladder(coords_ref[o, CAP + c, row, :], steps[2, g, row, :], steps[3, g, row, :], 8)
             blocks.append(jnp.concatenate([t[0] for t in along] + [t[1] for t in along], axis=0).astype(BF16))
         return jnp.concatenate(blocks, axis=1)
 
@@ -192,7 +212,7 @@
         for h in range(2):
             row = pl.ds(b + h, 1)
             lanes = slice(VB * h, VB * (h + 1))
-            weights = ladder(coords_ref[o, 0, c, row, :], steps[0, g, row, :], steps[1, g, row, :], 4)
+            weights = ladder(coords_ref[o, c, row, :], steps[0, g, row, :], steps[1, g, row, :], 4)
             for q in range(2):
                 real = imag = None
                 for i, (cos, sin) in enumerate(weights):
@@ -226,7 +246,7 @@
 
         @pl.when(limits[g] > 0)
         def _():
-            x, y = coords_ref[o, 0, c], coords_ref[o, 1, c]
+            x, y = coords_ref[o, c], coords_ref[o, CAP + c]
             real = imag = jnp.zeros((MAXB, VB), F32)
             for q, centre_y in enumerate((centre_own, centre_other)):
                 total_real = sums[4 * g + 2 * q, pl.ds(0, MAXB, stride=8), :]
@@ -240,7 +260,7 @@
             scale = 1.0 / (math.sqrt(FH) * SG)
             value = (jnp.concatenate([real, imag], axis=0) * scale).astype(BF16)
             for copy in range(4):
-                out_ref[o, copy, c] = value
+                out_ref[o * 4 + copy, pl.ds(pl.multiple_of(2 * MAXB * c, 2 * MAXB), 2 * MAXB), :] = value
 
 
 def degrid(units, total, limits, centres, own, other, coords, together=TOGETHER):
@@ -248,12 +268,14 @@
     vmem = pl.BlockSpec(memory_space=pltpu.VMEM)
     return pl.pallas_call(
         functools.partial(degrid_kernel, together),
-        out_shape=jax.ShapeDtypeStruct((16, 4, CAP, 2 * MAXB, VB), BF16),
-        in_specs=[smem] * 4 + [vmem] * 3,
+        out_shape=jax.ShapeDtypeStruct((64, CAP * 2 * MAXB, VB), BF16),
+        in_specs=[smem] * 4 + [vmem, pl.BlockSpec(memory_space=pltpu.HBM), vmem],
         out_specs=vmem,
         scratch_shapes=[
             pltpu.VMEM((4, 16 * CAP, MAXB, VB), F32),
             pltpu.VMEM(((16 * CAP + 1) * 4, 8 * MAXB, VB), F32),
+            pltpu.VMEM((S, 2 * W, 2 * W), BF16),
+            pltpu.SemaphoreType.DMA,
         ],
         compiler_params=pltpu.CompilerParams(vmem_limit_bytes=VMEM_LIMIT),
         cost_estimate=pl.CostEstimate(flops=12_000_000_000, bytes_accessed=8_000_000, transcendentals=0),
@@ -290,9 +312,10 @@
         for inner_row in range(2):
             part_real = part_imag = jnp.zeros((MAXB, VB), F32)
             for inner_col in range(2):
-                comp = parts_ref[0, 2 * inner_row + inner_col, c].astype(F32)
+                rows = slice(2 * MAXB * c, 2 * MAXB * (c + 1))
+                comp = parts_ref[2 * inner_row + inner_col, rows, :].astype(F32)
                 for o in range(1, 16):
-                    comp = comp + parts_ref[o, 2 * inner_row + inner_col, c].astype(F32)
+                    comp = comp + parts_ref[4 * o + 2 * inner_row + inner_col, rows, :].astype(F32)
                 real, imag = comp[:MAXB], comp[MAXB:]
                 right_real, right_imag = rights[inner_col]
                 part_real = part_real + (real * right_real + imag * right_imag)
@@ -323,8 +346,10 @@
     core = lax.axis_index("core")
     pol = lax.axis_index("pol")
 
-    spread = jnp.broadcast_to(coords[None], (16,) + coords.shape)
+    spread = jnp.broadcast_to(coords.reshape(1, 2 * CAP * MAXB, VB), (16, 2 * CAP * MAXB, VB))
     coords_all = lax.all_to_all(spread, ("z", "x"), split_axis=0, concat_axis=0, tiled=True)
+
+    coords_all = coords_all.reshape(16, 2 * CAP, MAXB, VB)
 
     index = jnp.arange(S, dtype=jnp.int32)
     before = index[None, :] < index[:, None]
@@ -356,9 +381,7 @@
     sent, coords_all = lax.optimization_barrier((own, coords_all))
     other = lax.ppermute(sent, "core", [(0, 1), (1, 0)])
     parts = degrid(units, total, limits, centres, own, other, coords_all)
-    parts = parts.reshape(64, CAP, 2 * MAXB, VB)
     parts = lax.all_to_all(parts, ("z", "x", "pol"), split_axis=0, concat_axis=0, tiled=True)
-    parts = parts.reshape(16, 4, CAP, 2 * MAXB, VB)
     stations = jnp.moveaxis(station_ids, 2, 1)
     place = jnp.stack([chip, pol]).astype(jnp.int32)
     return correct(limits, place, parts, stations, jones_table)

time: 68.9 us -> 65.3 us (0.948)
  waiting for transfers between devices: 22.5 us -> 25.4 us
  starting transfers between devices: 19 us -> 16.2 us
  local copies, waits for them, and re-layouts: 3.97 us -> 1.63 us
  Pallas kernels: 21.7 us -> 20.5 us
    all_to_all x1, starting transfers between devices: 10.9 us -> 8.26 us  [on_device(): lax.all_to_all(parts, ('z', 'x', 'pol'), split_axis=0, concat_axis=0, til...]
    all_to_all x1, waiting for transfers between devices: 0.01 us -> 2.58 us  [on_device(): lax.all_to_all(spread, ('z', 'x'), split_axis=0, concat_axis=0, tiled=True)]
    unnamed x13 -> x9, local copies, waits for them, and re-layouts: 2.36 us -> 0.03 us
  transfers between devices with their start and end apart: 3 -> 3, of which waited for: 2 -> 3; matrix products, arithmetic and copies ran while one was open for 2% -> 2% of each run, Pallas kernels for 14% -> 14%
where the time goes in v3:
time: 65.3 us; the launch traced here: 65 us
  waiting for transfers between devices  25.4 us (39%)
  Pallas kernels  20.5 us (31%)
  starting transfers between devices  16.2 us (25%)
  local copies, waits for them, and re-layouts  1.63 us (2%)
  other arithmetic  1.19 us (2%)
    all_to_all x1, waiting for transfers between devices, on_device(): lax.all_to_all(parts, ('z', 'x', 'pol'), split_axis=0, concat_axis=0, til...  19.7 us
    pallas_call x1, Pallas kernels, degrid(): pl.pallas_call(functools.partial(degrid_kernel, together), out_shape=jax....  10.2 us
    pallas_call x1, Pallas kernels, transform(): pl.pallas_call(transform_kernel, out_shape=jax.ShapeDtypeStruct((S, 2 * W...  8.92 us
    all_to_all x1, starting transfers between devices, on_device(): lax.all_to_all(parts, ('z', 'x', 'pol'), split_axis=0, concat_axis=0, til...  8.26 us
    all_to_all x1, starting transfers between devices, on_device(): lax.all_to_all(spread, ('z', 'x'), split_axis=0, concat_axis=0, tiled=True)  7.96 us
    ppermute x1, waiting for transfers between devices, on_device(): other = lax.ppermute(sent, 'core', [(0, 1), (1, 0)])  3.16 us
    all_to_all x1, waiting for transfers between devices, on_device(): lax.all_to_all(spread, ('z', 'x'), split_axis=0, concat_axis=0, tiled=True)  2.58 us
    broadcast_in_dim x1, local copies, waits for them, and re-layouts, on_device(): jnp.broadcast_to(coords.reshape(1, 2 * CAP * MAXB, VB), (16, 2 * CAP * MA...  1.6 us
  transfers between devices with their start and end apart: 3, of which 3 were waited for; matrix products, arithmetic and copies ran while one was open for 2% of the time, Pallas kernels for 14%

profile of v3, /device:TPU:0, one launch (start us, length us, event | category | flops | bytes accessed | tf_op | source)
XLA Modules:
  0.0 65.0 jit_solution(9071836883891556095)
XLA Ops:
  0.0 1.6 %broadcast_in_dim.53 = f32[16,64,128]{2,1,0:T(8,128)} broadcast(f32[64,128]{1,0:T(8,128)} %bitcast.14), dimensions={1,2} | broadcast | bytes 557056 | tf_op jit(solution)/shard_map/broadcast_in_dim | solution.py:349
  1.6 8.0 %all-to-all-start = ((f32[16,64,128]{2,1,0:T(8,128)}), f32[16,64,128]{2,1,0:T(8,128)S(1)}, u32[]{:S(2)}, u32[]{:S(2)}) async-start(f32[16,64,128]{2,1,0:T(8,128)} %broadcast_in_dim.53), calls=%async_computation | async-start | bytes 1048576 | tf_op jit(solution)/shard_map/all_to_all | solution.py:350
  9.6 0.0 copy-start.3
  9.6 0.0 copy-start.2
  9.6 8.9 %transform.1.own_ref = bf16[64,128,128]{2,1,0:T(8,128)(2,1)S(1)} custom-call(bf16[2,64,64,128]{3,2,1,0:T(8,128)(2,1)} %bitcast.15, bf16[1024,1024]{1,0:T(8,128)(2,1)} %constant.95.clone.first_hbm, bf16[64,128,128]{2,1,0:T(8,128)(2,1)} %constant.96.clone.second_hbm), custom_call_target="tpu_custom_call" | custom-call | flops 12000000000 | bytes 8000000 | tf_op jit(solution)/shard_map/transform/pallas_call | solution.py:153
  18.5 2.6 %all-to-all-done = f32[16,64,128]{2,1,0:T(8,128)S(1)} async-done(((f32[16,64,128]{2,1,0:T(8,128)}), f32[16,64,128]{2,1,0:T(8,128)S(1)}, u32[]{:S(2)}, u32[]{:S(2)}) %all-to-all-start) | async-done | bytes 524320 | tf_op jit(solution)/shard_map/all_to_all | solution.py:350
  21.1 0.0 collective-permute-start
  21.1 0.1 pad_maximum_fusion.centres
  21.2 0.0 copy-done.3
  21.2 0.2 select_reduce_fusion.3
  21.4 0.0 copy-done.2
  21.4 0.6 fusion.7
  22.0 0.1 select_reduce_fusion.1
  22.1 0.1 select_reduce_fusion.units
  22.2 3.2 %collective-permute-done.other_hbm = bf16[64,128,128]{2,1,0:T(8,128)(2,1)} collective-permute-done((bf16[64,128,128]{2,1,0:T(8,128)(2,1)S(1)}, bf16[64,128,128]{2,1,0:T(8,128)(2,1)}, u32[]{:S(2)}, u32[]{:S(2)}) %collective-permute-start) | collective-permute-done | bytes 2097184 | tf_op jit(solution)/shard_map/ppermute | solution.py:382
  25.4 10.2 %degrid.1 = bf16[64,64,128]{2,1,0:T(8,128)(2,1)} custom-call(s32[256]{0:T(256)S(1)} %select_reduce_fusion.units, s32[1]{0:T(128)} %bitcast.2.total, s32[64]{0:T(128)S(1)} %get-tuple-element.17.limits, f32[3]{0:T(128)S(1)} %pad_maximum_fusion.centres, bf16[64,128,128]{2,1,0:T(8,128)(2,1)S(1)} %transform.1.own_ref, ...), custom_call_target="tpu_custom_call" | custom-call | flops 12000000000 | bytes 8000000 | tf_op jit(solution)/shard_map/degrid/pallas_call | solution.py:269
  35.6 0.0 copy-start.1
  35.6 0.0 copy-start
  35.6 8.3 %all-to-all-start.1 = ((bf16[64,64,128]{2,1,0:T(8,128)(2,1)}), bf16[64,64,128]{2,1,0:T(8,128)(2,1)S(1)}, u32[]{:S(2)}, u32[]{:S(2)}) async-start(bf16[64,64,128]{2,1,0:T(8,128)(2,1)} %degrid.1), calls=%async_computation.1 | async-start | bytes 2097152 | tf_op jit(solution)/shard_map/all_to_all | solution.py:384
  43.9 0.0 copy-done.1
  43.9 0.1 pad_add_fusion.place
  44.0 19.7 %all-to-all-done.1.parts_ref = bf16[64,64,128]{2,1,0:T(8,128)(2,1)S(1)} async-done(((bf16[64,64,128]{2,1,0:T(8,128)(2,1)}), bf16[64,64,128]{2,1,0:T(8,128)(2,1)S(1)}, u32[]{:S(2)}, u32[]{:S(2)}) %all-to-all-start.1) | async-done | bytes 1048608 | tf_op jit(solution)/shard_map/all_to_all | solution.py:384
  63.6 0.0 copy-done
  63.6 1.4 %correct.1 = f32[1,2,4,8,128]{4,3,2,1,0:T(8,128)} custom-call(s32[64]{0:T(128)S(1)} %get-tuple-element.17.limits, s32[2]{0:T(128)S(1)} %pad_add_fusion.place, bf16[64,64,128]{2,1,0:T(8,128)(2,1)S(1)} %all-to-all-done.1.parts_ref, s32[4,2,8,128]{3,2,1,0:T(8,128)S(1)} %bitcast.13, f32[8,512]{1,0:T(8,128)S(1)} %copy-done), custom_call_target="tpu_custom_call" | custom-call | tf_op jit(solution)/shard_map/correct/pallas_call | solution.py:334
  (1 shorter events, 0.0 us)
Async XLA Ops:
  1.6 19.5 %all-to-all-start = ((f32[16,64,128]{2,1,0:T(8,128)}), f32[16,64,128]{2,1,0:T(8,128)S(1)}, u32[]{:S(2)}, u32[]{:S(2)}) async-start(f32[16,64,128]{2,1,0:T(8,128)} %broadcast_in_dim.53), calls=%async_computation | async-start | bytes 1048576 | tf_op jit(solution)/shard_map/all_to_all | solution.py:350
  9.6 11.6 %copy-start.3 = (s32[64]{0:T(128)S(1)}, s32[64]{0:T(128)}, u32[]{:S(2)}) copy-start(s32[64]{0:T(128)} %param.9) | copy-start | bytes 772
  9.6 11.8 %copy-start.2 = (s32[64]{0:T(128)S(1)}, s32[64]{0:T(128)}, u32[]{:S(2)}) copy-start(s32[64]{0:T(128)} %param.10) | copy-start | bytes 772
  21.1 4.3 %collective-permute-start = (bf16[64,128,128]{2,1,0:T(8,128)(2,1)S(1)}, bf16[64,128,128]{2,1,0:T(8,128)(2,1)}, u32[]{:S(2)}, u32[]{:S(2)}) collective-permute-start(bf16[64,128,128]{2,1,0:T(8,128)(2,1)S(1)} %transform.1.own_ref), channel_id=1, source_target_pairs={{0,4},{4,0},{1,5},{5,1},{2,6},{6,2},{3,7},{7,3},{8,12},{12,8},{9,1... | collective-permute-start | bytes 6291464 | tf_op jit(solution)/shard_map/ppermute | solution.py:382
  35.6 8.3 %copy-start.1 = (s32[4,8,2,128]{3,2,1,0:T(2,128)S(1)}, s32[4,8,2,128]{3,2,1,0:T(2,128)}, u32[]{:S(2)}) copy-start(s32[4,8,2,128]{3,2,1,0:T(2,128)} %param.12) | copy-start | bytes 98308
  35.6 28.0 %copy-start = (f32[8,512]{1,0:T(8,128)S(1)}, f32[8,512]{1,0:T(8,128)}, u32[]{:S(2)}) copy-start(f32[8,512]{1,0:T(8,128)} %table_ref.1) | copy-start | bytes 49156
  35.6 28.0 %all-to-all-start.1 = ((bf16[64,64,128]{2,1,0:T(8,128)(2,1)}), bf16[64,64,128]{2,1,0:T(8,128)(2,1)S(1)}, u32[]{:S(2)}, u32[]{:S(2)}) async-start(bf16[64,64,128]{2,1,0:T(8,128)(2,1)} %degrid.1), calls=%async_computation.1 | async-start | bytes 2097152 | tf_op jit(solution)/shard_map/all_to_all | solution.py:384

commit v4 on v3

--- a/solution.py
+++ b/solution.py
@@ -18,6 +18,7 @@
 SG = 512
 CAP = 4
 UNITS = 256
+TOTAL_AT = UNITS + 64
 GROUP = 16
 TOGETHER = 8
 VMEM_LIMIT = 48 * 1024 * 1024
@@ -145,6 +146,25 @@
                 out_ref[at, rows, :] = jnp.concatenate(halves, axis=1).astype(BF16)
 
 
+def spread_kernel(coords_ref, out_hbm, sems):
+    copies = [pltpu.make_async_copy(coords_ref, out_hbm.at[o], sems.at[o]) for o in range(16)]
+    for copy in copies:
+        copy.start()
+    for copy in copies:
+        copy.wait()
+
+
+def spread(coords):
+    return pl.pallas_call(
+        spread_kernel,
+        out_shape=jax.ShapeDtypeStruct((16,) + coords.shape, F32),
+        in_specs=[pl.BlockSpec(memory_space=pltpu.VMEM)],
+        out_specs=pl.BlockSpec(memory_space=pltpu.HBM),
+        scratch_shapes=[pltpu.SemaphoreType.DMA((16,))],
+        name="spread",
+    )(coords)
+
+
 def in_hbm(array):
     return pltpu.with_memory_space_constraint(array, pltpu.HBM)
 
@@ -169,17 +189,17 @@
     )(*(in_hbm(x) for x in (strips.reshape(2, W, W, 2 * W), jnp.asarray(first_table()), jnp.asarray(second_table()))))
 
 
-def degrid_kernel(together, units, total, limits, centres, own_ref, other_hbm, coords_ref, out_ref, steps, sums, other_ref, sem):
+def degrid_kernel(together, plan, own_ref, other_hbm, coords_ref, out_ref, steps, sums, other_ref, sem):
     other_copy = pltpu.make_async_copy(other_hbm, other_ref, sem)
     other_copy.start()
 
     @pl.loop(0, 16)
     def _(o):
-        for c in range(CAP):
-            for axis in range(2):
-                cos, sin = turns_to_phase(coords_ref[o, axis * CAP + c] * (8.0 / SG))
-                steps[2 * axis, o * CAP + c] = cos
-                steps[2 * axis + 1, o * CAP + c] = sin
+        cos, sin = turns_to_phase(coords_ref[o] * (8.0 / SG))
+        slots = pl.ds(o * CAP, CAP)
+        for axis in range(2):
+            steps[2 * axis, slots] = cos[CAP * axis : CAP * axis + CAP]
+            steps[2 * axis + 1, slots] = sin[CAP * axis : CAP * axis + CAP]
 
     other_copy.wait()
     cells = (lax.broadcasted_iota(jnp.int32, (8, VB), 0).astype(F32) + 0.5) * (1.0 / SG)
@@ -195,9 +215,9 @@
         return both
 
     def place(index):
-        word = units[index]
+        word = plan[index]
         g = word // (4 * S)
-        kept = jnp.where(index < total[0], g, 16 * CAP)
+        kept = jnp.where(index < plan[TOTAL_AT], g, 16 * CAP)
         return (g // CAP, g % CAP, g, kept, (word // 4) % S, 2 * (word % 4))
 
     def phases_of(o, c, g, kept, s, b):
@@ -227,7 +247,7 @@
                 sums[4 * kept + 2 * q, at, :] = real
                 sums[4 * kept + 2 * q + 1, at, :] = imag
 
-    @pl.loop(0, (total[0] + together - 1) // together)
+    @pl.loop(0, (plan[TOTAL_AT] + together - 1) // together)
     def _(step):
         at = [place(step * together + j) for j in range(together)]
         phases = [phases_of(*a) for a in at]
@@ -238,13 +258,16 @@
         for a, grid in zip(at, grids):
             finish(grid, *a)
 
-    centre_x, centre_own, centre_other = centres[0], centres[1], centres[2]
+    first_facet, other_facet = plan[TOTAL_AT + 1], plan[TOTAL_AT + 2]
+    centre_x = (W * (first_facet // R)).astype(F32) + (W // 2 - 0.5 - SG // 2)
+    centre_own = (W * (first_facet % R)).astype(F32) + (W - 0.5 - SG // 2)
+    centre_other = (W * (other_facet % R)).astype(F32) + (W - 0.5 - SG // 2)
 
     @pl.loop(0, 16 * CAP)
     def _(g):
         o, c = g // CAP, g % CAP
 
-        @pl.when(limits[g] > 0)
+        @pl.when(plan[UNITS + g] > 0)
         def _():
             x, y = coords_ref[o, c], coords_ref[o, CAP + c]
             real = imag = jnp.zeros((MAXB, VB), F32)
@@ -259,17 +282,16 @@
                 imag = imag + (cos * total_imag - sin * total_real)
             scale = 1.0 / (math.sqrt(FH) * SG)
             value = (jnp.concatenate([real, imag], axis=0) * scale).astype(BF16)
-            for copy in range(4):
-                out_ref[o * 4 + copy, pl.ds(pl.multiple_of(2 * MAXB * c, 2 * MAXB), 2 * MAXB), :] = value
-
-
-def degrid(units, total, limits, centres, own, other, coords, together=TOGETHER):
+            out_ref[o, pl.ds(pl.multiple_of(2 * MAXB * c, 2 * MAXB), 2 * MAXB), :] = value
+
+
+def degrid(plan, own, other, coords, together=TOGETHER):
     smem = pl.BlockSpec(memory_space=pltpu.SMEM)
     vmem = pl.BlockSpec(memory_space=pltpu.VMEM)
     return pl.pallas_call(
         functools.partial(degrid_kernel, together),
-        out_shape=jax.ShapeDtypeStruct((64, CAP * 2 * MAXB, VB), BF16),
-        in_specs=[smem] * 4 + [vmem, pl.BlockSpec(memory_space=pltpu.HBM), vmem],
+        out_shape=jax.ShapeDtypeStruct((16, CAP * 2 * MAXB, VB), BF16),
+        in_specs=[smem, vmem, pl.BlockSpec(memory_space=pltpu.HBM), vmem],
         out_specs=vmem,
         scratch_shapes=[
             pltpu.VMEM((4, 16 * CAP, MAXB, VB), F32),
@@ -280,13 +302,12 @@
         compiler_params=pltpu.CompilerParams(vmem_limit_bytes=VMEM_LIMIT),
         cost_estimate=pl.CostEstimate(flops=12_000_000_000, bytes_accessed=8_000_000, transcendentals=0),
         name="degrid",
-    )(units, total, limits, centres, own, other, coords)
-
-
-def correct_kernel(limits, place, parts_ref, stations_ref, table_ref, out_ref):
-    me, pol = place[0], place[1]
+    )(plan, own, other, coords)
+
+
+def jones_kernel(place, stations_ref, table_ref, out_ref):
+    pol = place[0]
     row_side, col_side = pol // 2, pol % 2
-    block = lax.broadcasted_iota(jnp.int32, (MAXB, VB), 0)
 
     def side(which):
         return [
@@ -303,42 +324,57 @@
         return value
 
     left_table, right_table = side(row_side), side(col_side)
-
     for c in range(CAP):
         left, right = stations_ref[c, 0], stations_ref[c, 1]
         lefts = [[entry(left_table, 2 * k + ri, left) for ri in range(2)] for k in range(2)]
         rights = [[entry(right_table, 2 * k + ri, right) for ri in range(2)] for k in range(2)]
+        for turn in range(4):
+            comp = (pol + 4 - turn) % 4
+            left_real, left_imag = (jnp.where(comp // 2 == 1, lefts[1][ri], lefts[0][ri]) for ri in range(2))
+            right_real, right_imag = (jnp.where(comp % 2 == 1, rights[1][ri], rights[0][ri]) for ri in range(2))
+            out_ref[turn, c, 0] = left_real * right_real + left_imag * right_imag
+            out_ref[turn, c, 1] = left_imag * right_real - left_real * right_imag
+
+
+def jones(place, stations, table):
+    smem = pl.BlockSpec(memory_space=pltpu.SMEM)
+    vmem = pl.BlockSpec(memory_space=pltpu.VMEM)
+    return pl.pallas_call(
+        jones_kernel,
+        out_shape=jax.ShapeDtypeStruct((4, CAP, 2, MAXB, VB), F32),
+        in_specs=[smem, vmem, vmem],
+        out_specs=vmem,
+        compiler_params=pltpu.CompilerParams(vmem_limit_bytes=VMEM_LIMIT),
+        name="jones",
+    )(place, stations, table)
+
+
+def correct_kernel(limits, jones_ref, own_ref, one_ref, two_ref, three_ref, out_ref):
+    block = lax.broadcasted_iota(jnp.int32, (MAXB, VB), 0)
+    for c in range(CAP):
         total_real = total_imag = jnp.zeros((MAXB, VB), F32)
-        for inner_row in range(2):
-            part_real = part_imag = jnp.zeros((MAXB, VB), F32)
-            for inner_col in range(2):
-                rows = slice(2 * MAXB * c, 2 * MAXB * (c + 1))
-                comp = parts_ref[2 * inner_row + inner_col, rows, :].astype(F32)
-                for o in range(1, 16):
-                    comp = comp + parts_ref[4 * o + 2 * inner_row + inner_col, rows, :].astype(F32)
-                real, imag = comp[:MAXB], comp[MAXB:]
-                right_real, right_imag = rights[inner_col]
-                part_real = part_real + (real * right_real + imag * right_imag)
-                part_imag = part_imag + (imag * right_real - real * right_imag)
-            left_real, left_imag = lefts[inner_row]
-            total_real = total_real + (left_real * part_real - left_imag * part_imag)
-            total_imag = total_imag + (left_real * part_imag + left_imag * part_real)
-        keep = block < limits[me * CAP + c]
+        for turn, ref in enumerate((own_ref, one_ref, two_ref, three_ref)):
+            at = 2 * MAXB * c
+            real, imag = ref[at : at + MAXB, :], ref[at + MAXB : at + 2 * MAXB, :]
+            step_real, step_imag = jones_ref[turn, c, 0], jones_ref[turn, c, 1]
+            total_real = total_real + (step_real * real - step_imag * imag)
+            total_imag = total_imag + (step_real * imag + step_imag * real)
+        keep = block < limits[c]
         out_ref[0, 0, c] = jnp.where(keep, total_real, 0.0)
         out_ref[0, 1, c] = jnp.where(keep, total_imag, 0.0)
 
 
-def correct(limits, place, parts, stations, table):
+def correct(limits, factors, parts):
     smem = pl.BlockSpec(memory_space=pltpu.SMEM)
     vmem = pl.BlockSpec(memory_space=pltpu.VMEM)
     return pl.pallas_call(
         correct_kernel,
         out_shape=jax.ShapeDtypeStruct((1, 2, CAP, MAXB, VB), F32),
-        in_specs=[smem] * 2 + [vmem] * 3,
+        in_specs=[smem] + [vmem] * 5,
         out_specs=vmem,
         compiler_params=pltpu.CompilerParams(vmem_limit_bytes=VMEM_LIMIT),
         name="correct",
-    )(limits, place, parts, stations, table)
+    )(limits, factors, *parts)
 
 
 def on_device(facets, owners, counts, coords, station_ids, jones_table):
@@ -346,8 +382,7 @@
     core = lax.axis_index("core")
     pol = lax.axis_index("pol")
 
-    spread = jnp.broadcast_to(coords.reshape(1, 2 * CAP * MAXB, VB), (16, 2 * CAP * MAXB, VB))
-    coords_all = lax.all_to_all(spread, ("z", "x"), split_axis=0, concat_axis=0, tiled=True)
+    coords_all = lax.all_to_all(spread(coords.reshape(2 * CAP * MAXB, VB)), ("z", "x"), split_axis=0, concat_axis=0, tiled=True)
 
     coords_all = coords_all.reshape(16, 2 * CAP, MAXB, VB)
 
@@ -362,29 +397,24 @@
     offset = unit_index - first_unit[None, :]
     words = (slot * S + index)[None, :] * 4 + offset
     units = jnp.sum(jnp.where((offset >= 0) & (offset < pairs[None, :]), words, 0), axis=1)
-    total = jnp.sum(pairs).reshape(1)
     slots = jnp.arange(16 * CAP, dtype=jnp.int32)[:, None]
     limits = jnp.sum(jnp.where((slots == slot[None, :]) & mine[None, :], counts[None, :], 0), axis=1)
-
-    first_facet = 2 * (chip * 2 + core)
-    other_facet = 2 * (chip * 2 + 1 - core)
-    half = SG // 2
-    centres = jnp.stack(
-        [
-            W * (first_facet // R) + (W // 2 - 0.5 - half),
-            W * (first_facet % R) + (W - 0.5 - half),
-            W * (other_facet % R) + (W - 0.5 - half),
-        ]
-    ).astype(F32)
+    facet = 2 * (chip * 2 + core)
+    extra = jnp.stack([jnp.sum(pairs), facet, facet + 2 - 4 * core])
+    plan = jnp.concatenate([units, limits, extra, jnp.zeros((61,), jnp.int32)])
+    own_limits = jnp.sum(
+        jnp.where((slot[None, :] == chip * CAP + jnp.arange(CAP)[:, None]) & mine[None, :], counts[None, :], 0), axis=1
+    )
 
     own = transform(facets[0])
     sent, coords_all = lax.optimization_barrier((own, coords_all))
     other = lax.ppermute(sent, "core", [(0, 1), (1, 0)])
-    parts = degrid(units, total, limits, centres, own, other, coords_all)
-    parts = lax.all_to_all(parts, ("z", "x", "pol"), split_axis=0, concat_axis=0, tiled=True)
-    stations = jnp.moveaxis(station_ids, 2, 1)
-    place = jnp.stack([chip, pol]).astype(jnp.int32)
-    return correct(limits, place, parts, stations, jones_table)
+    parts = degrid(plan, own, other, coords_all)
+    parts = lax.all_to_all(parts, ("z", "x"), split_axis=0, concat_axis=0, tiled=True)
+    visible = jnp.sum(parts.astype(F32), axis=0)
+    factors = jones(pol.reshape(1).astype(jnp.int32), jnp.moveaxis(station_ids, 2, 1), jones_table)
+    turns = [lax.ppermute(visible, "pol", [(i, (i + k) % 4) for i in range(4)]) for k in (1, 2, 3)]
+    return correct(own_limits, factors, [visible] + turns)
 
 
 def solution(mesh):

time: 65.3 us -> 59.6 us (0.913)
  waiting for transfers between devices: 25.4 us -> 17 us
  starting transfers between devices: 16.2 us -> 18.6 us
  Pallas kernels: 20.5 us -> 21.4 us
  local copies, waits for them, and re-layouts: 1.63 us -> 0.75 us
    all_to_all x2, waiting for transfers between devices: 22.2 us -> 12.6 us  [the longest x1 9.96 us: on_device(): lax.all_to_all(parts, ('z', 'x'), split_axis=0, concat_axis=0, tiled=True)]
    ppermute x0 -> x3, starting transfers between devices: none -> 5.91 us  [on_device(): lax.ppermute(visible, 'pol', [(i, (i + k) % 4) for i in range(4)])]
    all_to_all x2, starting transfers between devices: 16.2 us -> 12.7 us  [the longest x1 7.97 us: on_device(): lax.all_to_all(spread(coords.reshape(2 * CAP * MAXB, VB)), ('z', 'x'), sp...]
    ppermute x0 -> x3, waiting for transfers between devices: none -> 2.1 us  [on_device(): lax.ppermute(visible, 'pol', [(i, (i + k) % 4) for i in range(4)])]
    pallas_call x0 -> x2, Pallas kernels: none -> 1.93 us  [the longest x1 1.69 us: spread(): pl.pallas_call(spread_kernel, out_shape=jax.ShapeDtypeStruct((16,) + coor...]
    broadcast_in_dim x1, local copies, waits for them, and re-layouts: 1.6 us -> 0.01 us  [on_device(): plan = jnp.concatenate([units, limits, extra, jnp.zeros((61,), jnp.int32)])]
    pallas_call x1, Pallas kernels: 10.2 us -> 9.37 us  [degrid(): pl.pallas_call(functools.partial(degrid_kernel, together), out_shape=jax....]
    ppermute x1, waiting for transfers between devices: 3.16 us -> 2.37 us  [on_device(): other = lax.ppermute(sent, 'core', [(0, 1), (1, 0)])]
  transfers between devices with their start and end apart: 3 -> 6, of which waited for: 3 -> 5; matrix products, arithmetic and copies ran while one was open for 2% -> 3% of each run, Pallas kernels for 14% -> 15%
where the time goes in v4:
time: 59.6 us; the launch traced here: 59.3 us
  Pallas kernels  21.4 us (36%)
  starting transfers between devices  18.6 us (31%)
  waiting for transfers between devices  17 us (29%)
  other arithmetic  1.38 us (2%)
  local copies, waits for them, and re-layouts  0.75 us (1%)
    all_to_all x1, waiting for transfers between devices, on_device(): lax.all_to_all(parts, ('z', 'x'), split_axis=0, concat_axis=0, tiled=True)  9.96 us
    pallas_call x1, Pallas kernels, degrid(): pl.pallas_call(functools.partial(degrid_kernel, together), out_shape=jax....  9.37 us
    pallas_call x1, Pallas kernels, transform(): pl.pallas_call(transform_kernel, out_shape=jax.ShapeDtypeStruct((S, 2 * W...  8.91 us
    all_to_all x1, starting transfers between devices, on_device(): lax.all_to_all(spread(coords.reshape(2 * CAP * MAXB, VB)), ('z', 'x'), sp...  7.97 us
    ppermute x3, starting transfers between devices, on_device(): lax.ppermute(visible, 'pol', [(i, (i + k) % 4) for i in range(4)])  5.91 us
    all_to_all x1, starting transfers between devices, on_device(): lax.all_to_all(parts, ('z', 'x'), split_axis=0, concat_axis=0, tiled=True)  4.72 us
    all_to_all x1, waiting for transfers between devices, on_device(): lax.all_to_all(spread(coords.reshape(2 * CAP * MAXB, VB)), ('z', 'x'), sp...  2.59 us
    ppermute x1, waiting for transfers between devices, on_device(): other = lax.ppermute(sent, 'core', [(0, 1), (1, 0)])  2.37 us
  transfers between devices with their start and end apart: 6, of which 5 were waited for; matrix products, arithmetic and copies ran while one was open for 3% of the time, Pallas kernels for 15%

profile of v4, /device:TPU:0, one launch (start us, length us, event | category | flops | bytes accessed | tf_op | source)
XLA Modules:
  0.0 59.3 jit_solution(6203912908142324921)
XLA Ops:
  0.0 1.7 %spread.1 = f32[16,64,128]{2,1,0:T(8,128)} custom-call(f32[64,128]{1,0:T(8,128)} %bitcast.12), custom_call_target="tpu_custom_call" | custom-call | tf_op jit(solution)/shard_map/spread/pallas_call | solution.py:158
  1.7 8.0 %all-to-all-start = ((f32[16,64,128]{2,1,0:T(8,128)}), f32[16,64,128]{2,1,0:T(8,128)S(1)}, u32[]{:S(2)}, u32[]{:S(2)}) async-start(f32[16,64,128]{2,1,0:T(8,128)} %spread.1), calls=%async_computation | async-start | bytes 1048576 | tf_op jit(solution)/shard_map/all_to_all | solution.py:385
  9.7 0.0 copy-start.3
  9.7 0.0 copy-start.2
  9.7 8.9 %transform.1.own_ref = bf16[64,128,128]{2,1,0:T(8,128)(2,1)S(1)} custom-call(bf16[2,64,64,128]{3,2,1,0:T(8,128)(2,1)} %bitcast.13, bf16[1024,1024]{1,0:T(8,128)(2,1)} %constant.66.clone.first_hbm, bf16[64,128,128]{2,1,0:T(8,128)(2,1)} %constant.67.clone.second_hbm), custom_call_target="tpu_custom_call" | custom-call | flops 12000000000 | bytes 8000000 | tf_op jit(solution)/shard_map/transform/pallas_call | solution.py:173
  18.6 2.6 %all-to-all-done = f32[16,64,128]{2,1,0:T(8,128)S(1)} async-done(((f32[16,64,128]{2,1,0:T(8,128)}), f32[16,64,128]{2,1,0:T(8,128)S(1)}, u32[]{:S(2)}, u32[]{:S(2)}) %all-to-all-start) | async-done | bytes 524320 | tf_op jit(solution)/shard_map/all_to_all | solution.py:385
  21.2 0.2 select_reduce_fusion.3
  21.4 0.6 %fusion.7 = (s32[]{:T(128)}, s32[64]{0:T(128)S(1)}, pred[64]{0:T(512)(128)(4,1)S(1)}, s32[64]{0:T(128)S(1)}, s32[64]{0:T(128)S(1)}) fusion(s32[64]{0:T(128)S(1)} %copy-done.2, s32[]{:T(128)S(6)} %axis_index.49, s32[64]{0:T(128)S(1)} %copy-done.3, s32[64]{0:T(128)S(1)} %select_reduce_fusion.3), kind=kLoop, calls=%fused_computation.29 | loop fusion | flops 2751 | bytes 1608 | tf_op jit(solution)/shard_map/reduce_sum | solution.py:403
  22.0 0.1 select_reduce_fusion.2
  22.2 0.1 select_reduce_fusion.1
  22.3 0.1 select_reduce_fusion
  22.4 0.7 %concatenate.3.plan = s32[384]{0:T(512)S(1)} concatenate(s32[256]{0:T(256)S(1)} %select_reduce_fusion, s32[64]{0:T(128)S(1)} %select_reduce_fusion.1, s32[1]{0:T(128)} %bitcast.2, s32[1]{0:T(128)} %bitcast.3, s32[1]{0:T(128)} %bitcast.4, s32[61]{0:T(128)S(1)} %broadcast_in_dim.66), dimensions={0} | concatenate | bytes 3072 | tf_op jit(solution)/shard_map/concatenate | solution.py:404
  23.1 2.4 %collective-permute-done.other_hbm = bf16[64,128,128]{2,1,0:T(8,128)(2,1)} collective-permute-done((bf16[64,128,128]{2,1,0:T(8,128)(2,1)S(1)}, bf16[64,128,128]{2,1,0:T(8,128)(2,1)}, u32[]{:S(2)}, u32[]{:S(2)}) %collective-permute-start) | collective-permute-done | bytes 2097184 | tf_op jit(solution)/shard_map/ppermute | solution.py:411
  25.5 9.4 %degrid.1 = bf16[16,64,128]{2,1,0:T(8,128)(2,1)} custom-call(s32[384]{0:T(512)S(1)} %concatenate.3.plan, bf16[64,128,128]{2,1,0:T(8,128)(2,1)S(1)} %transform.1.own_ref, bf16[64,128,128]{2,1,0:T(8,128)(2,1)} %collective-permute-done.other_hbm, f32[16,8,8,128]{3,2,1,0:T(8,128)S(1)} %bitcast.10), custom_call_target="tpu_custom_call" | custom-call | flops 12000000000 | bytes 8000000 | tf_op jit(solution)/shard_map/degrid/pallas_call | solution.py:291
  34.9 4.7 %all-to-all-start.1 = ((bf16[16,64,128]{2,1,0:T(8,128)(2,1)}), bf16[16,64,128]{2,1,0:T(8,128)(2,1)S(1)}, u32[]{:S(2)}, u32[]{:S(2)}) async-start(bf16[16,64,128]{2,1,0:T(8,128)(2,1)} %degrid.1), calls=%async_computation.1 | async-start | bytes 524288 | tf_op jit(solution)/shard_map/all_to_all | solution.py:413
  39.6 10.0 %all-to-all-done.1 = bf16[16,64,128]{2,1,0:T(8,128)(2,1)S(1)} async-done(((bf16[16,64,128]{2,1,0:T(8,128)(2,1)}), bf16[16,64,128]{2,1,0:T(8,128)(2,1)S(1)}, u32[]{:S(2)}, u32[]{:S(2)}) %all-to-all-start.1) | async-done | bytes 262176 | tf_op jit(solution)/shard_map/all_to_all | solution.py:413
  49.6 1.7 %collective-permute-start.1 = (f32[64,128]{1,0:T(8,128)S(1)}, f32[64,128]{1,0:T(8,128)S(1)}, u32[]{:S(2)}, u32[]{:S(2)}) collective-permute-start(f32[64,128]{1,0:T(8,128)S(1)} %convert_reduce_fusion.own_ref), channel_id=1, source_target_pairs={{0,1},{1,2},{2,3},{3,0},{4,5},{5,6},{6,7},{7,4},{8,9},{9,10},{10,1... | collective-permute-start | bytes 98312 | tf_op jit(solution)/shard_map/ppermute | solution.py:416
  51.3 2.9 %collective-permute-start.2 = (f32[64,128]{1,0:T(8,128)S(1)}, f32[64,128]{1,0:T(8,128)S(1)}, u32[]{:S(2)}, u32[]{:S(2)}) collective-permute-start(f32[64,128]{1,0:T(8,128)S(1)} %convert_reduce_fusion.own_ref), channel_id=1, source_target_pairs={{0,2},{1,3},{2,0},{3,1},{4,6},{5,7},{6,4},{7,5},{8,10},{9,11},{10,... | collective-permute-start | bytes 98312 | tf_op jit(solution)/shard_map/ppermute | solution.py:416
  54.2 1.3 %collective-permute-start.3 = (f32[64,128]{1,0:T(8,128)S(1)}, f32[64,128]{1,0:T(8,128)S(1)}, u32[]{:S(2)}, u32[]{:S(2)}) collective-permute-start(f32[64,128]{1,0:T(8,128)S(1)} %convert_reduce_fusion.own_ref), channel_id=1, source_target_pairs={{0,3},{1,0},{2,1},{3,2},{4,7},{5,4},{6,5},{7,6},{8,11},{9,8},{10,9... | collective-permute-start | bytes 98312 | tf_op jit(solution)/shard_map/ppermute | solution.py:416
  55.5 0.2 select_reduce_fusion.4.limits
  55.7 0.2 jones.1.jones_ref
  56.0 0.7 %collective-permute-done.2.two_ref = f32[64,128]{1,0:T(8,128)S(1)} collective-permute-done((f32[64,128]{1,0:T(8,128)S(1)}, f32[64,128]{1,0:T(8,128)S(1)}, u32[]{:S(2)}, u32[]{:S(2)}) %collective-permute-start.2) | collective-permute-done | bytes 32800 | tf_op jit(solution)/shard_map/ppermute | solution.py:416
  56.7 1.4 %collective-permute-done.3.three_ref = f32[64,128]{1,0:T(8,128)S(1)} collective-permute-done((f32[64,128]{1,0:T(8,128)S(1)}, f32[64,128]{1,0:T(8,128)S(1)}, u32[]{:S(2)}, u32[]{:S(2)}) %collective-permute-start.3) | collective-permute-done | bytes 32800 | tf_op jit(solution)/shard_map/ppermute | solution.py:416
  58.1 1.2 %correct.1 = f32[1,2,4,8,128]{4,3,2,1,0:T(8,128)} custom-call(s32[4]{0:T(128)S(1)} %select_reduce_fusion.4.limits, f32[4,4,2,8,128]{4,3,2,1,0:T(8,128)S(1)} %jones.1.jones_ref, f32[64,128]{1,0:T(8,128)S(1)} %convert_reduce_fusion.own_ref, f32[64,128]{1,0:T(8,128)S(1)} %collective-permute-done.1.one_ref, f32[64,128]{1,0:T(8,128)S(1)} %collective-permute-done.2.two_ref, ...), custom_call_target="tpu_custom_call" | custom-call | tf_op jit(solution)/shard_map/correct/pallas_call | solution.py:370
  (12 shorter events, 0.1 us)
Async XLA Ops:
  1.7 19.5 %all-to-all-start = ((f32[16,64,128]{2,1,0:T(8,128)}), f32[16,64,128]{2,1,0:T(8,128)S(1)}, u32[]{:S(2)}, u32[]{:S(2)}) async-start(f32[16,64,128]{2,1,0:T(8,128)} %spread.1), calls=%async_computation | async-start | bytes 1048576 | tf_op jit(solution)/shard_map/all_to_all | solution.py:385
  9.7 11.5 %copy-start.3 = (s32[64]{0:T(128)S(1)}, s32[64]{0:T(128)}, u32[]{:S(2)}) copy-start(s32[64]{0:T(128)} %param.9) | copy-start | bytes 772
  9.7 11.7 %copy-start.2 = (s32[64]{0:T(128)S(1)}, s32[64]{0:T(128)}, u32[]{:S(2)}) copy-start(s32[64]{0:T(128)} %param.10) | copy-start | bytes 772
  21.2 4.3 %collective-permute-start = (bf16[64,128,128]{2,1,0:T(8,128)(2,1)S(1)}, bf16[64,128,128]{2,1,0:T(8,128)(2,1)}, u32[]{:S(2)}, u32[]{:S(2)}) collective-permute-start(bf16[64,128,128]{2,1,0:T(8,128)(2,1)S(1)} %transform.1.own_ref), channel_id=1, source_target_pairs={{0,4},{4,0},{1,5},{5,1},{2,6},{6,2},{3,7},{7,3},{8,12},{12,8},{9,1... | collective-permute-start | bytes 6291464 | tf_op jit(solution)/shard_map/ppermute | solution.py:411
  23.1 32.6 %copy-start.1 = (s32[4,8,2,128]{3,2,1,0:T(2,128)S(1)}, s32[4,8,2,128]{3,2,1,0:T(2,128)}, u32[]{:S(2)}) copy-start(s32[4,8,2,128]{3,2,1,0:T(2,128)} %param.12) | copy-start | bytes 98308
  23.1 32.6 %copy-start = (f32[8,512]{1,0:T(8,128)S(1)}, f32[8,512]{1,0:T(8,128)}, u32[]{:S(2)}) copy-start(f32[8,512]{1,0:T(8,128)} %table_ref.1) | copy-start | bytes 49156
  34.9 14.7 %all-to-all-start.1 = ((bf16[16,64,128]{2,1,0:T(8,128)(2,1)}), bf16[16,64,128]{2,1,0:T(8,128)(2,1)S(1)}, u32[]{:S(2)}, u32[]{:S(2)}) async-start(bf16[16,64,128]{2,1,0:T(8,128)(2,1)} %degrid.1), calls=%async_computation.1 | async-start | bytes 524288 | tf_op jit(solution)/shard_map/all_to_all | solution.py:413
  49.6 6.4 %collective-permute-start.1 = (f32[64,128]{1,0:T(8,128)S(1)}, f32[64,128]{1,0:T(8,128)S(1)}, u32[]{:S(2)}, u32[]{:S(2)}) collective-permute-start(f32[64,128]{1,0:T(8,128)S(1)} %convert_reduce_fusion.own_ref), channel_id=1, source_target_pairs={{0,1},{1,2},{2,3},{3,0},{4,5},{5,6},{6,7},{7,4},{8,9},{9,10},{10,1... | collective-permute-start | bytes 98312 | tf_op jit(solution)/shard_map/ppermute | solution.py:416
  51.3 5.4 %collective-permute-start.2 = (f32[64,128]{1,0:T(8,128)S(1)}, f32[64,128]{1,0:T(8,128)S(1)}, u32[]{:S(2)}, u32[]{:S(2)}) collective-permute-start(f32[64,128]{1,0:T(8,128)S(1)} %convert_reduce_fusion.own_ref), channel_id=1, source_target_pairs={{0,2},{1,3},{2,0},{3,1},{4,6},{5,7},{6,4},{7,5},{8,10},{9,11},{10,... | collective-permute-start | bytes 98312 | tf_op jit(solution)/shard_map/ppermute | solution.py:416
  54.2 3.9 %collective-permute-start.3 = (f32[64,128]{1,0:T(8,128)S(1)}, f32[64,128]{1,0:T(8,128)S(1)}, u32[]{:S(2)}, u32[]{:S(2)}) collective-permute-start(f32[64,128]{1,0:T(8,128)S(1)} %convert_reduce_fusion.own_ref), channel_id=1, source_target_pairs={{0,3},{1,0},{2,1},{3,2},{4,7},{5,4},{6,5},{7,6},{8,11},{9,8},{10,9... | collective-permute-start | bytes 98312 | tf_op jit(solution)/shard_map/ppermute | solution.py:416

commit v5 on v4

--- a/solution.py
+++ b/solution.py
@@ -30,7 +30,7 @@
     index = np.arange(W)
     angles = (index[:, None] * index[None, :] % W) * (2.0 * math.pi / W)
     waves = np.concatenate([np.cos(angles[: W // 2 + 1]), np.sin(angles[1 : W // 2])], axis=0)
-    return np.kron(waves, np.eye(GROUP)).astype(BF16)
+    return np.repeat(waves, GROUP, axis=1).astype(BF16)
 
 
 def second_table():
@@ -70,39 +70,51 @@
 
 
 def transform_kernel(
-    facets_hbm, first_hbm, second_hbm, out_ref, facets_ref, first_ref, second_ref, sections, mixed, sems
+    facets_hbm, waves_hbm, second_hbm, out_ref, facets_ref, waves_ref, second_ref, first_ref, sections, mixed, sems
 ):
     half = W // 2
-    first_copy = pltpu.make_async_copy(first_hbm, first_ref, sems.at[0])
-    second_copy = pltpu.make_async_copy(second_hbm, second_ref, sems.at[1])
+    wide = W * GROUP
+    waves_copy = pltpu.make_async_copy(waves_hbm, waves_ref, sems.at[4])
+    quarters = [pl.ds(16 * i, 16) for i in range(4)]
+    second_copies = [
+        pltpu.make_async_copy(second_hbm.at[at], second_ref.at[at], sems.at[i]) for i, at in enumerate(quarters)
+    ]
     strip_copies = [
-        pltpu.make_async_copy(facets_hbm.at[:, :, pl.ds(GROUP * h, GROUP), :], facets_ref.at[h], sems.at[2 + h])
-        for h in range(W // GROUP)
+        pltpu.make_async_copy(facets_hbm.at[f, at], facets_ref.at[f, at], sems.at[5 + 4 * f + i])
+        for f in range(2)
+        for i, at in enumerate(quarters)
     ]
-    strip_copies[0].start()
-    first_copy.start()
-    for copy in strip_copies[1:]:
+    for copy in [waves_copy] + strip_copies + second_copies:
         copy.start()
-    second_copy.start()
     row = lax.broadcasted_iota(jnp.int32, (2 * W, 2 * W), 0)
     lane = lax.broadcasted_iota(jnp.int32, (2 * W, 2 * W), 1)
     mirror = jnp.where(row == jnp.where(lane < W, W - 1, 3 * W - 1) - lane, 1.0, 0.0).astype(BF16)
+
+    pieces = [slice(piece * 256, piece * 256 + 256) for piece in range(4)]
+    cell = lax.broadcasted_iota(jnp.int32, (256, wide), 0) & (GROUP - 1)
+    same = cell == (lax.broadcasted_iota(jnp.int32, (256, wide), 1) & (GROUP - 1))
+    wave = lax.broadcasted_iota(jnp.int32, (256, W), 1)
+    line = lax.broadcasted_iota(jnp.int32, (256, W), 0) >> 4
+    waves_copy.wait()
+    for piece, rows in enumerate(pieces):
+        pick = jnp.where(line + 16 * piece == wave, 1.0, 0.0).astype(BF16)
+        spread_waves = jnp.dot(pick, waves_ref[...], preferred_element_type=F32)
+        first_ref[rows, :] = jnp.where(same, spread_waves, 0.0).astype(BF16)
+
+    for copy in strip_copies:
+        copy.wait()
     for h in range(W // GROUP):
         at = slice(GROUP * h, GROUP * h + GROUP)
-        strip_copies[h].wait()
-        mirrored = jnp.dot(
-            facets_ref[h, 0].reshape(W * GROUP, 2 * W), mirror, preferred_element_type=F32
-        ).astype(BF16)
-        strips = jnp.concatenate([mirrored, facets_ref[h, 1].reshape(W * GROUP, 2 * W)], axis=1)
-        if h == 0:
-            first_copy.wait()
-        for piece in range(4):
-            rows = slice(piece * 256, piece * 256 + 256)
+        strip = [facets_ref[f, :, at, :].reshape(wide, 2 * W) for f in range(2)]
+        mirrored = jnp.dot(strip[0], mirror, preferred_element_type=F32).astype(BF16)
+        strips = jnp.concatenate([mirrored, strip[1]], axis=1)
+        for piece, rows in enumerate(pieces):
             part = jnp.dot(first_ref[rows, :], strips, preferred_element_type=F32).astype(BF16)
             for f in range(2):
                 block = part[:, 2 * W * f : 2 * W * (f + 1)].reshape(16, GROUP, 2 * W)
                 sections[f, piece * 16 : piece * 16 + 16, at, :] = block
-    second_copy.wait()
+    for copy in second_copies:
+        copy.wait()
 
     low_lanes = lax.broadcasted_iota(jnp.int32, (S, 2 * W), 1) < W
 
@@ -116,10 +128,10 @@
         )
         return jnp.dot(second_ref[k1], section, preferred_element_type=F32)
 
-    @pl.loop(0, half // 4)
+    @pl.loop(0, half // 16)
     def _(step):
-        for inner in range(4):
-            index = step * 4 + inner
+        for inner in range(16):
+            index = step * 16 + inner
             above = window(half + index, half - index)
             below = window(half - 1 - index, half - 1 - index)
             for pick, grid in enumerate((above + below, above - below)):
@@ -158,11 +170,11 @@
     return pl.pallas_call(
         spread_kernel,
         out_shape=jax.ShapeDtypeStruct((16,) + coords.shape, F32),
-        in_specs=[pl.BlockSpec(memory_space=pltpu.VMEM)],
+        in_specs=[pl.BlockSpec(memory_space=pltpu.HBM)],
         out_specs=pl.BlockSpec(memory_space=pltpu.HBM),
         scratch_shapes=[pltpu.SemaphoreType.DMA((16,))],
         name="spread",
-    )(coords)
+    )(in_hbm(coords))
 
 
 def in_hbm(array):
@@ -176,12 +188,13 @@
         in_specs=[pl.BlockSpec(memory_space=pltpu.HBM)] * 3,
         out_specs=pl.BlockSpec(memory_space=pltpu.VMEM),
         scratch_shapes=[
-            pltpu.VMEM((W // GROUP, 2, W, GROUP, 2 * W), BF16),
+            pltpu.VMEM((2, W, W, 2 * W), BF16),
+            pltpu.VMEM((W, W * GROUP), BF16),
+            pltpu.VMEM((W, 2 * W, 2 * W), BF16),
             pltpu.VMEM((W * GROUP, W * GROUP), BF16),
-            pltpu.VMEM((W, 2 * W, 2 * W), BF16),
             pltpu.VMEM((2, W, W, 2 * W), BF16),
             pltpu.VMEM((4, W // 2, S, 2 * W), F32),
-            pltpu.SemaphoreType.DMA((2 + W // GROUP,)),
+            pltpu.SemaphoreType.DMA((13,)),
         ],
         compiler_params=pltpu.CompilerParams(vmem_limit_bytes=VMEM_LIMIT),
         cost_estimate=pl.CostEstimate(flops=12_000_000_000, bytes_accessed=8_000_000, transcendentals=0),
@@ -216,9 +229,9 @@
 
     def place(index):
         word = plan[index]
-        g = word // (4 * S)
+        g = word >> 8
         kept = jnp.where(index < plan[TOTAL_AT], g, 16 * CAP)
-        return (g // CAP, g % CAP, g, kept, (word // 4) % S, 2 * (word % 4))
+        return (g >> 2, g & 3, g, kept, (word >> 2) & (S - 1), (word & 3) << 1)
 
     def phases_of(o, c, g, kept, s, b):
         blocks = []
@@ -263,12 +276,10 @@
     centre_own = (W * (first_facet % R)).astype(F32) + (W - 0.5 - SG // 2)
     centre_other = (W * (other_facet % R)).astype(F32) + (W - 0.5 - SG // 2)
 
-    @pl.loop(0, 16 * CAP)
-    def _(g):
-        o, c = g // CAP, g % CAP
-
-        @pl.when(plan[UNITS + g] > 0)
-        def _():
+    @pl.loop(0, 16)
+    def _(o):
+        for c in range(CAP):
+            g = o * CAP + c
             x, y = coords_ref[o, c], coords_ref[o, CAP + c]
             real = imag = jnp.zeros((MAXB, VB), F32)
             for q, centre_y in enumerate((centre_own, centre_other)):
@@ -282,7 +293,7 @@
                 imag = imag + (cos * total_imag - sin * total_real)
             scale = 1.0 / (math.sqrt(FH) * SG)
             value = (jnp.concatenate([real, imag], axis=0) * scale).astype(BF16)
-            out_ref[o, pl.ds(pl.multiple_of(2 * MAXB * c, 2 * MAXB), 2 * MAXB), :] = value
+            out_ref[o, 2 * MAXB * c : 2 * MAXB * (c + 1), :] = value
 
 
 def degrid(plan, own, other, coords, together=TOGETHER):
@@ -305,7 +316,7 @@
     )(plan, own, other, coords)
 
 
-def jones_kernel(place, stations_ref, table_ref, out_ref):
+def jones_kernel(place, stations_ref, table_ref, out_ref, mask_ref):
     pol = place[0]
     row_side, col_side = pol // 2, pol % 2
 
@@ -324,7 +335,9 @@
         return value
 
     left_table, right_table = side(row_side), side(col_side)
+    block = lax.broadcasted_iota(jnp.int32, (MAXB, VB), 0)
     for c in range(CAP):
+        mask_ref[c] = jnp.where(block < place[1 + c], 1.0, 0.0)
         left, right = stations_ref[c, 0], stations_ref[c, 1]
         lefts = [[entry(left_table, 2 * k + ri, left) for ri in range(2)] for k in range(2)]
         rights = [[entry(right_table, 2 * k + ri, right) for ri in range(2)] for k in range(2)]
@@ -341,16 +354,18 @@
     vmem = pl.BlockSpec(memory_space=pltpu.VMEM)
     return pl.pallas_call(
         jones_kernel,
-        out_shape=jax.ShapeDtypeStruct((4, CAP, 2, MAXB, VB), F32),
+        out_shape=[
+            jax.ShapeDtypeStruct((4, CAP, 2, MAXB, VB), F32),
+            jax.ShapeDtypeStruct((CAP, MAXB, VB), F32),
+        ],
         in_specs=[smem, vmem, vmem],
-        out_specs=vmem,
+        out_specs=[vmem, vmem],
         compiler_params=pltpu.CompilerParams(vmem_limit_bytes=VMEM_LIMIT),
         name="jones",
     )(place, stations, table)
 
 
-def correct_kernel(limits, jones_ref, own_ref, one_ref, two_ref, three_ref, out_ref):
-    block = lax.broadcasted_iota(jnp.int32, (MAXB, VB), 0)
+def correct_kernel(jones_ref, mask_ref, own_ref, one_ref, two_ref, three_ref, out_ref):
     for c in range(CAP):
         total_real = total_imag = jnp.zeros((MAXB, VB), F32)
         for turn, ref in enumerate((own_ref, one_ref, two_ref, three_ref)):
@@ -359,22 +374,21 @@
             step_real, step_imag = jones_ref[turn, c, 0], jones_ref[turn, c, 1]
             total_real = total_real + (step_real * real - step_imag * imag)
             total_imag = total_imag + (step_real * imag + step_imag * real)
-        keep = block < limits[c]
+        keep = mask_ref[c] > 0.0
         out_ref[0, 0, c] = jnp.where(keep, total_real, 0.0)
         out_ref[0, 1, c] = jnp.where(keep, total_imag, 0.0)
 
 
-def correct(limits, factors, parts):
-    smem = pl.BlockSpec(memory_space=pltpu.SMEM)
+def correct(factors, mask, parts):
     vmem = pl.BlockSpec(memory_space=pltpu.VMEM)
     return pl.pallas_call(
         correct_kernel,
         out_shape=jax.ShapeDtypeStruct((1, 2, CAP, MAXB, VB), F32),
-        in_specs=[smem] + [vmem] * 5,
+        in_specs=[vmem] * 6,
         out_specs=vmem,
         compiler_params=pltpu.CompilerParams(vmem_limit_bytes=VMEM_LIMIT),
         name="correct",
-    )(limits, factors, *parts)
+    )(factors, mask, *parts)
 
 
 def on_device(facets, owners, counts, coords, station_ids, jones_table):
@@ -412,9 +426,10 @@
     parts = degrid(plan, own, other, coords_all)
     parts = lax.all_to_all(parts, ("z", "x"), split_axis=0, concat_axis=0, tiled=True)
     visible = jnp.sum(parts.astype(F32), axis=0)
-    factors = jones(pol.reshape(1).astype(jnp.int32), jnp.moveaxis(station_ids, 2, 1), jones_table)
+    place = jnp.concatenate([pol.reshape(1), own_limits]).astype(jnp.int32)
+    factors, mask = jones(place, jnp.moveaxis(station_ids, 2, 1), jones_table)
     turns = [lax.ppermute(visible, "pol", [(i, (i + k) % 4) for i in range(4)]) for k in (1, 2, 3)]
-    return correct(own_limits, factors, [visible] + turns)
+    return correct(factors, mask, [visible] + turns)
 
 
 def solution(mesh):

time: 59.6 us -> 73.3 us (1.23)
  Pallas kernels: 21.4 us -> 36.8 us
  starting transfers between devices: 18.6 us -> 17.4 us
    pallas_call x1, Pallas kernels: 1.69 us -> 17.1 us  [spread(): pl.pallas_call(spread_kernel, out_shape=jax.ShapeDtypeStruct((16,) + coor...]
    pallas_call x1, Pallas kernels: 9.37 us -> 10.9 us  [degrid(): pl.pallas_call(functools.partial(degrid_kernel, together), out_shape=jax....]
    all_to_all x1, waiting for transfers between devices: 2.59 us -> 4.11 us  [on_device(): lax.all_to_all(spread(coords.reshape(2 * CAP * MAXB, VB)), ('z', 'x'), sp...]
    pallas_call x1, Pallas kernels: 8.91 us -> 7.39 us  [transform(): pl.pallas_call(transform_kernel, out_shape=jax.ShapeDtypeStruct((S, 2 * W...]
    all_to_all x1, waiting for transfers between devices: 9.96 us -> 8.45 us  [on_device(): lax.all_to_all(parts, ('z', 'x'), split_axis=0, concat_axis=0, tiled=True)]
    all_to_all x1, starting transfers between devices: 4.72 us -> 3.54 us  [on_device(): lax.all_to_all(parts, ('z', 'x'), split_axis=0, concat_axis=0, tiled=True)]
  transfers between devices with their start and end apart: 6 -> 6, of which waited for: 5 -> 5; matrix products, arithmetic and copies ran while one was open for 3% -> 3% of each run, Pallas kernels for 15% -> 11%
where the time goes in v5:
time: 73.3 us; the launch traced here: 73.2 us
  Pallas kernels  36.8 us (50%)
  starting transfers between devices  17.4 us (24%)
  waiting for transfers between devices  16.6 us (23%)
  other arithmetic  1.46 us (2%)
  local copies, waits for them, and re-layouts  0.75 us (1%)
    pallas_call x1, Pallas kernels, spread(): pl.pallas_call(spread_kernel, out_shape=jax.ShapeDtypeStruct((16,) + coor...  17.1 us
    pallas_call x1, Pallas kernels, degrid(): pl.pallas_call(functools.partial(degrid_kernel, together), out_shape=jax....  10.9 us
    all_to_all x1, waiting for transfers between devices, on_device(): lax.all_to_all(parts, ('z', 'x'), split_axis=0, concat_axis=0, tiled=True)  8.45 us
    all_to_all x1, starting transfers between devices, on_device(): lax.all_to_all(spread(coords.reshape(2 * CAP * MAXB, VB)), ('z', 'x'), sp...  7.97 us
    pallas_call x1, Pallas kernels, transform(): pl.pallas_call(transform_kernel, out_shape=jax.ShapeDtypeStruct((S, 2 * W...  7.39 us
    ppermute x3, starting transfers between devices, on_device(): lax.ppermute(visible, 'pol', [(i, (i + k) % 4) for i in range(4)])  5.87 us
    all_to_all x1, waiting for transfers between devices, on_device(): lax.all_to_all(spread(coords.reshape(2 * CAP * MAXB, VB)), ('z', 'x'), sp...  4.11 us
    all_to_all x1, starting transfers between devices, on_device(): lax.all_to_all(parts, ('z', 'x'), split_axis=0, concat_axis=0, tiled=True)  3.54 us
  transfers between devices with their start and end apart: 6, of which 5 were waited for; matrix products, arithmetic and copies ran while one was open for 3% of the time, Pallas kernels for 11%

profile of v5, /device:TPU:0, one launch (start us, length us, event | category | flops | bytes accessed | tf_op | source)
XLA Modules:
  0.0 73.2 jit_solution(14929201316452068356)
XLA Ops:
  0.0 17.1 %spread.1 = f32[16,64,128]{2,1,0:T(8,128)} custom-call(f32[64,128]{1,0:T(8,128)} %bitcast.12), custom_call_target="tpu_custom_call" | custom-call | tf_op jit(solution)/shard_map/spread/pallas_call | solution.py:170
  17.1 8.0 %all-to-all-start = ((f32[16,64,128]{2,1,0:T(8,128)}), f32[16,64,128]{2,1,0:T(8,128)S(1)}, u32[]{:S(2)}, u32[]{:S(2)}) async-start(f32[16,64,128]{2,1,0:T(8,128)} %spread.1), calls=%async_computation | async-start | bytes 1048576 | tf_op jit(solution)/shard_map/all_to_all | solution.py:399
  25.1 0.0 copy-start.3
  25.1 7.4 %transform.1.own_ref = bf16[64,128,128]{2,1,0:T(8,128)(2,1)S(1)} custom-call(bf16[2,64,64,128]{3,2,1,0:T(8,128)(2,1)} %bitcast.13, bf16[64,1024]{1,0:T(8,128)(2,1)} %constant.66.clone.waves_hbm, bf16[64,128,128]{2,1,0:T(8,128)(2,1)} %constant.67.clone.second_hbm), custom_call_target="tpu_custom_call" | custom-call | flops 12000000000 | bytes 8000000 | tf_op jit(solution)/shard_map/transform/pallas_call | solution.py:185
  32.5 4.1 %all-to-all-done = f32[16,64,128]{2,1,0:T(8,128)S(1)} async-done(((f32[16,64,128]{2,1,0:T(8,128)}), f32[16,64,128]{2,1,0:T(8,128)S(1)}, u32[]{:S(2)}, u32[]{:S(2)}) %all-to-all-start) | async-done | bytes 524320 | tf_op jit(solution)/shard_map/all_to_all | solution.py:399
  36.7 0.2 select_reduce_fusion.3
  36.8 0.6 fusion.7
  37.5 0.1 select_reduce_fusion.2
  37.6 0.1 select_reduce_fusion.1
  37.7 0.1 select_reduce_fusion
  37.8 0.7 concatenate.7.plan
  38.6 2.4 %collective-permute-done.other_hbm = bf16[64,128,128]{2,1,0:T(8,128)(2,1)} collective-permute-done((bf16[64,128,128]{2,1,0:T(8,128)(2,1)S(1)}, bf16[64,128,128]{2,1,0:T(8,128)(2,1)}, u32[]{:S(2)}, u32[]{:S(2)}) %collective-permute-start) | collective-permute-done | bytes 2097184 | tf_op jit(solution)/shard_map/ppermute | solution.py:425
  40.9 10.9 %degrid.1 = bf16[16,64,128]{2,1,0:T(8,128)(2,1)} custom-call(s32[384]{0:T(512)S(1)} %concatenate.7.plan, bf16[64,128,128]{2,1,0:T(8,128)(2,1)S(1)} %transform.1.own_ref, bf16[64,128,128]{2,1,0:T(8,128)(2,1)} %collective-permute-done.other_hbm, f32[16,8,8,128]{3,2,1,0:T(8,128)S(1)} %bitcast.10), custom_call_target="tpu_custom_call" | custom-call | flops 12000000000 | bytes 8000000 | tf_op jit(solution)/shard_map/degrid/pallas_call | solution.py:302
  51.8 3.5 %all-to-all-start.1 = ((bf16[16,64,128]{2,1,0:T(8,128)(2,1)}), bf16[16,64,128]{2,1,0:T(8,128)(2,1)S(1)}, u32[]{:S(2)}, u32[]{:S(2)}) async-start(bf16[16,64,128]{2,1,0:T(8,128)(2,1)} %degrid.1), calls=%async_computation.1 | async-start | bytes 524288 | tf_op jit(solution)/shard_map/all_to_all | solution.py:427
  55.4 0.2 select_reduce_fusion.4
  55.6 8.5 %all-to-all-done.1 = bf16[16,64,128]{2,1,0:T(8,128)(2,1)S(1)} async-done(((bf16[16,64,128]{2,1,0:T(8,128)(2,1)}), bf16[16,64,128]{2,1,0:T(8,128)(2,1)S(1)}, u32[]{:S(2)}, u32[]{:S(2)}) %all-to-all-start.1) | async-done | bytes 262176 | tf_op jit(solution)/shard_map/all_to_all | solution.py:427
  64.1 1.6 %collective-permute-start.1 = (f32[64,128]{1,0:T(8,128)S(1)}, f32[64,128]{1,0:T(8,128)S(1)}, u32[]{:S(2)}, u32[]{:S(2)}) collective-permute-start(f32[64,128]{1,0:T(8,128)S(1)} %convert_reduce_fusion.own_ref), channel_id=1, source_target_pairs={{0,1},{1,2},{2,3},{3,0},{4,5},{5,6},{6,7},{7,4},{8,9},{9,10},{10,1... | collective-permute-start | bytes 98312 | tf_op jit(solution)/shard_map/ppermute | solution.py:431
  65.7 2.9 %collective-permute-start.2 = (f32[64,128]{1,0:T(8,128)S(1)}, f32[64,128]{1,0:T(8,128)S(1)}, u32[]{:S(2)}, u32[]{:S(2)}) collective-permute-start(f32[64,128]{1,0:T(8,128)S(1)} %convert_reduce_fusion.own_ref), channel_id=1, source_target_pairs={{0,2},{1,3},{2,0},{3,1},{4,6},{5,7},{6,4},{7,5},{8,10},{9,11},{10,... | collective-permute-start | bytes 98312 | tf_op jit(solution)/shard_map/ppermute | solution.py:431
  68.6 1.3 %collective-permute-start.3 = (f32[64,128]{1,0:T(8,128)S(1)}, f32[64,128]{1,0:T(8,128)S(1)}, u32[]{:S(2)}, u32[]{:S(2)}) collective-permute-start(f32[64,128]{1,0:T(8,128)S(1)} %convert_reduce_fusion.own_ref), channel_id=1, source_target_pairs={{0,3},{1,0},{2,1},{3,2},{4,7},{5,4},{6,5},{7,6},{8,11},{9,8},{10,9... | collective-permute-start | bytes 98312 | tf_op jit(solution)/shard_map/ppermute | solution.py:431
  70.0 0.1 pad_add_fusion.place
  70.0 0.8 %jones.1 = (f32[4,4,2,8,128]{4,3,2,1,0:T(8,128)S(1)}, f32[4,8,128]{2,1,0:T(8,128)S(1)}) custom-call(s32[5]{0:T(128)S(1)} %pad_add_fusion.place, s32[4,2,8,128]{3,2,1,0:T(8,128)S(1)} %bitcast.11, f32[8,512]{1,0:T(8,128)S(1)} %copy-done), custom_call_target="tpu_custom_call" | custom-call | tf_op jit(solution)/shard_map/jones/pallas_call | solution.py:355
  70.9 0.3 collective-permute-done.2.two_ref
  71.2 1.4 %collective-permute-done.3.three_ref = f32[64,128]{1,0:T(8,128)S(1)} collective-permute-done((f32[64,128]{1,0:T(8,128)S(1)}, f32[64,128]{1,0:T(8,128)S(1)}, u32[]{:S(2)}, u32[]{:S(2)}) %collective-permute-start.3) | collective-permute-done | bytes 32800 | tf_op jit(solution)/shard_map/ppermute | solution.py:431
  72.5 0.6 correct.1
  (13 shorter events, 0.1 us)
Async XLA Ops:
  17.1 19.5 %all-to-all-start = ((f32[16,64,128]{2,1,0:T(8,128)}), f32[16,64,128]{2,1,0:T(8,128)S(1)}, u32[]{:S(2)}, u32[]{:S(2)}) async-start(f32[16,64,128]{2,1,0:T(8,128)} %spread.1), calls=%async_computation | async-start | bytes 1048576 | tf_op jit(solution)/shard_map/all_to_all | solution.py:399
  25.1 11.5 %copy-start.3 = (s32[64]{0:T(128)S(1)}, s32[64]{0:T(128)}, u32[]{:S(2)}) copy-start(s32[64]{0:T(128)} %param.9) | copy-start | bytes 772
  25.1 11.7 %copy-start.2 = (s32[64]{0:T(128)S(1)}, s32[64]{0:T(128)}, u32[]{:S(2)}) copy-start(s32[64]{0:T(128)} %param.10) | copy-start | bytes 772
  36.6 4.3 %collective-permute-start = (bf16[64,128,128]{2,1,0:T(8,128)(2,1)S(1)}, bf16[64,128,128]{2,1,0:T(8,128)(2,1)}, u32[]{:S(2)}, u32[]{:S(2)}) collective-permute-start(bf16[64,128,128]{2,1,0:T(8,128)(2,1)S(1)} %transform.1.own_ref), channel_id=1, source_target_pairs={{0,4},{4,0},{1,5},{5,1},{2,6},{6,2},{3,7},{7,3},{8,12},{12,8},{9,1... | collective-permute-start | bytes 6291464 | tf_op jit(solution)/shard_map/ppermute | solution.py:425
  38.6 31.5 %copy-start.1 = (s32[4,8,2,128]{3,2,1,0:T(2,128)S(1)}, s32[4,8,2,128]{3,2,1,0:T(2,128)}, u32[]{:S(2)}) copy-start(s32[4,8,2,128]{3,2,1,0:T(2,128)} %param.12) | copy-start | bytes 98308
  38.6 31.5 %copy-start = (f32[8,512]{1,0:T(8,128)S(1)}, f32[8,512]{1,0:T(8,128)}, u32[]{:S(2)}) copy-start(f32[8,512]{1,0:T(8,128)} %table_ref.1) | copy-start | bytes 49156
  51.8 12.2 %all-to-all-start.1 = ((bf16[16,64,128]{2,1,0:T(8,128)(2,1)}), bf16[16,64,128]{2,1,0:T(8,128)(2,1)S(1)}, u32[]{:S(2)}, u32[]{:S(2)}) async-start(bf16[16,64,128]{2,1,0:T(8,128)(2,1)} %degrid.1), calls=%async_computation.1 | async-start | bytes 524288 | tf_op jit(solution)/shard_map/all_to_all | solution.py:427
  64.1 6.8 %collective-permute-start.1 = (f32[64,128]{1,0:T(8,128)S(1)}, f32[64,128]{1,0:T(8,128)S(1)}, u32[]{:S(2)}, u32[]{:S(2)}) collective-permute-start(f32[64,128]{1,0:T(8,128)S(1)} %convert_reduce_fusion.own_ref), channel_id=1, source_target_pairs={{0,1},{1,2},{2,3},{3,0},{4,5},{5,6},{6,7},{7,4},{8,9},{9,10},{10,1... | collective-permute-start | bytes 98312 | tf_op jit(solution)/shard_map/ppermute | solution.py:431
  65.7 5.4 %collective-permute-start.2 = (f32[64,128]{1,0:T(8,128)S(1)}, f32[64,128]{1,0:T(8,128)S(1)}, u32[]{:S(2)}, u32[]{:S(2)}) collective-permute-start(f32[64,128]{1,0:T(8,128)S(1)} %convert_reduce_fusion.own_ref), channel_id=1, source_target_pairs={{0,2},{1,3},{2,0},{3,1},{4,6},{5,7},{6,4},{7,5},{8,10},{9,11},{10,... | collective-permute-start | bytes 98312 | tf_op jit(solution)/shard_map/ppermute | solution.py:431
  68.6 3.9 %collective-permute-start.3 = (f32[64,128]{1,0:T(8,128)S(1)}, f32[64,128]{1,0:T(8,128)S(1)}, u32[]{:S(2)}, u32[]{:S(2)}) collective-permute-start(f32[64,128]{1,0:T(8,128)S(1)} %convert_reduce_fusion.own_ref), channel_id=1, source_target_pairs={{0,3},{1,0},{2,1},{3,2},{4,7},{5,4},{6,5},{7,6},{8,11},{9,8},{10,9... | collective-permute-start | bytes 98312 | tf_op jit(solution)/shard_map/ppermute | solution.py:431

commit v6 on v5

--- a/solution.py
+++ b/solution.py
@@ -170,11 +170,11 @@
     return pl.pallas_call(
         spread_kernel,
         out_shape=jax.ShapeDtypeStruct((16,) + coords.shape, F32),
-        in_specs=[pl.BlockSpec(memory_space=pltpu.HBM)],
+        in_specs=[pl.BlockSpec(memory_space=pltpu.VMEM)],
         out_specs=pl.BlockSpec(memory_space=pltpu.HBM),
         scratch_shapes=[pltpu.SemaphoreType.DMA((16,))],
         name="spread",
-    )(in_hbm(coords))
+    )(coords)
 
 
 def in_hbm(array):

time: 73.3 us -> 56.7 us (0.77)
  Pallas kernels: 36.8 us -> 20.4 us
    pallas_call x1, Pallas kernels: 17.1 us -> 1.69 us  [spread(): pl.pallas_call(spread_kernel, out_shape=jax.ShapeDtypeStruct((16,) + coor...]
    pallas_call x1, Pallas kernels: 10.9 us -> 9.9 us  [degrid(): pl.pallas_call(functools.partial(degrid_kernel, together), out_shape=jax....]
  transfers between devices with their start and end apart: 6 -> 6, of which waited for: 5 -> 5; matrix products, arithmetic and copies ran while one was open for 3% -> 4% of each run, Pallas kernels for 11% -> 14%
where the time goes in v6:
time: 56.7 us; the launch traced here: 56.9 us
  Pallas kernels  20.4 us (36%)
  starting transfers between devices  17.4 us (31%)
  waiting for transfers between devices  16.7 us (29%)
  other arithmetic  1.46 us (3%)
  local copies, waits for them, and re-layouts  0.75 us (1%)
    pallas_call x1, Pallas kernels, degrid(): pl.pallas_call(functools.partial(degrid_kernel, together), out_shape=jax....  9.9 us
    all_to_all x1, waiting for transfers between devices, on_device(): lax.all_to_all(parts, ('z', 'x'), split_axis=0, concat_axis=0, tiled=True)  8.55 us
    all_to_all x1, starting transfers between devices, on_device(): lax.all_to_all(spread(coords.reshape(2 * CAP * MAXB, VB)), ('z', 'x'), sp...  7.97 us
    pallas_call x1, Pallas kernels, transform(): pl.pallas_call(transform_kernel, out_shape=jax.ShapeDtypeStruct((S, 2 * W...  7.39 us
    ppermute x3, starting transfers between devices, on_device(): lax.ppermute(visible, 'pol', [(i, (i + k) % 4) for i in range(4)])  5.9 us
    all_to_all x1, waiting for transfers between devices, on_device(): lax.all_to_all(spread(coords.reshape(2 * CAP * MAXB, VB)), ('z', 'x'), sp...  4.11 us
    all_to_all x1, starting transfers between devices, on_device(): lax.all_to_all(parts, ('z', 'x'), split_axis=0, concat_axis=0, tiled=True)  3.54 us
    ppermute x1, waiting for transfers between devices, on_device(): other = lax.ppermute(sent, 'core', [(0, 1), (1, 0)])  2.37 us
  transfers between devices with their start and end apart: 6, of which 5 were waited for; matrix products, arithmetic and copies ran while one was open for 4% of the time, Pallas kernels for 14%

profile of v6, /device:TPU:0, one launch (start us, length us, event | category | flops | bytes accessed | tf_op | source)
XLA Modules:
  0.0 56.9 jit_solution(16955046069394143444)
XLA Ops:
  0.0 1.7 %spread.1 = f32[16,64,128]{2,1,0:T(8,128)} custom-call(f32[64,128]{1,0:T(8,128)} %bitcast.12), custom_call_target="tpu_custom_call" | custom-call | tf_op jit(solution)/shard_map/spread/pallas_call | solution.py:170
  1.7 8.0 %all-to-all-start = ((f32[16,64,128]{2,1,0:T(8,128)}), f32[16,64,128]{2,1,0:T(8,128)S(1)}, u32[]{:S(2)}, u32[]{:S(2)}) async-start(f32[16,64,128]{2,1,0:T(8,128)} %spread.1), calls=%async_computation | async-start | bytes 1048576 | tf_op jit(solution)/shard_map/all_to_all | solution.py:399
  9.7 0.0 copy-start.3
  9.7 7.4 %transform.1.own_ref = bf16[64,128,128]{2,1,0:T(8,128)(2,1)S(1)} custom-call(bf16[2,64,64,128]{3,2,1,0:T(8,128)(2,1)} %bitcast.13, bf16[64,1024]{1,0:T(8,128)(2,1)} %constant.66.clone.waves_hbm, bf16[64,128,128]{2,1,0:T(8,128)(2,1)} %constant.67.clone.second_hbm), custom_call_target="tpu_custom_call" | custom-call | flops 12000000000 | bytes 8000000 | tf_op jit(solution)/shard_map/transform/pallas_call | solution.py:185
  17.1 4.1 %all-to-all-done = f32[16,64,128]{2,1,0:T(8,128)S(1)} async-done(((f32[16,64,128]{2,1,0:T(8,128)}), f32[16,64,128]{2,1,0:T(8,128)S(1)}, u32[]{:S(2)}, u32[]{:S(2)}) %all-to-all-start) | async-done | bytes 524320 | tf_op jit(solution)/shard_map/all_to_all | solution.py:399
  21.2 0.2 select_reduce_fusion.3
  21.4 0.6 %fusion.7 = (s32[]{:T(128)}, s32[64]{0:T(128)S(1)}, pred[64]{0:T(512)(128)(4,1)S(1)}, s32[64]{0:T(128)S(1)}, s32[64]{0:T(128)S(1)}) fusion(s32[64]{0:T(128)S(1)} %copy-done.2, s32[]{:T(128)S(6)} %axis_index.51, s32[64]{0:T(128)S(1)} %copy-done.3, s32[64]{0:T(128)S(1)} %select_reduce_fusion.3), kind=kLoop, calls=%fused_computation.30 | loop fusion | flops 2751 | bytes 1608 | tf_op jit(solution)/shard_map/reduce_sum | solution.py:417
  22.0 0.1 select_reduce_fusion.2
  22.2 0.1 select_reduce_fusion.1
  22.3 0.1 select_reduce_fusion
  22.4 0.7 %concatenate.7.plan = s32[384]{0:T(512)S(1)} concatenate(s32[256]{0:T(256)S(1)} %select_reduce_fusion, s32[64]{0:T(128)S(1)} %select_reduce_fusion.1, s32[1]{0:T(128)} %bitcast.2, s32[1]{0:T(128)} %bitcast.3, s32[1]{0:T(128)} %bitcast.4, s32[61]{0:T(128)S(1)} %broadcast_in_dim.66), dimensions={0} | concatenate | bytes 3072 | tf_op jit(solution)/shard_map/concatenate | solution.py:418
  23.1 2.4 %collective-permute-done.other_hbm = bf16[64,128,128]{2,1,0:T(8,128)(2,1)} collective-permute-done((bf16[64,128,128]{2,1,0:T(8,128)(2,1)S(1)}, bf16[64,128,128]{2,1,0:T(8,128)(2,1)}, u32[]{:S(2)}, u32[]{:S(2)}) %collective-permute-start) | collective-permute-done | bytes 2097184 | tf_op jit(solution)/shard_map/ppermute | solution.py:425
  25.5 9.9 %degrid.1 = bf16[16,64,128]{2,1,0:T(8,128)(2,1)} custom-call(s32[384]{0:T(512)S(1)} %concatenate.7.plan, bf16[64,128,128]{2,1,0:T(8,128)(2,1)S(1)} %transform.1.own_ref, bf16[64,128,128]{2,1,0:T(8,128)(2,1)} %collective-permute-done.other_hbm, f32[16,8,8,128]{3,2,1,0:T(8,128)S(1)} %bitcast.10), custom_call_target="tpu_custom_call" | custom-call | flops 12000000000 | bytes 8000000 | tf_op jit(solution)/shard_map/degrid/pallas_call | solution.py:302
  35.4 3.5 %all-to-all-start.1 = ((bf16[16,64,128]{2,1,0:T(8,128)(2,1)}), bf16[16,64,128]{2,1,0:T(8,128)(2,1)S(1)}, u32[]{:S(2)}, u32[]{:S(2)}) async-start(bf16[16,64,128]{2,1,0:T(8,128)(2,1)} %degrid.1), calls=%async_computation.1 | async-start | bytes 524288 | tf_op jit(solution)/shard_map/all_to_all | solution.py:427
  39.0 0.2 select_reduce_fusion.4
  39.2 8.6 %all-to-all-done.1 = bf16[16,64,128]{2,1,0:T(8,128)(2,1)S(1)} async-done(((bf16[16,64,128]{2,1,0:T(8,128)(2,1)}), bf16[16,64,128]{2,1,0:T(8,128)(2,1)S(1)}, u32[]{:S(2)}, u32[]{:S(2)}) %all-to-all-start.1) | async-done | bytes 262176 | tf_op jit(solution)/shard_map/all_to_all | solution.py:427
  47.8 1.6 %collective-permute-start.1 = (f32[64,128]{1,0:T(8,128)S(1)}, f32[64,128]{1,0:T(8,128)S(1)}, u32[]{:S(2)}, u32[]{:S(2)}) collective-permute-start(f32[64,128]{1,0:T(8,128)S(1)} %convert_reduce_fusion.own_ref), channel_id=1, source_target_pairs={{0,1},{1,2},{2,3},{3,0},{4,5},{5,6},{6,7},{7,4},{8,9},{9,10},{10,1... | collective-permute-start | bytes 98312 | tf_op jit(solution)/shard_map/ppermute | solution.py:431
  49.4 2.9 %collective-permute-start.2 = (f32[64,128]{1,0:T(8,128)S(1)}, f32[64,128]{1,0:T(8,128)S(1)}, u32[]{:S(2)}, u32[]{:S(2)}) collective-permute-start(f32[64,128]{1,0:T(8,128)S(1)} %convert_reduce_fusion.own_ref), channel_id=1, source_target_pairs={{0,2},{1,3},{2,0},{3,1},{4,6},{5,7},{6,4},{7,5},{8,10},{9,11},{10,... | collective-permute-start | bytes 98312 | tf_op jit(solution)/shard_map/ppermute | solution.py:431
  52.3 1.3 %collective-permute-start.3 = (f32[64,128]{1,0:T(8,128)S(1)}, f32[64,128]{1,0:T(8,128)S(1)}, u32[]{:S(2)}, u32[]{:S(2)}) collective-permute-start(f32[64,128]{1,0:T(8,128)S(1)} %convert_reduce_fusion.own_ref), channel_id=1, source_target_pairs={{0,3},{1,0},{2,1},{3,2},{4,7},{5,4},{6,5},{7,6},{8,11},{9,8},{10,9... | collective-permute-start | bytes 98312 | tf_op jit(solution)/shard_map/ppermute | solution.py:431
  53.7 0.1 pad_add_fusion.place
  53.7 0.8 %jones.1 = (f32[4,4,2,8,128]{4,3,2,1,0:T(8,128)S(1)}, f32[4,8,128]{2,1,0:T(8,128)S(1)}) custom-call(s32[5]{0:T(128)S(1)} %pad_add_fusion.place, s32[4,2,8,128]{3,2,1,0:T(8,128)S(1)} %bitcast.11, f32[8,512]{1,0:T(8,128)S(1)} %copy-done), custom_call_target="tpu_custom_call" | custom-call | tf_op jit(solution)/shard_map/jones/pallas_call | solution.py:355
  54.5 0.3 collective-permute-done.2.two_ref
  54.8 1.4 %collective-permute-done.3.three_ref = f32[64,128]{1,0:T(8,128)S(1)} collective-permute-done((f32[64,128]{1,0:T(8,128)S(1)}, f32[64,128]{1,0:T(8,128)S(1)}, u32[]{:S(2)}, u32[]{:S(2)}) %collective-permute-start.3) | collective-permute-done | bytes 32800 | tf_op jit(solution)/shard_map/ppermute | solution.py:431
  56.2 0.6 %correct.1 = f32[1,2,4,8,128]{4,3,2,1,0:T(8,128)} custom-call(f32[4,4,2,8,128]{4,3,2,1,0:T(8,128)S(1)} %get-tuple-element.9.jones_ref, f32[4,8,128]{2,1,0:T(8,128)S(1)} %get-tuple-element.10.mask_ref, f32[64,128]{1,0:T(8,128)S(1)} %convert_reduce_fusion.own_ref, f32[64,128]{1,0:T(8,128)S(1)} %collective-permute-done.1.one_ref, ...), custom_call_target="tpu_custom_call" | custom-call | tf_op jit(solution)/shard_map/correct/pallas_call | solution.py:384
  (13 shorter events, 0.1 us)
Async XLA Ops:
  1.7 19.5 %all-to-all-start = ((f32[16,64,128]{2,1,0:T(8,128)}), f32[16,64,128]{2,1,0:T(8,128)S(1)}, u32[]{:S(2)}, u32[]{:S(2)}) async-start(f32[16,64,128]{2,1,0:T(8,128)} %spread.1), calls=%async_computation | async-start | bytes 1048576 | tf_op jit(solution)/shard_map/all_to_all | solution.py:399
  9.7 11.5 %copy-start.3 = (s32[64]{0:T(128)S(1)}, s32[64]{0:T(128)}, u32[]{:S(2)}) copy-start(s32[64]{0:T(128)} %param.9) | copy-start | bytes 772
  9.7 11.7 %copy-start.2 = (s32[64]{0:T(128)S(1)}, s32[64]{0:T(128)}, u32[]{:S(2)}) copy-start(s32[64]{0:T(128)} %param.10) | copy-start | bytes 772
  21.2 4.3 %collective-permute-start = (bf16[64,128,128]{2,1,0:T(8,128)(2,1)S(1)}, bf16[64,128,128]{2,1,0:T(8,128)(2,1)}, u32[]{:S(2)}, u32[]{:S(2)}) collective-permute-start(bf16[64,128,128]{2,1,0:T(8,128)(2,1)S(1)} %transform.1.own_ref), channel_id=1, source_target_pairs={{0,4},{4,0},{1,5},{5,1},{2,6},{6,2},{3,7},{7,3},{8,12},{12,8},{9,1... | collective-permute-start | bytes 6291464 | tf_op jit(solution)/shard_map/ppermute | solution.py:425
  23.1 30.6 %copy-start.1 = (s32[4,8,2,128]{3,2,1,0:T(2,128)S(1)}, s32[4,8,2,128]{3,2,1,0:T(2,128)}, u32[]{:S(2)}) copy-start(s32[4,8,2,128]{3,2,1,0:T(2,128)} %param.12) | copy-start | bytes 98308
  23.1 30.6 %copy-start = (f32[8,512]{1,0:T(8,128)S(1)}, f32[8,512]{1,0:T(8,128)}, u32[]{:S(2)}) copy-start(f32[8,512]{1,0:T(8,128)} %table_ref.1) | copy-start | bytes 49156
  35.4 12.3 %all-to-all-start.1 = ((bf16[16,64,128]{2,1,0:T(8,128)(2,1)}), bf16[16,64,128]{2,1,0:T(8,128)(2,1)S(1)}, u32[]{:S(2)}, u32[]{:S(2)}) async-start(bf16[16,64,128]{2,1,0:T(8,128)(2,1)} %degrid.1), calls=%async_computation.1 | async-start | bytes 524288 | tf_op jit(solution)/shard_map/all_to_all | solution.py:427
  47.8 6.8 %collective-permute-start.1 = (f32[64,128]{1,0:T(8,128)S(1)}, f32[64,128]{1,0:T(8,128)S(1)}, u32[]{:S(2)}, u32[]{:S(2)}) collective-permute-start(f32[64,128]{1,0:T(8,128)S(1)} %convert_reduce_fusion.own_ref), channel_id=1, source_target_pairs={{0,1},{1,2},{2,3},{3,0},{4,5},{5,6},{6,7},{7,4},{8,9},{9,10},{10,1... | collective-permute-start | bytes 98312 | tf_op jit(solution)/shard_map/ppermute | solution.py:431
  49.4 5.4 %collective-permute-start.2 = (f32[64,128]{1,0:T(8,128)S(1)}, f32[64,128]{1,0:T(8,128)S(1)}, u32[]{:S(2)}, u32[]{:S(2)}) collective-permute-start(f32[64,128]{1,0:T(8,128)S(1)} %convert_reduce_fusion.own_ref), channel_id=1, source_target_pairs={{0,2},{1,3},{2,0},{3,1},{4,6},{5,7},{6,4},{7,5},{8,10},{9,11},{10,... | collective-permute-start | bytes 98312 | tf_op jit(solution)/shard_map/ppermute | solution.py:431
  52.3 3.9 %collective-permute-start.3 = (f32[64,128]{1,0:T(8,128)S(1)}, f32[64,128]{1,0:T(8,128)S(1)}, u32[]{:S(2)}, u32[]{:S(2)}) collective-permute-start(f32[64,128]{1,0:T(8,128)S(1)} %convert_reduce_fusion.own_ref), channel_id=1, source_target_pairs={{0,3},{1,0},{2,1},{3,2},{4,7},{5,4},{6,5},{7,6},{8,11},{9,8},{10,9... | collective-permute-start | bytes 98312 | tf_op jit(solution)/shard_map/ppermute | solution.py:431

commit v7 on v6

--- a/solution.py
+++ b/solution.py
@@ -206,13 +206,16 @@
     other_copy = pltpu.make_async_copy(other_hbm, other_ref, sem)
     other_copy.start()
 
-    @pl.loop(0, 16)
-    def _(o):
-        cos, sin = turns_to_phase(coords_ref[o] * (8.0 / SG))
-        slots = pl.ds(o * CAP, CAP)
-        for axis in range(2):
-            steps[2 * axis, slots] = cos[CAP * axis : CAP * axis + CAP]
-            steps[2 * axis + 1, slots] = sin[CAP * axis : CAP * axis + CAP]
+    rounds = (plan[TOTAL_AT + 3] + 3) >> 2
+
+    @pl.loop(0, rounds)
+    def _(step):
+        for j in range(4):
+            g = plan[UNITS + 4 * step + j]
+            for axis in range(2):
+                cos, sin = turns_to_phase(coords_ref[g >> 2, CAP * axis + (g & 3)] * (8.0 / SG))
+                steps[2 * axis, g] = cos
+                steps[2 * axis + 1, g] = sin
 
     other_copy.wait()
     cells = (lax.broadcasted_iota(jnp.int32, (8, VB), 0).astype(F32) + 0.5) * (1.0 / SG)
@@ -276,10 +279,11 @@
     centre_own = (W * (first_facet % R)).astype(F32) + (W - 0.5 - SG // 2)
     centre_other = (W * (other_facet % R)).astype(F32) + (W - 0.5 - SG // 2)
 
-    @pl.loop(0, 16)
-    def _(o):
-        for c in range(CAP):
-            g = o * CAP + c
+    @pl.loop(0, rounds)
+    def _(step):
+        for j in range(4):
+            g = plan[UNITS + 4 * step + j]
+            o, c = g >> 2, g & 3
             x, y = coords_ref[o, c], coords_ref[o, CAP + c]
             real = imag = jnp.zeros((MAXB, VB), F32)
             for q, centre_y in enumerate((centre_own, centre_other)):
@@ -293,7 +297,7 @@
                 imag = imag + (cos * total_imag - sin * total_real)
             scale = 1.0 / (math.sqrt(FH) * SG)
             value = (jnp.concatenate([real, imag], axis=0) * scale).astype(BF16)
-            out_ref[o, 2 * MAXB * c : 2 * MAXB * (c + 1), :] = value
+            out_ref[o, pl.ds(pl.multiple_of(2 * MAXB * c, 2 * MAXB), 2 * MAXB), :] = value
 
 
 def degrid(plan, own, other, coords, together=TOGETHER):
@@ -412,10 +416,11 @@
     words = (slot * S + index)[None, :] * 4 + offset
     units = jnp.sum(jnp.where((offset >= 0) & (offset < pairs[None, :]), words, 0), axis=1)
     slots = jnp.arange(16 * CAP, dtype=jnp.int32)[:, None]
-    limits = jnp.sum(jnp.where((slots == slot[None, :]) & mine[None, :], counts[None, :], 0), axis=1)
+    place = jnp.sum(jnp.where(before & mine[None, :], 1, 0), axis=1)
+    own_slots = jnp.sum(jnp.where((slots == place[None, :]) & mine[None, :], slot[None, :], 0), axis=1)
     facet = 2 * (chip * 2 + core)
-    extra = jnp.stack([jnp.sum(pairs), facet, facet + 2 - 4 * core])
-    plan = jnp.concatenate([units, limits, extra, jnp.zeros((61,), jnp.int32)])
+    extra = jnp.stack([jnp.sum(pairs), facet, facet + 2 - 4 * core, jnp.sum(jnp.where(mine, 1, 0))])
+    plan = jnp.concatenate([units, own_slots, extra, jnp.zeros((60,), jnp.int32)])
     own_limits = jnp.sum(
         jnp.where((slot[None, :] == chip * CAP + jnp.arange(CAP)[:, None]) & mine[None, :], counts[None, :], 0), axis=1
     )

time: 56.7 us -> 57 us (level)
  Pallas kernels: 20.4 us -> 19.1 us
  other arithmetic: 1.46 us -> 2.23 us
  local copies, waits for them, and re-layouts: 0.75 us -> 1.37 us
    ppermute x1, waiting for transfers between devices: 2.37 us -> 0.99 us  [on_device(): other = lax.ppermute(sent, 'core', [(0, 1), (1, 0)])]
    pallas_call x1, Pallas kernels: 9.9 us -> 8.62 us  [degrid(): pl.pallas_call(functools.partial(degrid_kernel, together), out_shape=jax....]
    all_to_all x1, waiting for transfers between devices: 8.55 us -> 9.59 us  [on_device(): lax.all_to_all(parts, ('z', 'x'), split_axis=0, concat_axis=0, tiled=True)]
    reduce_sum x2 -> x4, other arithmetic: 0.76 us -> 1.53 us  [the longest x1 0.65 us: on_device(): jnp.sum(jnp.where(mine, 1, 0))]
    concatenate x1, local copies, waits for them, and re-layouts: 0.73 us -> 1.34 us  [on_device(): jnp.concatenate([units, own_slots, extra, jnp.zeros((60,), jnp.int32)])]
  transfers between devices with their start and end apart: 6 -> 6, of which waited for: 5 -> 5; matrix products, arithmetic and copies ran while one was open for 4% -> 6% of each run, Pallas kernels for 14% -> 14%
where the time goes in v7:
time: 57 us; the launch traced here: 56.6 us
  Pallas kernels  19.1 us (34%)
  starting transfers between devices  17.4 us (31%)
  waiting for transfers between devices  16.4 us (29%)
  other arithmetic  2.23 us (4%)
  local copies, waits for them, and re-layouts  1.37 us (2%)
    all_to_all x1, waiting for transfers between devices, on_device(): lax.all_to_all(parts, ('z', 'x'), split_axis=0, concat_axis=0, tiled=True)  9.59 us
    pallas_call x1, Pallas kernels, degrid(): pl.pallas_call(functools.partial(degrid_kernel, together), out_shape=jax....  8.62 us
    all_to_all x1, starting transfers between devices, on_device(): lax.all_to_all(spread(coords.reshape(2 * CAP * MAXB, VB)), ('z', 'x'), sp...  7.97 us
    pallas_call x1, Pallas kernels, transform(): pl.pallas_call(transform_kernel, out_shape=jax.ShapeDtypeStruct((S, 2 * W...  7.39 us
    ppermute x3, starting transfers between devices, on_device(): lax.ppermute(visible, 'pol', [(i, (i + k) % 4) for i in range(4)])  5.91 us
    all_to_all x1, waiting for transfers between devices, on_device(): lax.all_to_all(spread(coords.reshape(2 * CAP * MAXB, VB)), ('z', 'x'), sp...  4.11 us
    all_to_all x1, starting transfers between devices, on_device(): lax.all_to_all(parts, ('z', 'x'), split_axis=0, concat_axis=0, tiled=True)  3.54 us
    pallas_call x1, Pallas kernels, spread(): pl.pallas_call(spread_kernel, out_shape=jax.ShapeDtypeStruct((16,) + coor...  1.69 us
  transfers between devices with their start and end apart: 6, of which 5 were waited for; matrix products, arithmetic and copies ran while one was open for 6% of the time, Pallas kernels for 14%

profile of v7, /device:TPU:0, one launch (start us, length us, event | category | flops | bytes accessed | tf_op | source)
XLA Modules:
  0.0 56.6 jit_solution(10659695391252790188)
XLA Ops:
  0.0 1.7 %spread.1 = f32[16,64,128]{2,1,0:T(8,128)} custom-call(f32[64,128]{1,0:T(8,128)} %bitcast.13), custom_call_target="tpu_custom_call" | custom-call | tf_op jit(solution)/shard_map/spread/pallas_call | solution.py:170
  1.7 8.0 %all-to-all-start = ((f32[16,64,128]{2,1,0:T(8,128)}), f32[16,64,128]{2,1,0:T(8,128)S(1)}, u32[]{:S(2)}, u32[]{:S(2)}) async-start(f32[16,64,128]{2,1,0:T(8,128)} %spread.1), calls=%async_computation | async-start | bytes 1048576 | tf_op jit(solution)/shard_map/all_to_all | solution.py:403
  9.7 7.4 %transform.1.own_ref = bf16[64,128,128]{2,1,0:T(8,128)(2,1)S(1)} custom-call(bf16[2,64,64,128]{3,2,1,0:T(8,128)(2,1)} %bitcast.14, bf16[64,1024]{1,0:T(8,128)(2,1)} %constant.66.clone.waves_hbm, bf16[64,128,128]{2,1,0:T(8,128)(2,1)} %constant.67.clone.second_hbm), custom_call_target="tpu_custom_call" | custom-call | flops 12000000000 | bytes 8000000 | tf_op jit(solution)/shard_map/transform/pallas_call | solution.py:185
  17.1 4.1 %all-to-all-done = f32[16,64,128]{2,1,0:T(8,128)S(1)} async-done(((f32[16,64,128]{2,1,0:T(8,128)}), f32[16,64,128]{2,1,0:T(8,128)S(1)}, u32[]{:S(2)}, u32[]{:S(2)}) %all-to-all-start) | async-done | bytes 524320 | tf_op jit(solution)/shard_map/all_to_all | solution.py:403
  21.2 0.2 select_reduce_fusion.4
  21.4 0.7 %select_reduce_fusion.6 = (s32[]{:T(128)}, pred[64]{0:T(512)(128)(4,1)S(1)}, s32[64]{0:T(128)S(1)}, s32[64]{0:T(128)S(1)}) fusion(s32[]{:T(128)S(6)} %axis_index.51, s32[64]{0:T(128)S(1)} %copy-done.3, s32[64]{0:T(128)S(1)} %select_reduce_fusion.4), kind=kLoop, calls=%fused_computation.28 | loop fusion | flops 1727 | bytes 1096 | tf_op jit(solution)/shard_map/reduce_sum | solution.py:422
  22.0 0.6 %fusion.9 = (s32[]{:T(128)}, s32[64]{0:T(128)S(1)}) fusion(pred[64]{0:T(512)(128)(4,1)S(1)} %get-tuple-element.14, s32[64]{0:T(128)S(1)} %copy-done.2), kind=kLoop, calls=%fused_computation.33 | loop fusion | flops 1151 | bytes 580 | tf_op jit(solution)/shard_map/reduce_sum | solution.py:422
  22.7 0.1 select_reduce_fusion.3
  22.8 0.1 select_reduce_fusion.2
  22.9 0.1 select_reduce_fusion.1
  23.0 0.1 select_reduce_fusion
  23.2 1.3 %concatenate.7.plan = s32[384]{0:T(512)S(1)} concatenate(s32[256]{0:T(256)S(1)} %select_reduce_fusion, s32[64]{0:T(128)S(1)} %select_reduce_fusion.1, s32[1]{0:T(128)} %bitcast.2, s32[1]{0:T(128)} %bitcast.3, s32[1]{0:T(128)} %bitcast.4, s32[1]{0:T(128)} %bitcast.5, s32[60]{0:T(128)S(1)} %broadcast_in_dim.73), dimensions={0} | concatenate | bytes 3072 | tf_op jit(solution)/shard_map/concatenate | solution.py:423
  24.5 1.0 %collective-permute-done.other_hbm = bf16[64,128,128]{2,1,0:T(8,128)(2,1)} collective-permute-done((bf16[64,128,128]{2,1,0:T(8,128)(2,1)S(1)}, bf16[64,128,128]{2,1,0:T(8,128)(2,1)}, u32[]{:S(2)}, u32[]{:S(2)}) %collective-permute-start) | collective-permute-done | bytes 2097184 | tf_op jit(solution)/shard_map/ppermute | solution.py:430
  25.5 8.6 %degrid.1 = bf16[16,64,128]{2,1,0:T(8,128)(2,1)} custom-call(s32[384]{0:T(512)S(1)} %concatenate.7.plan, bf16[64,128,128]{2,1,0:T(8,128)(2,1)S(1)} %transform.1.own_ref, bf16[64,128,128]{2,1,0:T(8,128)(2,1)} %collective-permute-done.other_hbm, f32[16,8,8,128]{3,2,1,0:T(8,128)S(1)} %bitcast.11), custom_call_target="tpu_custom_call" | custom-call | flops 12000000000 | bytes 8000000 | tf_op jit(solution)/shard_map/degrid/pallas_call | solution.py:306
  34.1 3.5 %all-to-all-start.1 = ((bf16[16,64,128]{2,1,0:T(8,128)(2,1)}), bf16[16,64,128]{2,1,0:T(8,128)(2,1)S(1)}, u32[]{:S(2)}, u32[]{:S(2)}) async-start(bf16[16,64,128]{2,1,0:T(8,128)(2,1)} %degrid.1), calls=%async_computation.1 | async-start | bytes 524288 | tf_op jit(solution)/shard_map/all_to_all | solution.py:432
  37.7 0.2 select_reduce_fusion.5
  37.9 9.6 %all-to-all-done.1 = bf16[16,64,128]{2,1,0:T(8,128)(2,1)S(1)} async-done(((bf16[16,64,128]{2,1,0:T(8,128)(2,1)}), bf16[16,64,128]{2,1,0:T(8,128)(2,1)S(1)}, u32[]{:S(2)}, u32[]{:S(2)}) %all-to-all-start.1) | async-done | bytes 262176 | tf_op jit(solution)/shard_map/all_to_all | solution.py:432
  47.5 1.6 %collective-permute-start.1 = (f32[64,128]{1,0:T(8,128)S(1)}, f32[64,128]{1,0:T(8,128)S(1)}, u32[]{:S(2)}, u32[]{:S(2)}) collective-permute-start(f32[64,128]{1,0:T(8,128)S(1)} %convert_reduce_fusion.own_ref), channel_id=1, source_target_pairs={{0,1},{1,2},{2,3},{3,0},{4,5},{5,6},{6,7},{7,4},{8,9},{9,10},{10,1... | collective-permute-start | bytes 98312 | tf_op jit(solution)/shard_map/ppermute | solution.py:436
  49.2 2.9 %collective-permute-start.2 = (f32[64,128]{1,0:T(8,128)S(1)}, f32[64,128]{1,0:T(8,128)S(1)}, u32[]{:S(2)}, u32[]{:S(2)}) collective-permute-start(f32[64,128]{1,0:T(8,128)S(1)} %convert_reduce_fusion.own_ref), channel_id=1, source_target_pairs={{0,2},{1,3},{2,0},{3,1},{4,6},{5,7},{6,4},{7,5},{8,10},{9,11},{10,... | collective-permute-start | bytes 98312 | tf_op jit(solution)/shard_map/ppermute | solution.py:436
  52.1 1.3 %collective-permute-start.3 = (f32[64,128]{1,0:T(8,128)S(1)}, f32[64,128]{1,0:T(8,128)S(1)}, u32[]{:S(2)}, u32[]{:S(2)}) collective-permute-start(f32[64,128]{1,0:T(8,128)S(1)} %convert_reduce_fusion.own_ref), channel_id=1, source_target_pairs={{0,3},{1,0},{2,1},{3,2},{4,7},{5,4},{6,5},{7,6},{8,11},{9,8},{10,9... | collective-permute-start | bytes 98312 | tf_op jit(solution)/shard_map/ppermute | solution.py:436
  53.5 0.8 %jones.1 = (f32[4,4,2,8,128]{4,3,2,1,0:T(8,128)S(1)}, f32[4,8,128]{2,1,0:T(8,128)S(1)}) custom-call(s32[5]{0:T(128)S(1)} %pad_add_fusion.place, s32[4,2,8,128]{3,2,1,0:T(8,128)S(1)} %bitcast.12, f32[8,512]{1,0:T(8,128)S(1)} %copy-done), custom_call_target="tpu_custom_call" | custom-call | tf_op jit(solution)/shard_map/jones/pallas_call | solution.py:359
  54.3 0.3 collective-permute-done.2.two_ref
  54.6 1.4 %collective-permute-done.3.three_ref = f32[64,128]{1,0:T(8,128)S(1)} collective-permute-done((f32[64,128]{1,0:T(8,128)S(1)}, f32[64,128]{1,0:T(8,128)S(1)}, u32[]{:S(2)}, u32[]{:S(2)}) %collective-permute-start.3) | collective-permute-done | bytes 32800 | tf_op jit(solution)/shard_map/ppermute | solution.py:436
  56.0 0.6 %correct.1 = f32[1,2,4,8,128]{4,3,2,1,0:T(8,128)} custom-call(f32[4,4,2,8,128]{4,3,2,1,0:T(8,128)S(1)} %get-tuple-element.9.jones_ref, f32[4,8,128]{2,1,0:T(8,128)S(1)} %get-tuple-element.10.mask_ref, f32[64,128]{1,0:T(8,128)S(1)} %convert_reduce_fusion.own_ref, f32[64,128]{1,0:T(8,128)S(1)} %collective-permute-done.1.one_ref, ...), custom_call_target="tpu_custom_call" | custom-call | tf_op jit(solution)/shard_map/correct/pallas_call | solution.py:388
  (15 shorter events, 0.2 us)
Async XLA Ops:
  1.7 19.5 %all-to-all-start = ((f32[16,64,128]{2,1,0:T(8,128)}), f32[16,64,128]{2,1,0:T(8,128)S(1)}, u32[]{:S(2)}, u32[]{:S(2)}) async-start(f32[16,64,128]{2,1,0:T(8,128)} %spread.1), calls=%async_computation | async-start | bytes 1048576 | tf_op jit(solution)/shard_map/all_to_all | solution.py:403
  9.7 11.5 %copy-start.3 = (s32[64]{0:T(128)S(1)}, s32[64]{0:T(128)}, u32[]{:S(2)}) copy-start(s32[64]{0:T(128)} %param.9) | copy-start | bytes 772
  9.7 12.4 %copy-start.2 = (s32[64]{0:T(128)S(1)}, s32[64]{0:T(128)}, u32[]{:S(2)}) copy-start(s32[64]{0:T(128)} %param.10) | copy-start | bytes 772
  21.2 4.3 %collective-permute-start = (bf16[64,128,128]{2,1,0:T(8,128)(2,1)S(1)}, bf16[64,128,128]{2,1,0:T(8,128)(2,1)}, u32[]{:S(2)}, u32[]{:S(2)}) collective-permute-start(bf16[64,128,128]{2,1,0:T(8,128)(2,1)S(1)} %transform.1.own_ref), channel_id=1, source_target_pairs={{0,4},{4,0},{1,5},{5,1},{2,6},{6,2},{3,7},{7,3},{8,12},{12,8},{9,1... | collective-permute-start | bytes 6291464 | tf_op jit(solution)/shard_map/ppermute | solution.py:430
  24.5 29.0 %copy-start.1 = (s32[4,8,2,128]{3,2,1,0:T(2,128)S(1)}, s32[4,8,2,128]{3,2,1,0:T(2,128)}, u32[]{:S(2)}) copy-start(s32[4,8,2,128]{3,2,1,0:T(2,128)} %param.12) | copy-start | bytes 98308
  24.5 29.0 %copy-start = (f32[8,512]{1,0:T(8,128)S(1)}, f32[8,512]{1,0:T(8,128)}, u32[]{:S(2)}) copy-start(f32[8,512]{1,0:T(8,128)} %table_ref.1) | copy-start | bytes 49156
  34.1 13.3 %all-to-all-start.1 = ((bf16[16,64,128]{2,1,0:T(8,128)(2,1)}), bf16[16,64,128]{2,1,0:T(8,128)(2,1)S(1)}, u32[]{:S(2)}, u32[]{:S(2)}) async-start(bf16[16,64,128]{2,1,0:T(8,128)(2,1)} %degrid.1), calls=%async_computation.1 | async-start | bytes 524288 | tf_op jit(solution)/shard_map/all_to_all | solution.py:432
  47.5 6.8 %collective-permute-start.1 = (f32[64,128]{1,0:T(8,128)S(1)}, f32[64,128]{1,0:T(8,128)S(1)}, u32[]{:S(2)}, u32[]{:S(2)}) collective-permute-start(f32[64,128]{1,0:T(8,128)S(1)} %convert_reduce_fusion.own_ref), channel_id=1, source_target_pairs={{0,1},{1,2},{2,3},{3,0},{4,5},{5,6},{6,7},{7,4},{8,9},{9,10},{10,1... | collective-permute-start | bytes 98312 | tf_op jit(solution)/shard_map/ppermute | solution.py:436
  49.2 5.4 %collective-permute-start.2 = (f32[64,128]{1,0:T(8,128)S(1)}, f32[64,128]{1,0:T(8,128)S(1)}, u32[]{:S(2)}, u32[]{:S(2)}) collective-permute-start(f32[64,128]{1,0:T(8,128)S(1)} %convert_reduce_fusion.own_ref), channel_id=1, source_target_pairs={{0,2},{1,3},{2,0},{3,1},{4,6},{5,7},{6,4},{7,5},{8,10},{9,11},{10,... | collective-permute-start | bytes 98312 | tf_op jit(solution)/shard_map/ppermute | solution.py:436
  52.1 3.9 %collective-permute-start.3 = (f32[64,128]{1,0:T(8,128)S(1)}, f32[64,128]{1,0:T(8,128)S(1)}, u32[]{:S(2)}, u32[]{:S(2)}) collective-permute-start(f32[64,128]{1,0:T(8,128)S(1)} %convert_reduce_fusion.own_ref), channel_id=1, source_target_pairs={{0,3},{1,0},{2,1},{3,2},{4,7},{5,4},{6,5},{7,6},{8,11},{9,8},{10,9... | collective-permute-start | bytes 98312 | tf_op jit(solution)/shard_map/ppermute | solution.py:436

commit v8 on v7

--- a/solution.py
+++ b/solution.py
@@ -70,7 +70,8 @@
 
 
 def transform_kernel(
-    facets_hbm, waves_hbm, second_hbm, out_ref, facets_ref, waves_ref, second_ref, first_ref, sections, mixed, sems
+    facets_hbm, waves_hbm, second_hbm, coords_hbm, out_ref, spread_hbm,
+    facets_ref, waves_ref, second_ref, coords_ref, first_ref, sections, mixed, sems, spread_sems,
 ):
     half = W // 2
     wide = W * GROUP
@@ -84,7 +85,9 @@
         for f in range(2)
         for i, at in enumerate(quarters)
     ]
-    for copy in [waves_copy] + strip_copies + second_copies:
+    coords_copy = pltpu.make_async_copy(coords_hbm, coords_ref, sems.at[13])
+    spread_copies = [pltpu.make_async_copy(coords_ref, spread_hbm.at[o], spread_sems.at[o]) for o in range(16)]
+    for copy in [coords_copy, waves_copy] + strip_copies + second_copies:
         copy.start()
     row = lax.broadcasted_iota(jnp.int32, (2 * W, 2 * W), 0)
     lane = lax.broadcasted_iota(jnp.int32, (2 * W, 2 * W), 1)
@@ -101,6 +104,9 @@
         spread_waves = jnp.dot(pick, waves_ref[...], preferred_element_type=F32)
         first_ref[rows, :] = jnp.where(same, spread_waves, 0.0).astype(BF16)
 
+    coords_copy.wait()
+    for copy in spread_copies:
+        copy.start()
     for copy in strip_copies:
         copy.wait()
     for h in range(W // GROUP):
@@ -157,49 +163,40 @@
                 rows = slice(half * kind + i, half * kind + i + 16)
                 out_ref[at, rows, :] = jnp.concatenate(halves, axis=1).astype(BF16)
 
-
-def spread_kernel(coords_ref, out_hbm, sems):
-    copies = [pltpu.make_async_copy(coords_ref, out_hbm.at[o], sems.at[o]) for o in range(16)]
-    for copy in copies:
-        copy.start()
-    for copy in copies:
+    for copy in spread_copies:
         copy.wait()
-
-
-def spread(coords):
-    return pl.pallas_call(
-        spread_kernel,
-        out_shape=jax.ShapeDtypeStruct((16,) + coords.shape, F32),
-        in_specs=[pl.BlockSpec(memory_space=pltpu.VMEM)],
-        out_specs=pl.BlockSpec(memory_space=pltpu.HBM),
-        scratch_shapes=[pltpu.SemaphoreType.DMA((16,))],
-        name="spread",
-    )(coords)
 
 
 def in_hbm(array):
     return pltpu.with_memory_space_constraint(array, pltpu.HBM)
 
 
-def transform(strips):
+def transform(strips, coords):
+    vmem = pl.BlockSpec(memory_space=pltpu.VMEM)
+    hbm = pl.BlockSpec(memory_space=pltpu.HBM)
     return pl.pallas_call(
         transform_kernel,
-        out_shape=jax.ShapeDtypeStruct((S, 2 * W, 2 * W), BF16),
-        in_specs=[pl.BlockSpec(memory_space=pltpu.HBM)] * 3,
-        out_specs=pl.BlockSpec(memory_space=pltpu.VMEM),
+        out_shape=[
+            jax.ShapeDtypeStruct((S, 2 * W, 2 * W), BF16),
+            jax.ShapeDtypeStruct((16,) + coords.shape, F32),
+        ],
+        in_specs=[hbm] * 4,
+        out_specs=[vmem, hbm],
         scratch_shapes=[
             pltpu.VMEM((2, W, W, 2 * W), BF16),
             pltpu.VMEM((W, W * GROUP), BF16),
             pltpu.VMEM((W, 2 * W, 2 * W), BF16),
+            pltpu.VMEM(coords.shape, F32),
             pltpu.VMEM((W * GROUP, W * GROUP), BF16),
             pltpu.VMEM((2, W, W, 2 * W), BF16),
             pltpu.VMEM((4, W // 2, S, 2 * W), F32),
-            pltpu.SemaphoreType.DMA((13,)),
+            pltpu.SemaphoreType.DMA((14,)),
+            pltpu.SemaphoreType.DMA((16,)),
         ],
         compiler_params=pltpu.CompilerParams(vmem_limit_bytes=VMEM_LIMIT),
         cost_estimate=pl.CostEstimate(flops=12_000_000_000, bytes_accessed=8_000_000, transcendentals=0),
         name="transform",
-    )(*(in_hbm(x) for x in (strips.reshape(2, W, W, 2 * W), jnp.asarray(first_table()), jnp.asarray(second_table()))))
+    )(*(in_hbm(x) for x in (strips.reshape(2, W, W, 2 * W), jnp.asarray(first_table()), jnp.asarray(second_table()), coords)))
 
 
 def degrid_kernel(together, plan, own_ref, other_hbm, coords_ref, out_ref, steps, sums, other_ref, sem):
@@ -400,7 +397,8 @@
     core = lax.axis_index("core")
     pol = lax.axis_index("pol")
 
-    coords_all = lax.all_to_all(spread(coords.reshape(2 * CAP * MAXB, VB)), ("z", "x"), split_axis=0, concat_axis=0, tiled=True)
+    own, spread = transform(facets[0], coords.reshape(2 * CAP * MAXB, VB))
+    coords_all = lax.all_to_all(spread, ("z", "x"), split_axis=0, concat_axis=0, tiled=True)
 
     coords_all = coords_all.reshape(16, 2 * CAP, MAXB, VB)
 
@@ -425,9 +423,7 @@
         jnp.where((slot[None, :] == chip * CAP + jnp.arange(CAP)[:, None]) & mine[None, :], counts[None, :], 0), axis=1
     )
 
-    own = transform(facets[0])
-    sent, coords_all = lax.optimization_barrier((own, coords_all))
-    other = lax.ppermute(sent, "core", [(0, 1), (1, 0)])
+    other = lax.ppermute(own, "core", [(0, 1), (1, 0)])
     parts = degrid(plan, own, other, coords_all)
     parts = lax.all_to_all(parts, ("z", "x"), split_axis=0, concat_axis=0, tiled=True)
     visible = jnp.sum(parts.astype(F32), axis=0)

time: 57 us -> 58.8 us (1.032)
  waiting for transfers between devices: 16.4 us -> 20.6 us
  Pallas kernels: 19.1 us -> 17.8 us
  starting transfers between devices: 17.4 us -> 16.3 us
    all_to_all x1, waiting for transfers between devices: 4.11 us -> 8.87 us  [on_device(): lax.all_to_all(spread, ('z', 'x'), split_axis=0, concat_axis=0, tiled=True)]
    ppermute x3, waiting for transfers between devices: 1.68 us -> 3.28 us  [on_device(): lax.ppermute(visible, 'pol', [(i, (i + k) % 4) for i in range(4)])]
    pallas_call x2 -> x1, Pallas kernels: 9.08 us -> 7.62 us  [transform(): pl.pallas_call(transform_kernel, out_shape=[jax.ShapeDtypeStruct((S, 2 *...]
    ppermute x3, starting transfers between devices: 5.91 us -> 4.68 us  [on_device(): lax.ppermute(visible, 'pol', [(i, (i + k) % 4) for i in range(4)])]
    all_to_all x1, waiting for transfers between devices: 9.59 us -> 8.45 us  [on_device(): lax.all_to_all(parts, ('z', 'x'), split_axis=0, concat_axis=0, tiled=True)]
    ppermute x1, waiting for transfers between devices: 0.99 us -> 0.01 us  [on_device(): other = lax.ppermute(own, 'core', [(0, 1), (1, 0)])]
  transfers between devices with their start and end apart: 6 -> 6, of which waited for: 5 -> 4; matrix products, arithmetic and copies ran while one was open for 6% -> 6% of each run, Pallas kernels for 14% -> 1%
where the time goes in v8:
time: 58.8 us; the launch traced here: 58.4 us
  waiting for transfers between devices  20.6 us (35%)
  Pallas kernels  17.8 us (30%)
  starting transfers between devices  16.3 us (28%)
  other arithmetic  2.23 us (4%)
  local copies, waits for them, and re-layouts  1.36 us (2%)
    all_to_all x1, waiting for transfers between devices, on_device(): lax.all_to_all(spread, ('z', 'x'), split_axis=0, concat_axis=0, tiled=True)  8.87 us
    pallas_call x1, Pallas kernels, degrid(): pl.pallas_call(functools.partial(degrid_kernel, together), out_shape=jax....  8.75 us
    all_to_all x1, waiting for transfers between devices, on_device(): lax.all_to_all(parts, ('z', 'x'), split_axis=0, concat_axis=0, tiled=True)  8.45 us
    all_to_all x1, starting transfers between devices, on_device(): lax.all_to_all(spread, ('z', 'x'), split_axis=0, concat_axis=0, tiled=True)  7.98 us
    pallas_call x1, Pallas kernels, transform(): pl.pallas_call(transform_kernel, out_shape=[jax.ShapeDtypeStruct((S, 2 *...  7.62 us
    ppermute x3, starting transfers between devices, on_device(): lax.ppermute(visible, 'pol', [(i, (i + k) % 4) for i in range(4)])  4.68 us
    all_to_all x1, starting transfers between devices, on_device(): lax.all_to_all(parts, ('z', 'x'), split_axis=0, concat_axis=0, tiled=True)  3.54 us
    ppermute x3, waiting for transfers between devices, on_device(): lax.ppermute(visible, 'pol', [(i, (i + k) % 4) for i in range(4)])  3.28 us
  transfers between devices with their start and end apart: 6, of which 4 were waited for; matrix products, arithmetic and copies ran while one was open for 6% of the time, Pallas kernels for 1%

profile of v8, /device:TPU:0, one launch (start us, length us, event | category | flops | bytes accessed | tf_op | source)
XLA Modules:
  0.0 58.4 jit_solution(1424254513801166046)
XLA Ops:
  0.0 7.6 %transform.1 = (bf16[64,128,128]{2,1,0:T(8,128)(2,1)S(1)}, f32[16,64,128]{2,1,0:T(8,128)}) custom-call(bf16[2,64,64,128]{3,2,1,0:T(8,128)(2,1)} %bitcast.13, bf16[64,1024]{1,0:T(8,128)(2,1)} %constant.66.clone.waves_hbm, bf16[64,128,128]{2,1,0:T(8,128)(2,1)} %constant.67.clone.second_hbm, f32[64,128]{1,0:T(8,128)} %bitcast.14), custom_call_target="tpu_custom_call" | custom-call | flops 12000000000 | bytes 8000000 | tf_op jit(solution)/shard_map/transform/pallas_call | solution.py:177
  7.6 0.1 collective-permute-start
  7.7 8.0 %all-to-all-start = ((f32[16,64,128]{2,1,0:T(8,128)}), f32[16,64,128]{2,1,0:T(8,128)S(1)}, u32[]{:S(2)}, u32[]{:S(2)}) async-start(f32[16,64,128]{2,1,0:T(8,128)} %get-tuple-element.12), calls=%async_computation | async-start | bytes 1048576 | tf_op jit(solution)/shard_map/all_to_all | solution.py:401
  15.7 0.2 select_reduce_fusion.4
  15.9 0.7 %select_reduce_fusion.6 = (s32[]{:T(128)}, pred[64]{0:T(512)(128)(4,1)S(1)}, s32[64]{0:T(128)S(1)}, s32[64]{0:T(128)S(1)}) fusion(s32[]{:T(128)S(6)} %axis_index.51, s32[64]{0:T(128)S(1)} %copy-done.3, s32[64]{0:T(128)S(1)} %select_reduce_fusion.4), kind=kLoop, calls=%fused_computation.28 | loop fusion | flops 1727 | bytes 1096 | tf_op jit(solution)/shard_map/reduce_sum | solution.py:420
  16.6 0.6 %fusion.9 = (s32[]{:T(128)}, s32[64]{0:T(128)S(1)}) fusion(pred[64]{0:T(512)(128)(4,1)S(1)} %get-tuple-element.14, s32[64]{0:T(128)S(1)} %copy-done.2), kind=kLoop, calls=%fused_computation.33 | loop fusion | flops 1151 | bytes 580 | tf_op jit(solution)/shard_map/reduce_sum | solution.py:420
  17.2 0.1 select_reduce_fusion.3
  17.3 0.1 select_reduce_fusion.2
  17.4 0.1 select_reduce_fusion.1
  17.5 0.1 select_reduce_fusion
  17.7 1.3 %concatenate.7.plan = s32[384]{0:T(512)S(1)} concatenate(s32[256]{0:T(256)S(1)} %select_reduce_fusion, s32[64]{0:T(128)S(1)} %select_reduce_fusion.1, s32[1]{0:T(128)} %bitcast.2, s32[1]{0:T(128)} %bitcast.3, s32[1]{0:T(128)} %bitcast.4, s32[1]{0:T(128)} %bitcast.5, s32[60]{0:T(128)S(1)} %broadcast_in_dim.73), dimensions={0} | concatenate | bytes 3072 | tf_op jit(solution)/shard_map/concatenate | solution.py:421
  19.0 8.9 %all-to-all-done = f32[16,64,128]{2,1,0:T(8,128)S(1)} async-done(((f32[16,64,128]{2,1,0:T(8,128)}), f32[16,64,128]{2,1,0:T(8,128)S(1)}, u32[]{:S(2)}, u32[]{:S(2)}) %all-to-all-start) | async-done | bytes 524320 | tf_op jit(solution)/shard_map/all_to_all | solution.py:401
  27.9 8.8 %degrid.1 = bf16[16,64,128]{2,1,0:T(8,128)(2,1)} custom-call(s32[384]{0:T(512)S(1)} %concatenate.7.plan, bf16[64,128,128]{2,1,0:T(8,128)(2,1)S(1)} %get-tuple-element.11.own_ref, bf16[64,128,128]{2,1,0:T(8,128)(2,1)} %collective-permute-done.other_hbm, f32[16,8,8,128]{3,2,1,0:T(8,128)S(1)} %bitcast.11), custom_call_target="tpu_custom_call" | custom-call | flops 12000000000 | bytes 8000000 | tf_op jit(solution)/shard_map/degrid/pallas_call | solution.py:303
  36.7 3.5 %all-to-all-start.1 = ((bf16[16,64,128]{2,1,0:T(8,128)(2,1)}), bf16[16,64,128]{2,1,0:T(8,128)(2,1)S(1)}, u32[]{:S(2)}, u32[]{:S(2)}) async-start(bf16[16,64,128]{2,1,0:T(8,128)(2,1)} %degrid.1), calls=%async_computation.1 | async-start | bytes 524288 | tf_op jit(solution)/shard_map/all_to_all | solution.py:428
  40.2 0.2 select_reduce_fusion.5
  40.4 8.5 %all-to-all-done.1 = bf16[16,64,128]{2,1,0:T(8,128)(2,1)S(1)} async-done(((bf16[16,64,128]{2,1,0:T(8,128)(2,1)}), bf16[16,64,128]{2,1,0:T(8,128)(2,1)S(1)}, u32[]{:S(2)}, u32[]{:S(2)}) %all-to-all-start.1) | async-done | bytes 262176 | tf_op jit(solution)/shard_map/all_to_all | solution.py:428
  48.9 3.1 %collective-permute-start.3 = (f32[64,128]{1,0:T(8,128)S(1)}, f32[64,128]{1,0:T(8,128)S(1)}, u32[]{:S(2)}, u32[]{:S(2)}) collective-permute-start(f32[64,128]{1,0:T(8,128)S(1)} %convert_reduce_fusion.own_ref), channel_id=1, source_target_pairs={{0,3},{1,0},{2,1},{3,2},{4,7},{5,4},{6,5},{7,6},{8,11},{9,8},{10,9... | collective-permute-start | bytes 98312 | tf_op jit(solution)/shard_map/ppermute | solution.py:432
  52.0 0.6 %collective-permute-start.2 = (f32[64,128]{1,0:T(8,128)S(1)}, f32[64,128]{1,0:T(8,128)S(1)}, u32[]{:S(2)}, u32[]{:S(2)}) collective-permute-start(f32[64,128]{1,0:T(8,128)S(1)} %convert_reduce_fusion.own_ref), channel_id=1, source_target_pairs={{0,2},{1,3},{2,0},{3,1},{4,6},{5,7},{6,4},{7,5},{8,10},{9,11},{10,... | collective-permute-start | bytes 98312 | tf_op jit(solution)/shard_map/ppermute | solution.py:432
  52.6 1.0 %collective-permute-start.1 = (f32[64,128]{1,0:T(8,128)S(1)}, f32[64,128]{1,0:T(8,128)S(1)}, u32[]{:S(2)}, u32[]{:S(2)}) collective-permute-start(f32[64,128]{1,0:T(8,128)S(1)} %convert_reduce_fusion.own_ref), channel_id=1, source_target_pairs={{0,1},{1,2},{2,3},{3,0},{4,5},{5,6},{6,7},{7,4},{8,9},{9,10},{10,1... | collective-permute-start | bytes 98312 | tf_op jit(solution)/shard_map/ppermute | solution.py:432
  53.6 0.1 pad_add_fusion.place
  53.7 0.8 %jones.1 = (f32[4,4,2,8,128]{4,3,2,1,0:T(8,128)S(1)}, f32[4,8,128]{2,1,0:T(8,128)S(1)}) custom-call(s32[5]{0:T(128)S(1)} %pad_add_fusion.place, s32[4,2,8,128]{3,2,1,0:T(8,128)S(1)} %bitcast.12, f32[8,512]{1,0:T(8,128)S(1)} %copy-done), custom_call_target="tpu_custom_call" | custom-call | tf_op jit(solution)/shard_map/jones/pallas_call | solution.py:356
  54.5 2.9 %collective-permute-done.2.two_ref = f32[64,128]{1,0:T(8,128)S(1)} collective-permute-done((f32[64,128]{1,0:T(8,128)S(1)}, f32[64,128]{1,0:T(8,128)S(1)}, u32[]{:S(2)}, u32[]{:S(2)}) %collective-permute-start.2) | collective-permute-done | bytes 32800 | tf_op jit(solution)/shard_map/ppermute | solution.py:432
  57.4 0.4 collective-permute-done.1.one_ref
  57.8 0.6 %correct.1 = f32[1,2,4,8,128]{4,3,2,1,0:T(8,128)} custom-call(f32[4,4,2,8,128]{4,3,2,1,0:T(8,128)S(1)} %get-tuple-element.9.jones_ref, f32[4,8,128]{2,1,0:T(8,128)S(1)} %get-tuple-element.10.mask_ref, f32[64,128]{1,0:T(8,128)S(1)} %convert_reduce_fusion.own_ref, f32[64,128]{1,0:T(8,128)S(1)} %collective-permute-done.1.one_ref, ...), custom_call_target="tpu_custom_call" | custom-call | tf_op jit(solution)/shard_map/correct/pallas_call | solution.py:385
  (14 shorter events, 0.1 us)
Async XLA Ops:
  0.0 15.7 %copy-start.3 = (s32[64]{0:T(128)S(1)}, s32[64]{0:T(128)}, u32[]{:S(2)}) copy-start(s32[64]{0:T(128)} %param.9) | copy-start | bytes 772
  0.0 16.5 %copy-start.2 = (s32[64]{0:T(128)S(1)}, s32[64]{0:T(128)}, u32[]{:S(2)}) copy-start(s32[64]{0:T(128)} %param.10) | copy-start | bytes 772
  7.6 20.3 %collective-permute-start = (bf16[64,128,128]{2,1,0:T(8,128)(2,1)S(1)}, bf16[64,128,128]{2,1,0:T(8,128)(2,1)}, u32[]{:S(2)}, u32[]{:S(2)}) collective-permute-start(bf16[64,128,128]{2,1,0:T(8,128)(2,1)S(1)} %get-tuple-element.11.own_ref), channel_id=1, source_target_pairs={{0,4},{4,0},{1,5},{5,1},{2,6},{6,2},{3,7},{7,3},{8,12},{12,8},{9,1... | collective-permute-start | bytes 6291464 | tf_op jit(solution)/shard_map/ppermute | solution.py:426
  7.7 20.2 %all-to-all-start = ((f32[16,64,128]{2,1,0:T(8,128)}), f32[16,64,128]{2,1,0:T(8,128)S(1)}, u32[]{:S(2)}, u32[]{:S(2)}) async-start(f32[16,64,128]{2,1,0:T(8,128)} %get-tuple-element.12), calls=%async_computation | async-start | bytes 1048576 | tf_op jit(solution)/shard_map/all_to_all | solution.py:401
  27.9 25.8 %copy-start.1 = (s32[4,8,2,128]{3,2,1,0:T(2,128)S(1)}, s32[4,8,2,128]{3,2,1,0:T(2,128)}, u32[]{:S(2)}) copy-start(s32[4,8,2,128]{3,2,1,0:T(2,128)} %param.12) | copy-start | bytes 98308
  27.9 25.8 %copy-start = (f32[8,512]{1,0:T(8,128)S(1)}, f32[8,512]{1,0:T(8,128)}, u32[]{:S(2)}) copy-start(f32[8,512]{1,0:T(8,128)} %table_ref.1) | copy-start | bytes 49156
  36.7 12.2 %all-to-all-start.1 = ((bf16[16,64,128]{2,1,0:T(8,128)(2,1)}), bf16[16,64,128]{2,1,0:T(8,128)(2,1)S(1)}, u32[]{:S(2)}, u32[]{:S(2)}) async-start(bf16[16,64,128]{2,1,0:T(8,128)(2,1)} %degrid.1), calls=%async_computation.1 | async-start | bytes 524288 | tf_op jit(solution)/shard_map/all_to_all | solution.py:428
  48.9 5.6 %collective-permute-start.3 = (f32[64,128]{1,0:T(8,128)S(1)}, f32[64,128]{1,0:T(8,128)S(1)}, u32[]{:S(2)}, u32[]{:S(2)}) collective-permute-start(f32[64,128]{1,0:T(8,128)S(1)} %convert_reduce_fusion.own_ref), channel_id=1, source_target_pairs={{0,3},{1,0},{2,1},{3,2},{4,7},{5,4},{6,5},{7,6},{8,11},{9,8},{10,9... | collective-permute-start | bytes 98312 | tf_op jit(solution)/shard_map/ppermute | solution.py:432
  52.0 5.4 %collective-permute-start.2 = (f32[64,128]{1,0:T(8,128)S(1)}, f32[64,128]{1,0:T(8,128)S(1)}, u32[]{:S(2)}, u32[]{:S(2)}) collective-permute-start(f32[64,128]{1,0:T(8,128)S(1)} %convert_reduce_fusion.own_ref), channel_id=1, source_target_pairs={{0,2},{1,3},{2,0},{3,1},{4,6},{5,7},{6,4},{7,5},{8,10},{9,11},{10,... | collective-permute-start | bytes 98312 | tf_op jit(solution)/shard_map/ppermute | solution.py:432
  52.6 5.1 %collective-permute-start.1 = (f32[64,128]{1,0:T(8,128)S(1)}, f32[64,128]{1,0:T(8,128)S(1)}, u32[]{:S(2)}, u32[]{:S(2)}) collective-permute-start(f32[64,128]{1,0:T(8,128)S(1)} %convert_reduce_fusion.own_ref), channel_id=1, source_target_pairs={{0,1},{1,2},{2,3},{3,0},{4,5},{5,6},{6,7},{7,4},{8,9},{9,10},{10,1... | collective-permute-start | bytes 98312 | tf_op jit(solution)/shard_map/ppermute | solution.py:432
